TPU v7x, 128 devices: a whole 4x4x4 slice. The times are simulated.
128 devices in a mesh: group: 32 (over y, z, core), tp: 4 (over x).
Axes of the slice: x: 4, y: 4, z: 4, core: 2. Of those that a mesh axis runs over, the one named last changes fastest.
Arguments:
- queries: bfloat16 [5120, 6144], P('group', 'tp'), may hold values from -180 to 180
- keys: bfloat16 [5120, 6144], P('group', 'tp'), may hold values from -6.2 to 6.2
- values: bfloat16 [5120, 6144], P('group', 'tp'), may hold values from -24 to 24
- out_weight: bfloat16 [6144, 6144], P('tp'), may hold values from -0.078125 to 0.078125
- gate_table: float32 [16, 6144], replicated, may hold values from 0.5 to 4
- block_mask: int32 [32, 32], replicated, may hold values 0 or 1
- levels: int32 [4], replicated, may hold values from 0 to 15
Outputs:
- update: bfloat16 [5120, 6144], P('group', 'tp')
All inputs are finite; a program needn't handle non-finite values.
Results may differ from a plain program's by a relative error of at most 0.017.
Values may be sent and summed in bfloat16 or wider, within the bound.
No kernel may reach another device: no remote copies, remote signals or barrier semaphores. Data moves between devices by JAX's collectives and lax.ppermute only.
A program may use at most 128 MiB of HBM per device.

v0:
```python
import jax
import jax.numpy as jnp
from jax import lax
from jax.sharding import PartitionSpec as P

HEAD_DIM = 128
VIDEO_GROUPS = 4


masked_score = -1e30


def visible_blocks(block_mask, query_block, block_count):
    key_block = jnp.arange(block_count, dtype=jnp.int32)
    per_group = block_count // VIDEO_GROUPS
    mask_row = jnp.sum(jnp.where(key_block[:, None] == query_block, block_mask, 0), axis=0)
    earlier = key_block // per_group <= query_block // per_group
    return (key_block == query_block) | (mask_row == 1) & earlier


def absorb_block(state, query_rows, key_rows, value_rows):
    running_max, running_sum, running_out = state
    scores = jnp.einsum(
        "qhd,khd->hqk", query_rows, key_rows, preferred_element_type=jnp.float32
    ) * HEAD_DIM ** (-0.5)
    block_max = jnp.max(scores, axis=-1)
    weights = jnp.exp(scores - block_max[..., None]).astype(jnp.bfloat16)
    block_sum = jnp.sum(weights.astype(jnp.float32), axis=-1)
    block_out = jnp.einsum("hqk,khd->hqd", weights, value_rows, preferred_element_type=jnp.float32)
    new_max = jnp.maximum(running_max, block_max)
    old_factor = jnp.exp(running_max - new_max)
    new_factor = jnp.exp(block_max - new_max)
    return (
        new_max,
        running_sum * old_factor + block_sum * new_factor,
        running_out * old_factor[..., None] + block_out * new_factor[..., None],
    )


def absorb_if(state, query_rows, flags, key_block, key_rows, value_rows):

    def taken(current):
        return absorb_block(current, query_rows, key_rows, value_rows)

    def skipped(current):
        return current

    return lax.cond(flags[key_block], taken, skipped, state)


def finish(state):
    normed = state[2] / state[1][..., None]
    heads_here, query_count, head_size = normed.shape
    return (
        jnp.transpose(normed, (1, 0, 2))
        .reshape(query_count, heads_here * head_size)
        .astype(jnp.bfloat16)
    )


def local(queries, keys, values, out_weight, gate_table, block_mask, levels):
    rows_here = queries.shape[0]
    heads_here = queries.shape[1] // HEAD_DIM
    block_count = lax.axis_size("group")
    own_block = lax.axis_index("group")
    query_parts = (queries,)
    query_blocks = (own_block,)
    flag_sets = tuple((visible_blocks(block_mask, target, block_count) for target in query_blocks))
    shaped = tuple(
        (part_rows.reshape(part_rows.shape[0], heads_here, HEAD_DIM) for part_rows in query_parts)
    )
    start_states = tuple(
        (
            (
                jnp.full((heads_here, part_rows.shape[0]), masked_score, jnp.float32),
                jnp.zeros((heads_here, part_rows.shape[0]), jnp.float32),
                jnp.zeros((heads_here, part_rows.shape[0], HEAD_DIM), jnp.float32),
            )
            for part_rows in query_parts
        )
    )
    key_piece = lax.all_gather(keys, "group", axis=0, tiled=True)
    value_piece = lax.all_gather(values, "group", axis=0, tiled=True)
    block_steps = key_piece.shape[0] // rows_here

    def visit(offset, states):
        key_rows = lax.dynamic_slice_in_dim(key_piece, offset * rows_here, rows_here, 0).reshape(
            rows_here, heads_here, HEAD_DIM
        )
        value_rows = lax.dynamic_slice_in_dim(
            value_piece, offset * rows_here, rows_here, 0
        ).reshape(rows_here, heads_here, HEAD_DIM)
        return tuple(
            (
                absorb_if(current, query_rows, flags, offset, key_rows, value_rows)
                for current, query_rows, flags in zip(states, shaped, flag_sets)
            )
        )

    final_states = lax.fori_loop(0, block_steps, visit, start_states)
    attended = tuple((finish(current) for current in final_states))[0]
    head_terms = jnp.dot(attended, out_weight, preferred_element_type=jnp.float32)
    summed = lax.psum_scatter(
        head_terms.astype(jnp.bfloat16), "tp", scatter_dimension=1, tiled=True
    ).astype(jnp.float32)
    columns = summed.shape[1]
    per_group = block_count // VIDEO_GROUPS
    video_group = own_block // per_group
    level_here = jnp.sum(
        jnp.where(jnp.arange(VIDEO_GROUPS, dtype=jnp.int32) == video_group, levels, 0)
    )
    level_index = jnp.arange(gate_table.shape[0], dtype=jnp.int32)
    gate_row = jnp.sum(jnp.where(level_index[:, None] == level_here, gate_table, 0.0), axis=0)
    gate_part = lax.dynamic_slice_in_dim(gate_row, lax.axis_index("tp") * columns, columns, 0)
    return (summed * gate_part[None, :]).astype(jnp.bfloat16)


def solution(mesh):
    return jax.shard_map(
        local,
        mesh=mesh,
        in_specs=(
            P("group", "tp"),
            P("group", "tp"),
            P("group", "tp"),
            P("tp", None),
            P(),
            P(),
            P(),
        ),
        out_specs=P("group", "tp"),
        check_vma=False,
    )
```

profile of v0, /device:TPU:6, one launch (start us, length us, event | category | flops | bytes accessed | tf_op | source)
XLA Modules:
  0.0 347.3 jit_solution(3526469843649244512)
XLA Ops:
  6.5 0.7 all-gather.3.cloned.1.call-update
  7.3 0.7 all-gather.5.cloned.1.call-update
  8.1 0.8 select_reduce_fusion.1
  9.0 73.3 %all-gather.3.cloned.1.call-done = bf16[5120,1536]{1,0:T(8,128)(2,1)} async-done(((bf16[160,1536]{1,0:T(8,128)(2,1)}), bf16[5120,1536]{1,0:T(8,128)(2,1)}) %all-gather.3.cloned.1.call-update) | async-done | bytes 15728656 | tf_op jit(solution)/shard_map/all_gather | solution.py:82
  82.3 72.0 %all-gather.5.cloned.1.call-done = bf16[5120,1536]{1,0:T(8,128)(2,1)} async-done(((bf16[160,1536]{1,0:T(8,128)(2,1)}), bf16[5120,1536]{1,0:T(8,128)(2,1)}) %all-gather.5.cloned.1.call-update) | async-done | bytes 15728656 | tf_op jit(solution)/shard_map/all_gather | solution.py:83
  154.4 68.8 %while.17 = (s32[]{:T(128)}, f32[12,160]{1,0:T(8,128)S(1)}, f32[12,160]{1,0:T(8,128)S(1)}, f32[12,160,128]{2,1,0:T(8,128)S(1)}, pred[32]{0:T(512)(128)(4,1)S(1)}...) while((s32[]{:T(128)}, f32[12,160]{1,0:T(8,128)S(1)}, ...), condition=%wide.region_6.7_spmd, body=%wide.region_1.6_spmd.sunk | while | flops 161103360 | bytes 9200906 | solution.py:100
  154.4 0.7 dynamic_slice.42
  155.8 3.4 conditional.2
  155.8 1.2 dynamic-slice_bitcast_fusion
  158.0 1.3 fusion.2
  159.3 0.7 dynamic_slice.42
  160.6 3.4 conditional.2
  160.7 1.2 dynamic-slice_bitcast_fusion
  162.8 1.3 fusion.2
  164.1 0.7 dynamic_slice.42
  165.5 3.4 conditional.2
  165.5 1.2 dynamic-slice_bitcast_fusion
  167.6 1.3 fusion.2
  168.9 0.7 dynamic_slice.42
  170.3 3.4 conditional.2
  170.3 1.2 dynamic-slice_bitcast_fusion
  172.4 1.3 fusion.2
  173.7 0.7 dynamic_slice.42
  175.1 3.4 conditional.2
  175.1 1.2 dynamic-slice_bitcast_fusion
  177.2 1.3 fusion.2
  178.6 0.7 dynamic_slice.42
  180.0 0.7 dynamic_slice.42
  181.3 3.4 conditional.2
  181.4 1.2 dynamic-slice_bitcast_fusion
  183.5 1.3 fusion.2
  184.8 0.7 dynamic_slice.42
  186.2 3.4 conditional.2
  186.2 1.2 dynamic-slice_bitcast_fusion
  188.3 1.3 fusion.2
  189.6 0.7 dynamic_slice.42
  191.0 0.7 dynamic_slice.42
  192.4 0.7 dynamic_slice.42
  193.8 0.7 dynamic_slice.42
  195.2 0.7 dynamic_slice.42
  196.6 0.7 dynamic_slice.42
  198.0 0.7 dynamic_slice.42
  199.4 0.7 dynamic_slice.42
  200.8 0.7 dynamic_slice.42
  202.2 0.7 dynamic_slice.42
  203.6 0.7 dynamic_slice.42
  205.0 0.7 dynamic_slice.42
  206.4 0.7 dynamic_slice.42
  207.8 0.7 dynamic_slice.42
  209.2 0.7 dynamic_slice.42
  210.7 0.7 dynamic_slice.42
  212.1 0.7 dynamic_slice.42
  213.5 0.7 dynamic_slice.42
  214.9 0.7 dynamic_slice.42
  216.3 0.7 dynamic_slice.42
  217.7 0.7 dynamic_slice.42
  219.1 0.7 dynamic_slice.42
  220.5 0.7 dynamic_slice.42
  221.9 0.7 dynamic_slice.42
  223.3 10.9 %convolution_convert_fusion = bf16[160,6144]{1,0:T(8,128)(2,1)} fusion(bf16[1536,6144]{1,0:T(8,128)(2,1)} %param.14, f32[12,160,128]{2,1,0:T(8,128)S(1)} %get-tuple-element.261, f32[12,160]{1,0:T(8,128)S(1)} %get-tuple-element.262), kind=kOutput, calls=%fused_computation.18 | convolution fusion | flops 3021373440 | bytes 21831168 | tf_op jit(solution)/shard_map/dot_general | solution.py:102
  234.9 0.6 fusion.13
  235.5 0.6 iota_compare_fusion
  236.4 102.5 %reduce-scatter.2.cloned.1.call-done = bf16[160,1536]{1,0:T(8,128)(2,1)} async-done(((bf16[160,6144]{1,0:T(8,128)(2,1)}), bf16[160,1536]{1,0:T(8,128)(2,1)}) %reduce-scatter.2.cloned.1.call-update) | async-done | bytes 491536 | tf_op jit(solution)/shard_map/reduce_scatter | solution.py:103
  338.8 1.9 multiply_convert_fusion
  (64 shorter events, 7.3 us)
Async XLA Ops:
  6.5 2.4 copy-start
  6.5 75.8 %all-gather.3.cloned.1.call-start = ((), (), s32[]{:S(2)}) async-start(), calls=%async_computation.1 | async-start | bytes 16220160 | tf_op jit(solution)/shard_map/all_gather | solution.py:82
  7.3 147.1 %all-gather.5.cloned.1.call-start = ((), (), s32[]{:S(2)}) async-start(), calls=%async_computation.2 | async-start | bytes 16220160 | tf_op jit(solution)/shard_map/all_gather | solution.py:83
  8.0 330.8 %reduce-scatter.2.cloned.1.call-start = ((), (), s32[]{:S(2)}) async-start(), calls=%async_computation.3 | async-start | bytes 2457600 | tf_op jit(solution)/shard_map/reduce_scatter | solution.py:103
  234.2 0.7 copy-start.2
  234.2 1.9 copy-start.1
Sparse Core Ops, SparseCore 0:
  9.6 72.6 all-gather.2
  84.6 69.7 all-gather.4
  234.4 104.4 reduce-scatter.1
where the time goes:
time: 351 us; the launch traced here: 347 us
  waiting for transfers between devices  249 us (71%)
  local copies, waits for them, and re-layouts  31.1 us (9%)
  loops' own time  23.7 us (7%)
  matrix products  23.1 us (7%)
  between operations  13.2 us (4%)
  other arithmetic  6.93 us (2%)
    reduce_scatter x1, waiting for transfers between devices, local(): lax.psum_scatter(head_terms.astype(jnp.bfloat16), 'tp', scatter_dimension...  102 us
    all_gather x1, waiting for transfers between devices, local(): key_piece = lax.all_gather(keys, 'group', axis=0, tiled=True)  73.3 us
    all_gather x1, waiting for transfers between devices, local(): value_piece = lax.all_gather(values, 'group', axis=0, tiled=True)  72 us
    another operation x1, loops' own time, local(): final_states = lax.fori_loop(0, block_steps, visit, start_states)  23 us
    dynamic_slice x32, local copies, waits for them, and re-layouts, absorb_if(): return lax.cond(flags[key_block], taken, skipped, state)  21.5 us
    dot_general x1, matrix products, local(): jnp.dot(attended, out_weight, preferred_element_type=jnp.float32)  10.9 us
    dot_general x7, matrix products, absorb_block(): jnp.einsum('hqk,khd->hqd', weights, value_rows, preferred_element_type=jn...  9.03 us
    cond x7, local copies, waits for them, and re-layouts  8.74 us
  transfers between devices with their start and end apart: 3, of which 3 were waited for; matrix products, arithmetic and copies ran while one was open for 1% of the time, Pallas kernels for 0%

commit v1 on v0

v1 whole, which is shorter than its diff:
```python
import functools

import jax
import jax.numpy as jnp
from jax import lax
from jax.experimental import pallas as pl
from jax.experimental.pallas import tpu as pltpu
from jax.sharding import Mesh, PartitionSpec as P

HEAD_DIM = 128
VIDEO_GROUPS = 4
TOK = 160
LOG2E = 1.4426950408889634

masked_score = -1e30


def visible_matrix(block_mask):
    blocks = block_mask.shape[0]
    block = jnp.arange(blocks, dtype=jnp.int32)
    per_group = blocks // VIDEO_GROUPS
    earlier = block[None, :] // per_group <= block[:, None] // per_group
    return (block[None, :] == block[:, None]) | ((block_mask == 1) & earlier)


def attend_kernel(pieces, bias_ref, q_ref, k_ref, v_ref, o_ref):
    factor = HEAD_DIM ** -0.5 * LOG2E
    for yq in range(VIDEO_GROUPS):
        n = TOK * (yq + 1)
        q = q_ref[yq]
        scores = []
        for p in range(pieces):
            s = lax.dot_general(
                q, k_ref[p, :n, :], (((1,), (1,)), ((), ())), preferred_element_type=jnp.float32
            )
            scores.append(s + bias_ref[p, yq : yq + 1, :n])
        top = functools.reduce(jnp.maximum, [jnp.max(s, axis=-1, keepdims=True) for s in scores])
        total = jnp.zeros((q.shape[0], 2 * HEAD_DIM), jnp.float32)
        for p in range(pieces):
            weights = jnp.exp2((scores[p] - top) * factor).astype(jnp.bfloat16)
            values = jnp.concatenate(
                [v_ref[p, :n, :], jnp.ones((n, HEAD_DIM), jnp.bfloat16)], axis=1
            )
            total = total + jnp.dot(weights, values, preferred_element_type=jnp.float32)
        o_ref[yq] = (total[:, :HEAD_DIM] / total[:, HEAD_DIM:]).astype(o_ref.dtype)


def attend(bias, q, kv):
    pieces, keys_here = kv.shape[:2]
    rows = q.shape[1]
    heads = q.shape[2] // HEAD_DIM
    return pl.pallas_call(
        functools.partial(attend_kernel, pieces),
        grid=(heads,),
        in_specs=[
            pl.BlockSpec(bias.shape, lambda h: (0, 0, 0)),
            pl.BlockSpec((VIDEO_GROUPS, rows, HEAD_DIM), lambda h: (0, 0, h)),
            pl.BlockSpec((pieces, keys_here, HEAD_DIM), lambda h: (0, 0, h)),
            pl.BlockSpec((pieces, keys_here, HEAD_DIM), lambda h: (0, 0, heads + h)),
        ],
        out_specs=pl.BlockSpec((VIDEO_GROUPS, rows, HEAD_DIM), lambda h: (0, 0, h)),
        out_shape=jax.ShapeDtypeStruct(q.shape, jnp.bfloat16),
        compiler_params=pltpu.CompilerParams(vmem_limit_bytes=48 * 2**20),
    )(bias, q, kv, kv)


def local(queries, keys, values, out_weight, gate_table, block_mask, levels):
    y, z, core = lax.axis_index("y"), lax.axis_index("z"), lax.axis_index("core")
    own = z * 2 + core
    visible = visible_matrix(block_mask).reshape(4, 8, 4, 8)
    seen = lax.dynamic_index_in_dim(visible, own, 1, keepdims=False)
    bias = jnp.where(jnp.transpose(seen, (2, 0, 1)), 0.0, masked_score).astype(jnp.float32)
    bias = jnp.repeat(bias, TOK, axis=2)

    parts = jnp.concatenate([a.reshape(TOK, 4, -1) for a in (queries, keys, values)], axis=2)
    width = queries.shape[1] // 4
    swapped = lax.all_to_all(jnp.transpose(parts, (1, 0, 2)), "y", 0, 0, tiled=True)
    q = swapped[:, :, :width]
    kv = swapped[:, :, width:].reshape(1, 4 * TOK, 2 * width)
    kv = lax.all_gather(kv, ("z", "core"), axis=0, tiled=True)
    out = attend(bias, q, kv)
    attended = lax.all_to_all(out, "y", 0, 0, tiled=True)
    attended = jnp.transpose(attended, (1, 0, 2)).reshape(TOK, -1)

    head_terms = jnp.dot(attended, out_weight, preferred_element_type=jnp.float32)
    summed = lax.psum_scatter(
        head_terms.astype(jnp.bfloat16), "tp", scatter_dimension=1, tiled=True
    ).astype(jnp.float32)
    columns = summed.shape[1]
    gate_part = lax.dynamic_slice(
        gate_table,
        (lax.dynamic_index_in_dim(levels, y, keepdims=False), lax.axis_index("tp") * columns),
        (1, columns),
    )
    return (summed * gate_part).astype(jnp.bfloat16)


def solution(mesh):
    fine = Mesh(mesh.devices.reshape(4, 4, 2, 4), ("y", "z", "core", "tp"))
    group = ("y", "z", "core")
    return jax.shard_map(
        local,
        mesh=fine,
        in_specs=(
            P(group, "tp"),
            P(group, "tp"),
            P(group, "tp"),
            P("tp", None),
            P(),
            P(),
            P(),
        ),
        out_specs=P(group, "tp"),
        check_vma=False,
    )
```

time: 351 us -> 162 us (0.46)
  waiting for transfers between devices: 249 us -> 69.9 us
  blocking collectives: 0 us -> 37.6 us
  local copies, waits for them, and re-layouts: 31.1 us -> 4.77 us
  loops' own time: 23.7 us -> 0 us
  Pallas kernels: 0 us -> 18.1 us
  matrix products: 23.1 us -> 10.9 us
  other arithmetic: 6.93 us -> 2.11 us
    all_gather x2 -> x1, waiting for transfers between devices: 145 us -> 47.5 us  [local(): kv = lax.all_gather(kv, ('z', 'core'), axis=0, tiled=True)]
    reduce_scatter x1, waiting for transfers between devices: 102 us -> 22.4 us  [local(): lax.psum_scatter(head_terms.astype(jnp.bfloat16), 'tp', scatter_dimension...]
    all_to_all x0 -> x2, blocking collectives: none -> 37.6 us  [the longest x1 23.9 us: local(): lax.all_to_all(jnp.transpose(parts, (1, 0, 2)), 'y', 0, 0, tiled=True)]
    another operation x33 -> x0, loops' own time: 23.7 us -> none  [the longest x1 23 us: local(): final_states = lax.fori_loop(0, block_steps, visit, start_states)]
    dynamic_slice x33 -> x2, local copies, waits for them, and re-layouts: 21.5 us -> 0.68 us  [the longest x1 0.59 us: local(): lax.dynamic_index_in_dim(levels, y, keepdims=False)]
    pallas_call x0 -> x1, Pallas kernels: none -> 18.1 us  [attend(): pl.pallas_call(functools.partial(attend_kernel, pieces), grid=(heads,), i...]
    dot_general x14 -> x0, matrix products: 12.1 us -> none  [the longest x7 9.03 us: absorb_block(): jnp.einsum('hqk,khd->hqd', weights, value_rows, preferred_element_type=jn...]
    cond x7 -> x0, local copies, waits for them, and re-layouts: 8.74 us -> none
  transfers between devices with their start and end apart: 3 -> 2, of which waited for: 3 -> 2; matrix products, arithmetic and copies ran while one was open for 1% -> 1% of each run, Pallas kernels for 0% -> 0%
where the time goes in v1:
time: 162 us; the launch traced here: 159 us
  waiting for transfers between devices  69.9 us (43%)
  blocking collectives  37.6 us (23%)
  Pallas kernels  18.1 us (11%)
  between operations  15.5 us (10%)
  matrix products  10.9 us (7%)
  local copies, waits for them, and re-layouts  4.77 us (3%)
  other arithmetic  2.11 us (1%)
    all_gather x1, waiting for transfers between devices, local(): kv = lax.all_gather(kv, ('z', 'core'), axis=0, tiled=True)  47.5 us
    all_to_all x1, blocking collectives, local(): lax.all_to_all(jnp.transpose(parts, (1, 0, 2)), 'y', 0, 0, tiled=True)  23.9 us
    reduce_scatter x1, waiting for transfers between devices, local(): lax.psum_scatter(head_terms.astype(jnp.bfloat16), 'tp', scatter_dimension...  22.4 us
    pallas_call x1, Pallas kernels, attend(): pl.pallas_call(functools.partial(attend_kernel, pieces), grid=(heads,), i...  18.1 us
    all_to_all x1, blocking collectives, local(): attended = lax.all_to_all(out, 'y', 0, 0, tiled=True)  13.6 us
    dot_general x1, matrix products, local(): jnp.dot(attended, out_weight, preferred_element_type=jnp.float32)  10.9 us
  transfers between devices with their start and end apart: 2, of which 2 were waited for; matrix products, arithmetic and copies ran while one was open for 1% of the time, Pallas kernels for 0%

profile of v1, /device:TPU:6, one launch (start us, length us, event | category | flops | bytes accessed | tf_op | source)
XLA Modules:
  0.0 158.8 jit_solution(4771635808196428943)
XLA Ops:
  6.5 0.0 copy-start
  6.5 0.0 all-gather.2.cloned.1.call-start
  6.5 1.1 copy.30
  7.7 1.3 copy_bitcast_fusion
  9.0 0.1 maximum_bitcast_fusion
  9.1 0.0 copy-start.1
  9.1 23.9 %all_to_all.10 = bf16[4,160,1152]{2,1,0:T(8,128)(2,1)S(1)} all-to-all(bf16[4,160,1152]{2,1,0:T(8,128)(2,1)S(1)} %maximum_bitcast_fusion), channel_id=1, replica_groups=mesh['y'=4,'z'=4,'core'=2,'tp'=4] {'y'}, dimensions={0} | all-to-all | bytes 2949120 | tf_op jit(solution)/shard_map/all_to_all | solution.py:77
  33.0 1.1 slice.9
  34.1 0.0 all-gather.2.cloned.1.call-update
  34.2 0.0 reduce-scatter.2.cloned.1.call-start
  34.2 0.0 copy-done.1
  34.2 0.1 fusion
  34.3 0.1 reshape.98
  34.4 0.1 copy.17
  34.5 0.1 broadcast_in_dim.17
  34.7 0.2 reshape.99.bias_ref
  34.8 0.1 slice.8.q_ref
  34.9 47.5 %all-gather.2.cloned.1.call-done.k_ref.v_ref = bf16[8,640,768]{2,1,0:T(8,128)(2,1)} async-done(((bf16[1,640,768]{2,1,0:T(8,128)(2,1)}), bf16[8,640,768]{2,1,0:T(8,128)(2,1)}) %all-gather.2.cloned.1.call-update) | async-done | bytes 7864336 | tf_op jit(solution)/shard_map/all_gather | solution.py:80
  82.3 18.1 %shard_map.73 = bf16[4,160,384]{2,1,0:T(8,128)(2,1)S(1)} custom-call(f32[8,4,640]{2,1,0:T(4,128)S(1)} %reshape.99.bias_ref, bf16[4,160,384]{2,1,0:T(8,128)(2,1)S(1)} %slice.8.q_ref, bf16[8,640,768]{2,1,0:T(8,128)(2,1)} %all-gather.2.cloned.1.call-done.k_ref.v_ref, bf16[8,640,768]{2,1,0:T(8,128)(2,1)} %all-gather.2.cloned.1.call-done.k_ref.v_ref), custom_call_target="tpu_custom_call" | custom-call | tf_op jit(solution)/shard_map/pallas_call | solution.py:52
  100.4 13.6 %all_to_all.11 = bf16[4,160,384]{2,1,0:T(8,128)(2,1)S(1)} all-to-all(bf16[4,160,384]{2,1,0:T(8,128)(2,1)S(1)} %shard_map.73), channel_id=1, replica_groups=mesh['y'=4,'z'=4,'core'=2,'tp'=4] {'y'}, dimensions={0} | all-to-all | bytes 983040 | tf_op jit(solution)/shard_map/all_to_all | solution.py:82
  114.1 0.1 copy.26
  114.1 0.0 copy-start.2
  114.1 10.9 %convolution_convert_fusion = bf16[160,6144]{1,0:T(8,128)(2,1)} fusion(bf16[160,1536]{1,0:T(8,128)(2,1)S(1)} %bitcast.26, bf16[1536,6144]{1,0:T(8,128)(2,1)} %param.10), kind=kOutput, calls=%fused_computation | convolution fusion | flops 3020881920 | bytes 21331968 | tf_op jit(solution)/shard_map/dot_general | solution.py:85
  125.0 0.0 reduce-scatter.2.cloned.1.call-update
  125.0 0.0 copy-done.2
  125.1 0.6 dynamic_slice.12
  127.6 0.0 copy-done
  127.6 0.1 dynamic-slice_reduce_fusion
  127.7 22.4 %reduce-scatter.2.cloned.1.call-done = bf16[160,1536]{1,0:T(8,128)(2,1)} async-done(((bf16[160,6144]{1,0:T(8,128)(2,1)}), bf16[160,1536]{1,0:T(8,128)(2,1)}) %reduce-scatter.2.cloned.1.call-update) | async-done | bytes 491536 | tf_op jit(solution)/shard_map/reduce_scatter | solution.py:86
  150.1 1.9 %multiply_convert_fusion = bf16[160,1536]{1,0:T(8,128)(2,1)} fusion(bf16[160,1536]{1,0:T(8,128)(2,1)} %reduce-scatter.2.cloned.1.call-done, f32[1536]{0:T(1024)S(1)} %dynamic-slice_reduce_fusion), kind=kLoop, calls=%fused_computation.2 | loop fusion | flops 737280 | bytes 989184 | tf_op jit(solution)/shard_map/convert_element_type | solution.py:95
  (2 shorter events, 0.0 us)
Async XLA Ops:
  6.5 121.1 %copy-start = (f32[16,6144]{1,0:T(8,128)S(1)}, f32[16,6144]{1,0:T(8,128)}, u32[]{:S(2)}) copy-start(f32[16,6144]{1,0:T(8,128)} %param.11) | copy-start | bytes 1179652
  6.5 75.8 %all-gather.2.cloned.1.call-start = ((), (), s32[]{:S(2)}) async-start(), calls=%async_computation.3 | async-start | bytes 8847360 | tf_op jit(solution)/shard_map/all_gather | solution.py:80
  9.1 25.1 %copy-start.1 = (s32[32,32]{1,0:T(8,128)S(1)}, s32[32,32]{1,0:T(8,128)}, u32[]{:S(2)}) copy-start(s32[32,32]{1,0:T(8,128)} %param.12) | copy-start | bytes 12292
  34.2 115.9 %reduce-scatter.2.cloned.1.call-start = ((), (), s32[]{:S(2)}) async-start(), calls=%async_computation.4 | async-start | bytes 2457600 | tf_op jit(solution)/shard_map/reduce_scatter | solution.py:86
  114.1 10.9 %copy-start.2 = (s32[4]{0:T(128)S(1)}, s32[4]{0:T(128)}, u32[]{:S(2)}) copy-start(s32[4]{0:T(128)} %param.13) | copy-start | bytes 52
Sparse Core Ops, SparseCore 0:
  34.3 48.0 all-gather.1
  125.2 24.8 reduce-scatter.1

commit v2 on v1

v2 whole, which is shorter than its diff:
```python
import functools

import jax
import jax.numpy as jnp
from jax import lax
from jax.experimental import pallas as pl
from jax.experimental.pallas import tpu as pltpu
from jax.sharding import Mesh, PartitionSpec as P

HEAD_DIM = 128
VIDEO_GROUPS = 4
TOK = 160
HEADS = 3
WIDTH = HEADS * HEAD_DIM
FACTOR = HEAD_DIM ** -0.5 * 1.4426950408889634

masked_score = -1e30
VMEM_GRANT = 56 * 2**20
VMEM_SMALL = 8 * 2**20


def visible_matrix(block_mask):
    blocks = block_mask.shape[0]
    block = jnp.arange(blocks, dtype=jnp.int32)
    per_group = blocks // VIDEO_GROUPS
    earlier = block[None, :] // per_group <= block[:, None] // per_group
    return (block[None, :] == block[:, None]) | ((block_mask == 1) & earlier)


Y_OFFSETS = (0, 3, 1, 2)


def start_all(copies):
    for copy in copies:
        copy.start()


def wait_all(copies):
    for copy in copies:
        copy.wait()


def pack_kernel(place_ref, queries, keys, values, *refs):
    outs, (both_s, query_s, sems, out_sems) = refs[:-4], refs[-4:]
    arrive, leave = [], []
    for j, distance in enumerate((0, 1, 3, 2)):
        first = lax.rem(place_ref[1] + distance, 4) * WIDTH
        source = pl.ds(pl.multiple_of(first, WIDTH), WIDTH)
        pairs = (
            (keys.at[:, source], both_s.at[j, :, pl.ds(0, WIDTH)]),
            (values.at[:, source], both_s.at[j, :, pl.ds(WIDTH, WIDTH)]),
            (queries.at[:, source], query_s.at[j]),
        )
        for i, (src, dst) in enumerate(pairs):
            arrive.append(pltpu.make_async_copy(src, dst, sems.at[3 * j + i]))
        leave.append(pltpu.make_async_copy(both_s.at[j], outs[j], out_sems.at[j]))
        leave.append(pltpu.make_async_copy(query_s.at[j], outs[4 + j], out_sems.at[4 + j]))
    start_all(arrive)
    for j in range(4):
        wait_all(arrive[3 * j : 3 * j + 3])
        start_all(leave[2 * j : 2 * j + 2])
    wait_all(leave)


def pack_by_owner(place, queries, keys, values):
    shape = lambda width: jax.ShapeDtypeStruct((TOK, width), jnp.bfloat16)
    hbm = pl.BlockSpec(memory_space=pltpu.HBM)
    outs = pl.pallas_call(
        pack_kernel,
        in_specs=[pl.BlockSpec(memory_space=pltpu.SMEM), hbm, hbm, hbm],
        out_specs=[hbm] * 8,
        out_shape=[shape(2 * WIDTH)] * 4 + [shape(WIDTH)] * 4,
        scratch_shapes=[
            pltpu.VMEM((4, TOK, 2 * WIDTH), jnp.bfloat16),
            pltpu.VMEM((4, TOK, WIDTH), jnp.bfloat16),
            pltpu.SemaphoreType.DMA((12,)),
            pltpu.SemaphoreType.DMA((8,)),
        ],
        compiler_params=pltpu.CompilerParams(vmem_limit_bytes=VMEM_GRANT),
        name="pack_by_owner",
    )(place, queries, keys, values)
    return outs[:4], outs[4:]


def stack_kernel(*refs):
    parts, out, sems = refs[:-2], refs[-2], refs[-1]
    rows = parts[0].shape[0]
    copies = [
        pltpu.make_async_copy(part, out.at[pl.ds(i * rows, rows), :], sems.at[i])
        for i, part in enumerate(parts)
    ]
    start_all(copies)
    wait_all(copies)


def stack(*parts):
    rows, width = parts[0].shape
    return pl.pallas_call(
        stack_kernel,
        in_specs=[pl.BlockSpec(memory_space=pltpu.VMEM)] * len(parts),
        out_specs=pl.BlockSpec(memory_space=pltpu.HBM),
        out_shape=jax.ShapeDtypeStruct((len(parts) * rows, width), parts[0].dtype),
        scratch_shapes=[pltpu.SemaphoreType.DMA((len(parts),))],
        compiler_params=pltpu.CompilerParams(vmem_limit_bytes=VMEM_SMALL),
        name="stack",
    )(*parts)


def take_kernel(first, x_ref, o_ref, sem):
    rows = o_ref.shape[0]
    copy = pltpu.make_async_copy(x_ref.at[pl.ds(first, rows), :], o_ref, sem)
    copy.start()
    copy.wait()


def take_rows(x, first, rows):
    return pl.pallas_call(
        functools.partial(take_kernel, first),
        in_specs=[pl.BlockSpec(memory_space=pltpu.VMEM)],
        out_specs=pl.BlockSpec(memory_space=pltpu.HBM),
        out_shape=jax.ShapeDtypeStruct((rows, x.shape[1]), x.dtype),
        scratch_shapes=[pltpu.SemaphoreType.DMA],
        compiler_params=pltpu.CompilerParams(vmem_limit_bytes=VMEM_SMALL),
        name="take_rows",
    )(x)


FIRST_SEGMENTS = ((0, 0, 160, 0, 0), (1, 0, 160, 1, 0), (1, 160, 160, 2, 0), (1, 320, 160, 3, 0))
FAR_SEGMENTS = (
    (0, 0, 160, 0, 0), (1, 0, 160, 1, 0), (1, 160, 80, 2, 0), (2, 0, 80, 2, 80), (2, 80, 160, 3, 0)
)


def lay_out(y, head, qs, parts, segments, q_s, k_s, v_s):
    arrays = 1 + max(segment[0] for segment in segments)
    pieces = len(parts) // arrays
    keys = slice(head * HEAD_DIM, (head + 1) * HEAD_DIM)
    values = slice((HEADS + head) * HEAD_DIM, (HEADS + head + 1) * HEAD_DIM)
    for j, offset in enumerate(Y_OFFSETS):
        group = lax.rem(y + offset, 4)
        for r in range(2):
            place = pl.ds(pl.multiple_of((group * 2 + r) * TOK, TOK), TOK)
            q_s[head, place, :] = qs[r][j * TOK : (j + 1) * TOK, keys]
    for array, row, rows, j, start in segments:
        group = lax.rem(y + Y_OFFSETS[j], 4)
        for p in range(pieces):
            part = parts[arrays * p + array]
            place = pl.ds(pl.multiple_of((group * pieces + p) * TOK + start, 16), rows)
            k_s[head, place, :] = part[row : row + rows, keys]
            v_s[head, place, :HEAD_DIM] = part[row : row + rows, values]
    v_s[head, :, HEAD_DIM:] = jnp.ones((v_s.shape[1], HEAD_DIM), jnp.bfloat16)


def partial_attention(bias_ref, q_s, k_s, v_s, head, yq):
    n = k_s.shape[1] // 4 * (yq + 1)
    q = q_s[head, 2 * TOK * yq : 2 * TOK * (yq + 1), :]
    s = lax.dot_general(
        q, k_s[head, :n, :], (((1,), (1,)), ((), ())), preferred_element_type=jnp.float32
    )
    s = s + jnp.concatenate(
        [jnp.broadcast_to(bias_ref[r, yq : yq + 1, :n], (TOK, n)) for r in range(2)], axis=0
    )
    top = jnp.max(s, axis=-1, keepdims=True)
    weights = jnp.exp2((s - top) * FACTOR).astype(jnp.bfloat16)
    return top, jnp.dot(weights, v_s[head, :n, :], preferred_element_type=jnp.float32)


def first_kernel(place_ref, bias_ref, *refs):
    qs, parts, (o_ref, lse_ref), scratch = refs[:2], refs[2:-5], refs[-5:-3], refs[-3:]
    for head in range(HEADS):
        columns = slice(head * HEAD_DIM, (head + 1) * HEAD_DIM)
        lay_out(place_ref[1], head, qs, parts, FIRST_SEGMENTS, *scratch)
        for yq in range(VIDEO_GROUPS):
            top, total = partial_attention(bias_ref, *scratch, head, yq)
            weight_sum = total[:, HEAD_DIM:]
            o_ref[yq, :, columns] = total[:, :HEAD_DIM] / weight_sum
            lse_ref[yq, :, columns] = top * FACTOR + jnp.log2(weight_sum)


def last_kernel(place_ref, bias_ref, *refs):
    qs, parts, scratch = refs[:2], refs[2:-9], refs[-3:]
    o_in, lse_in, o0, o1, lse0, lse1 = refs[-9:-3]
    for head in range(HEADS):
        columns = slice(head * HEAD_DIM, (head + 1) * HEAD_DIM)
        lay_out(place_ref[1], head, qs, parts, FAR_SEGMENTS, *scratch)
        for yq in range(VIDEO_GROUPS):
            top, total = partial_attention(bias_ref, *scratch, head, yq)
            scaled = top * FACTOR
            before = lse_in[yq, :, columns]
            both = jnp.maximum(scaled, before)
            new_factor = jnp.exp2(scaled - both)
            old_factor = jnp.exp2(before - both)
            weight_sum = total[:, HEAD_DIM:] * new_factor + old_factor
            out = total[:, :HEAD_DIM] * new_factor + o_in[yq, :, columns] * old_factor
            out = (out / weight_sum).astype(jnp.bfloat16)
            lse = both + jnp.log2(weight_sum)
            o0[yq, :, columns], o1[yq, :, columns] = out[:TOK], out[TOK:]
            lse0[yq, :, columns], lse1[yq, :, columns] = lse[:TOK], lse[TOK:]


def attention_call(kernel, place, bias, qs, parts, state, outs, keys_here, name, flops):
    vmem = pl.BlockSpec(memory_space=pltpu.VMEM)
    operands = (bias, *qs, *parts, *state)
    return pl.pallas_call(
        kernel,
        in_specs=[pl.BlockSpec(memory_space=pltpu.SMEM)] + [vmem] * len(operands),
        out_specs=[vmem] * len(outs),
        out_shape=outs,
        scratch_shapes=[
            pltpu.VMEM((HEADS, 8 * TOK, HEAD_DIM), jnp.bfloat16),
            pltpu.VMEM((HEADS, keys_here, HEAD_DIM), jnp.bfloat16),
            pltpu.VMEM((HEADS, keys_here, 2 * HEAD_DIM), jnp.bfloat16),
        ],
        compiler_params=pltpu.CompilerParams(vmem_limit_bytes=20 * 2**20),
        cost_estimate=pl.CostEstimate(flops=flops, bytes_accessed=2**20, transcendentals=0),
        name=name,
    )(place, *operands)


def merge_kernel(place_ref, oa, la, ob, lb, *outs):
    for out_ref, distance in zip(outs, (0, 1, 3, 2)):
        group = lax.rem(place_ref[1] + distance, 4)
        a, b = la[group], lb[group]
        top = jnp.maximum(a, b)
        wa, wb = jnp.exp2(a - top), jnp.exp2(b - top)
        out = oa[group].astype(jnp.float32) * wa + ob[group].astype(jnp.float32) * wb
        out_ref[...] = (out / (wa + wb)).astype(out_ref.dtype)


def merge_cores(place, oa, la, ob, lb):
    vmem = pl.BlockSpec(memory_space=pltpu.VMEM)
    return pl.pallas_call(
        merge_kernel,
        in_specs=[pl.BlockSpec(memory_space=pltpu.SMEM)] + [vmem] * 4,
        out_specs=[vmem] * 4,
        out_shape=[jax.ShapeDtypeStruct((TOK, WIDTH), jnp.bfloat16)] * 4,
        compiler_params=pltpu.CompilerParams(vmem_limit_bytes=VMEM_SMALL),
        name="merge_cores",
    )(place, oa, la, ob, lb)


def project_kernel(places, added, place_ref, *refs):
    parts, w_ref, refs = refs[:4], refs[4], refs[5:]
    extra, outs, rows_s = refs[:added], refs[added:-1], refs[-1]
    for part, offset in zip(parts, Y_OFFSETS):
        first = lax.rem(place_ref[1] + offset, 4) * WIDTH
        rows_s[:, pl.ds(pl.multiple_of(first, WIDTH), WIDTH)] = part[...]
    columns = w_ref.shape[1] // 8
    for i, (distance, half) in enumerate(places):
        first = (lax.rem(place_ref[0] + distance, 4) * 2 + half) * columns
        weights = w_ref[:, pl.ds(pl.multiple_of(first, columns), columns)]
        term = jnp.dot(rows_s[...], weights, preferred_element_type=jnp.float32)
        if added:
            term = term + extra[i][...].astype(jnp.float32)
        outs[i][...] = term.astype(outs[i].dtype)


def project(place, attended, out_weight, places, extra=(), dtype=jnp.bfloat16):
    depth, columns = out_weight.shape[0], out_weight.shape[1] // 8
    count = len(places)
    vmem = pl.BlockSpec(memory_space=pltpu.VMEM)
    return pl.pallas_call(
        functools.partial(project_kernel, places, len(extra)),
        in_specs=[pl.BlockSpec(memory_space=pltpu.SMEM)] + [vmem] * (5 + len(extra)),
        out_specs=[vmem] * count,
        out_shape=[jax.ShapeDtypeStruct((TOK, columns), dtype)] * count,
        scratch_shapes=[pltpu.VMEM((TOK, depth), jnp.bfloat16)],
        compiler_params=pltpu.CompilerParams(vmem_limit_bytes=VMEM_SMALL),
        cost_estimate=pl.CostEstimate(
            flops=2 * count * TOK * depth * columns,
            bytes_accessed=2 * count * depth * columns,
            transcendentals=0,
        ),
        name="project",
    )(place, *attended, out_weight, *extra)


def final_kernel(own_a, own_b, direct_a, direct_b, summed_a, summed_b, gate_ref, o_ref):
    columns = own_a.shape[1]
    for i, (own, direct, summed) in enumerate(
        ((own_a, direct_a, summed_a), (own_b, direct_b, summed_b))
    ):
        place = slice(i * columns, (i + 1) * columns)
        total = own[...] + direct[...].astype(jnp.float32) + summed[...].astype(jnp.float32)
        o_ref[:, place] = (total * gate_ref[:, place]).astype(o_ref.dtype)


def finish(halves, gate):
    rows, columns = halves[0].shape
    vmem = pl.BlockSpec(memory_space=pltpu.VMEM)
    return pl.pallas_call(
        final_kernel,
        in_specs=[vmem] * 7,
        out_specs=vmem,
        out_shape=jax.ShapeDtypeStruct((rows, 2 * columns), jnp.bfloat16),
        compiler_params=pltpu.CompilerParams(vmem_limit_bytes=VMEM_SMALL),
        name="finish",
    )(*halves, gate)


def shift(x, axis, step):
    size = lax.axis_size(axis)
    return lax.ppermute(x, axis, [(i, (i + step) % size) for i in range(size)])


def local(queries, keys, values, out_weight, gate_table, block_mask, levels):
    barrier = lax.optimization_barrier
    x, y, z, core = (lax.axis_index(name) for name in ("tp", "y", "z", "core"))
    place = jnp.stack([x, y, z, core])

    visible = visible_matrix(block_mask).reshape(4, 4, 2, 4, 4, 2)
    seen = lax.dynamic_index_in_dim(visible, z, 1, keepdims=False)
    seen = lax.dynamic_index_in_dim(seen, core, 4, keepdims=False)
    seen = jnp.stack(
        [lax.dynamic_index_in_dim(seen, c, 1, keepdims=False) for c in (core, 1 - core)], axis=0
    )
    seen = jnp.stack(
        [lax.dynamic_index_in_dim(seen, (z + d) % 4, 3, keepdims=False) for d in (0, 3, 1, 2)],
        axis=3,
    )
    bias = jnp.repeat(jnp.where(seen, 0.0, masked_score).astype(jnp.float32), TOK, axis=3)
    bias = bias.reshape(2, 4, 4, 4 * TOK)
    bias_first = bias[..., : 3 * TOK].reshape(2, 4, 12 * TOK)
    bias_last = bias[..., 3 * TOK :].reshape(2, 4, 4 * TOK)

    columns = gate_table.shape[1] // 4
    gate_part = lax.dynamic_slice(
        gate_table,
        (lax.dynamic_index_in_dim(levels, y, keepdims=False), x * columns),
        (1, columns),
    )

    (own, up, down, across), (q_own, q_up, q_down, q_across) = pack_by_owner(
        place, queries, keys, values
    )
    from_down, from_up = shift(up, "y", 1), shift(down, "y", -1)
    from_across = shift(across, "y", 2)
    own_before, own_after = shift(own, "z", 1), shift(own, "z", -1)

    own_far = shift(own_before, "z", 1)

    arrived = (from_down, from_up, from_across, q_up, q_down, q_across)
    arrived, own_before, own_after, own_far, bias_first, bias_last, gate_part = barrier(
        (arrived, own_before, own_after, own_far, bias_first, bias_last, gate_part)
    )
    from_down, from_up, from_across, q_up, q_down, q_across = arrived
    rest = stack(from_down, from_up, from_across)
    rest_before, rest_after = shift(rest, "z", 1), shift(rest, "z", -1)
    q_here = stack(q_own, shift(q_up, "y", 1), shift(q_down, "y", -1), shift(q_across, "y", 2))
    q_there = shift(q_here, "core", 1)
    q_there, rest_before, rest_after = barrier((q_there, rest_before, rest_after))
    half = rest.shape[0] // 2
    far = (
        own_far,
        shift(take_rows(rest_before, 0, half), "z", 1),
        shift(take_rows(rest_after, half, half), "z", -1),
    )
    qs = (q_here, q_there)
    parts = (own, rest, own_before, rest_before, own_after, rest_after)

    both = lambda dtype: jax.ShapeDtypeStruct((VIDEO_GROUPS, 2 * TOK, WIDTH), dtype)
    one = lambda dtype: jax.ShapeDtypeStruct((VIDEO_GROUPS, TOK, WIDTH), dtype)
    f32, bf16 = jnp.float32, jnp.bfloat16
    state = attention_call(
        first_kernel, place, bias_first, qs, parts, (),
        [both(f32), both(f32)], 12 * TOK, "attend_first", 100 * 10**9,
    )
    o_own, o_other, lse_own, lse_other = attention_call(
        last_kernel, place, bias_last, qs, far, state,
        [one(bf16), one(bf16), one(f32), one(f32)], 4 * TOK, "attend_last", 6 * 10**9,
    )
    out, out_up, out_down, out_across = merge_cores(
        place, o_own, lse_own, shift(o_other, "core", 1), shift(lse_other, "core", 1)
    )
    attended = (out, shift(out_up, "y", 1), shift(out_down, "y", -1), shift(out_across, "y", 2))

    across_a, across_b = project(place, attended, out_weight, ((2, 0), (2, 1)))
    from_left, from_right = shift(across_a, "tp", 1), shift(across_b, "tp", -1)
    right_b, left_a = project(place, attended, out_weight, ((1, 1), (3, 0)))
    direct_b, direct_a = shift(right_b, "tp", 1), shift(left_a, "tp", -1)
    own_a, own_b = project(place, attended, out_weight, ((0, 0), (0, 1)), dtype=f32)
    right_a, left_b = project(
        place, attended, out_weight, ((1, 0), (3, 1)), (from_left, from_right)
    )
    summed_a, summed_b = shift(right_a, "tp", 1), shift(left_b, "tp", -1)
    return finish((own_a, own_b, direct_a, direct_b, summed_a, summed_b), gate_part)


def solution(mesh):
    fine = Mesh(mesh.devices.reshape(4, 4, 2, 4), ("y", "z", "core", "tp"))
    group = ("y", "z", "core")
    return jax.shard_map(
        local,
        mesh=fine,
        in_specs=(
            P(group, "tp"),
            P(group, "tp"),
            P(group, "tp"),
            P("tp", None),
            P(),
            P(),
            P(),
        ),
        out_specs=P(group, "tp"),
        check_vma=False,
    )
```

time: 162 us -> 97.1 us (0.60); the launches traced: 159 us -> 96.8 us
  waiting for transfers between devices: 69.9 us -> 29.6 us
  blocking collectives: 37.6 us -> 0 us
  starting transfers between devices: 0.04 us -> 32.8 us
  between operations: 15.5 us -> 2.45 us
  matrix products: 10.9 us -> 0 us
  Pallas kernels: 18.1 us -> 27.1 us
  local copies, waits for them, and re-layouts: 4.77 us -> 3.1 us
    all_gather x1 -> x0, waiting for transfers between devices: 47.5 us -> none  [local(): kv = lax.all_gather(kv, ('z', 'core'), axis=0, tiled=True)]
    all_to_all x2 -> x0, blocking collectives: 37.6 us -> none  [the longest x1 23.9 us: local(): lax.all_to_all(jnp.transpose(parts, (1, 0, 2)), 'y', 0, 0, tiled=True)]
    ppermute x0 -> x25, starting transfers between devices: none -> 32.8 us  [shift(): return lax.ppermute(x, axis, [(i, (i + step) % size) for i in range(size)])]
    ppermute x0 -> x25, waiting for transfers between devices: none -> 29.6 us  [shift(): return lax.ppermute(x, axis, [(i, (i + step) % size) for i in range(size)])]
    reduce_scatter x1 -> x0, waiting for transfers between devices: 22.4 us -> none  [local(): lax.psum_scatter(head_terms.astype(jnp.bfloat16), 'tp', scatter_dimension...]
    dot_general x1 -> x0, matrix products: 10.9 us -> none  [local(): jnp.dot(attended, out_weight, preferred_element_type=jnp.float32)]
    pallas_call x1 -> x13, Pallas kernels: 18.1 us -> 27.1 us  [the longest x2 13.9 us: attention_call(): pl.pallas_call(kernel, in_specs=[pl.BlockSpec(memory_space=pltpu.SMEM)] +...]
    reshape x5 -> x4, local copies, waits for them, and re-layouts: 2.7 us -> 0.58 us  [the longest x1 0.19 us: local(): visible = visible_matrix(block_mask).reshape(4, 4, 2, 4, 4, 2)]
  transfers between devices with their start and end apart: 2 -> 25, of which waited for: 2 -> 14; matrix products, arithmetic and copies ran while one was open for 1% -> 4% of each run, Pallas kernels for 0% -> 15%
where the time goes in v2:
time: 97.1 us; the launch traced here: 96.8 us
  starting transfers between devices  32.8 us (34%)
  waiting for transfers between devices  29.6 us (30%)
  Pallas kernels  27.1 us (28%)
  local copies, waits for them, and re-layouts  3.1 us (3%)
  between operations  2.45 us (3%)
  other arithmetic  1.65 us (2%)
    ppermute x25, starting transfers between devices, shift(): return lax.ppermute(x, axis, [(i, (i + step) % size) for i in range(size)])  32.8 us
    ppermute x25, waiting for transfers between devices, shift(): return lax.ppermute(x, axis, [(i, (i + step) % size) for i in range(size)])  29.6 us
    pallas_call x2, Pallas kernels, attention_call(): pl.pallas_call(kernel, in_specs=[pl.BlockSpec(memory_space=pltpu.SMEM)] +...  13.9 us
    pallas_call x4, Pallas kernels, project(): pl.pallas_call(functools.partial(project_kernel, places, len(extra)), in_...  6.23 us
    pallas_call x1, Pallas kernels, pack_by_owner(): pl.pallas_call(pack_kernel, in_specs=[pl.BlockSpec(memory_space=pltpu.SME...  3.02 us
  transfers between devices with their start and end apart: 25, of which 14 were waited for; matrix products, arithmetic and copies ran while one was open for 4% of the time, Pallas kernels for 15%

profile of v2, /device:TPU:6, one launch (start us, length us, event | category | flops | bytes accessed | tf_op | source)
XLA Modules:
  0.0 96.8 jit_solution(9184716674523829117)
XLA Ops:
  0.0 0.6 pad_add_fusion.place_ref
  0.7 3.0 %pack_by_owner.1 = (bf16[160,768]{1,0:T(8,128)(2,1)}, bf16[160,768]{1,0:T(8,128)(2,1)}, bf16[160,768]{1,0:T(8,128)(2,1)}, bf16[160,768]{1,0:T(8,128)(2,1)}, bf16...) custom-call(s32[4]{0:T(128)} %pad_add_fusion.place_ref, ...), custom_call_target="tpu_custom_call" | custom-call | tf_op jit(solution)/shard_map/pack_by_owner/pallas_call | solution.py:68
  3.7 2.0 %collective-permute-start.3 = (bf16[160,768]{1,0:T(8,128)(2,1)}, bf16[160,768]{1,0:T(8,128)(2,1)S(1)}, u32[]{:S(2)}, u32[]{:S(2)}) collective-permute-start(bf16[160,768]{1,0:T(8,128)(2,1)} %get-tuple-element.52.refs_2_), channel_id=1, source_target_pairs={{0,8},{8,16},{16,24},{24,0},{1,9},{9,17},{17,25},{25,1},{2,10},{10... | collective-permute-start | bytes 737288 | tf_op jit(solution)/shard_map/ppermute | solution.py:303
  5.7 2.2 %collective-permute-start.4 = (bf16[160,768]{1,0:T(8,128)(2,1)}, bf16[160,768]{1,0:T(8,128)(2,1)S(1)}, u32[]{:S(2)}, u32[]{:S(2)}) collective-permute-start(bf16[160,768]{1,0:T(8,128)(2,1)} %get-tuple-element.52.refs_2_), channel_id=1, source_target_pairs={{0,24},{8,0},{16,8},{24,16},{1,25},{9,1},{17,9},{25,17},{2,26},{10... | collective-permute-start | bytes 737288 | tf_op jit(solution)/shard_map/ppermute | solution.py:303
  7.9 1.6 %collective-permute-start = (bf16[160,768]{1,0:T(8,128)(2,1)}, bf16[160,768]{1,0:T(8,128)(2,1)S(1)}, u32[]{:S(2)}, u32[]{:S(2)}) collective-permute-start(bf16[160,768]{1,0:T(8,128)(2,1)} %get-tuple-element.46), channel_id=1, source_target_pairs={{0,32},{32,64},{64,96},{96,0},{1,33},{33,65},{65,97},{97,1},{2,34}... | collective-permute-start | bytes 737288 | tf_op jit(solution)/shard_map/ppermute | solution.py:303
  9.5 1.7 %collective-permute-start.1 = (bf16[160,768]{1,0:T(8,128)(2,1)}, bf16[160,768]{1,0:T(8,128)(2,1)S(1)}, u32[]{:S(2)}, u32[]{:S(2)}) collective-permute-start(bf16[160,768]{1,0:T(8,128)(2,1)} %get-tuple-element.47), channel_id=1, source_target_pairs={{0,96},{32,0},{64,32},{96,64},{1,97},{33,1},{65,33},{97,65},{2,98}... | collective-permute-start | bytes 737288 | tf_op jit(solution)/shard_map/ppermute | solution.py:303
  11.1 2.0 %collective-permute-start.2 = (bf16[160,768]{1,0:T(8,128)(2,1)}, bf16[160,768]{1,0:T(8,128)(2,1)S(1)}, u32[]{:S(2)}, u32[]{:S(2)}) collective-permute-start(bf16[160,768]{1,0:T(8,128)(2,1)} %get-tuple-element.48), channel_id=1, source_target_pairs={{0,64},{32,96},{64,0},{96,32},{1,65},{33,97},{65,1},{97,33},{2,66}... | collective-permute-start | bytes 737288 | tf_op jit(solution)/shard_map/ppermute | solution.py:303
  13.1 0.9 collective-permute-done.3.refs_4_
  14.0 0.8 fusion
  14.8 0.2 reshape.94
  15.0 0.7 dynamic-slice_reduce_fusion.1
  15.7 0.1 dynamic-slice_add_fusion.3
  15.9 0.1 add_select_fusion
  16.0 0.1 broadcast_in_dim.17
  16.1 0.2 reshape.95
  16.2 0.1 slice.9
  16.3 0.1 reshape.96.bias_ref
  16.5 0.1 reshape.97.bias_ref
  16.6 0.7 dynamic_slice.37
  19.3 0.9 dynamic_slice.38.gate_ref
  20.2 3.0 %collective-permute-done.2.refs_2_ = bf16[160,768]{1,0:T(8,128)(2,1)S(1)} collective-permute-done((bf16[160,768]{1,0:T(8,128)(2,1)}, bf16[160,768]{1,0:T(8,128)(2,1)S(1)}, u32[]{:S(2)}, u32[]{:S(2)}) %collective-permute-start.2) | collective-permute-done | bytes 245792 | tf_op jit(solution)/shard_map/ppermute | solution.py:303
  23.3 1.0 stack.43.refs_3_
  24.3 0.1 collective-permute-start.10
  24.3 3.2 %collective-permute-start.11 = (bf16[480,768]{1,0:T(8,128)(2,1)S(1)}, bf16[480,768]{1,0:T(8,128)(2,1)S(1)}, u32[]{:S(2)}, u32[]{:S(2)}) collective-permute-start(bf16[480,768]{1,0:T(8,128)(2,1)S(1)} %stack.43.refs_3_), channel_id=1, source_target_pairs={{0,24},{8,0},{16,8},{24,16},{1,25},{9,1},{17,9},{25,17},{2,26},{10... | collective-permute-start | bytes 2211848 | tf_op jit(solution)/shard_map/ppermute | solution.py:303
  27.6 1.1 %collective-permute-start.6 = (bf16[160,384]{1,0:T(8,128)(2,1)S(1)}, bf16[160,384]{1,0:T(8,128)(2,1)S(1)}, u32[]{:S(2)}, u32[]{:S(2)}) collective-permute-start(bf16[160,384]{1,0:T(8,128)(2,1)S(1)} %copy-done.5), channel_id=1, source_target_pairs={{0,32},{32,64},{64,96},{96,0},{1,33},{33,65},{65,97},{97,1},{2,34}... | collective-permute-start | bytes 368648 | tf_op jit(solution)/shard_map/ppermute | solution.py:303
  28.7 2.1 %collective-permute-start.7 = (bf16[160,384]{1,0:T(8,128)(2,1)S(1)}, bf16[160,384]{1,0:T(8,128)(2,1)S(1)}, u32[]{:S(2)}, u32[]{:S(2)}) collective-permute-start(bf16[160,384]{1,0:T(8,128)(2,1)S(1)} %copy-done.4), channel_id=1, source_target_pairs={{0,96},{32,0},{64,32},{96,64},{1,97},{33,1},{65,33},{97,65},{2,98}... | collective-permute-start | bytes 368648 | tf_op jit(solution)/shard_map/ppermute | solution.py:303
  30.8 1.1 %collective-permute-start.8 = (bf16[160,384]{1,0:T(8,128)(2,1)S(1)}, bf16[160,384]{1,0:T(8,128)(2,1)S(1)}, u32[]{:S(2)}, u32[]{:S(2)}) collective-permute-start(bf16[160,384]{1,0:T(8,128)(2,1)S(1)} %copy-done.3), channel_id=1, source_target_pairs={{0,64},{32,96},{64,0},{96,32},{1,65},{33,97},{65,1},{97,33},{2,66}... | collective-permute-start | bytes 368648 | tf_op jit(solution)/shard_map/ppermute | solution.py:303
  31.9 3.1 %collective-permute-done.6.refs_1_ = bf16[160,384]{1,0:T(8,128)(2,1)S(1)} collective-permute-done((bf16[160,384]{1,0:T(8,128)(2,1)S(1)}, bf16[160,384]{1,0:T(8,128)(2,1)S(1)}, u32[]{:S(2)}, u32[]{:S(2)}) %collective-permute-start.6) | collective-permute-done | bytes 122912 | tf_op jit(solution)/shard_map/ppermute | solution.py:303
  35.0 2.2 %collective-permute-done.8.refs_3_ = bf16[160,384]{1,0:T(8,128)(2,1)S(1)} collective-permute-done((bf16[160,384]{1,0:T(8,128)(2,1)S(1)}, bf16[160,384]{1,0:T(8,128)(2,1)S(1)}, u32[]{:S(2)}, u32[]{:S(2)}) %collective-permute-start.8) | collective-permute-done | bytes 122912 | tf_op jit(solution)/shard_map/ppermute | solution.py:303
  37.2 0.7 stack.42.refs_0_
  37.9 0.1 collective-permute-start.9
  37.9 1.9 %collective-permute-done.9.refs_1_ = bf16[640,384]{1,0:T(8,128)(2,1)S(1)} collective-permute-done((bf16[640,384]{1,0:T(8,128)(2,1)S(1)}, bf16[640,384]{1,0:T(8,128)(2,1)S(1)}, u32[]{:S(2)}, u32[]{:S(2)}) %collective-permute-start.9) | collective-permute-done | bytes 491552 | tf_op jit(solution)/shard_map/ppermute | solution.py:303
  39.8 2.8 %collective-permute-done.10.x_ref.refs_5_ = bf16[480,768]{1,0:T(8,128)(2,1)S(1)} collective-permute-done((bf16[480,768]{1,0:T(8,128)(2,1)S(1)}, bf16[480,768]{1,0:T(8,128)(2,1)S(1)}, u32[]{:S(2)}, u32[]{:S(2)}) %collective-permute-start.10) | collective-permute-done | bytes 737312 | tf_op jit(solution)/shard_map/ppermute | solution.py:303
  42.6 0.2 take_rows.2
  42.7 0.1 collective-permute-start.12
  42.8 0.2 take_rows.3
  43.1 3.5 %collective-permute-start.13 = (bf16[240,768]{1,0:T(8,128)(2,1)S(1)}, bf16[240,768]{1,0:T(8,128)(2,1)S(1)}, u32[]{:S(2)}, u32[]{:S(2)}) collective-permute-start(bf16[240,768]{1,0:T(8,128)(2,1)S(1)} %take_rows.3), channel_id=1, source_target_pairs={{0,24},{8,0},{16,8},{24,16},{1,25},{9,1},{17,9},{25,17},{2,26},{10... | collective-permute-start | bytes 1105928 | tf_op jit(solution)/shard_map/ppermute | solution.py:303
  46.5 9.0 %attend_first.1 = (f32[4,320,384]{2,1,0:T(8,128)S(1)}, f32[4,320,384]{2,1,0:T(8,128)S(1)}) custom-call(s32[4]{0:T(128)S(1)} %copy-done.1, f32[2,4,1920]{2,1,0:T(4,128)S(1)} %reshape.96.bias_ref, bf16[640,384]{1,0:T(8,128)(2,1)S(1)} %stack.42.refs_0_, bf16[640,384]{1,0:T(8,128)(2,1)S(1)} %collective-permute-done.9.refs_1_, bf16[160,768]{1,0:T(8,128)(2,1)S(1)} %copy-done.2, ...), custom_call_target="tpu_custom_call" | custom-call | flops 99999997952 | bytes 1048576 | tf_op jit(solution)/shard_map/attend_first/pallas_call | solution.py:204
  55.6 4.9 %attend_last.1 = (bf16[4,160,384]{2,1,0:T(8,128)(2,1)S(1)}, bf16[4,160,384]{2,1,0:T(8,128)(2,1)S(1)}, f32[4,160,384]{2,1,0:T(8,128)S(1)}, f32[4,160,384]{2,1,0:T(8,128)S(1)}) custom-call(s32[4]{0:T(128)S(1)} %copy-done.1, f32[2,4,640]{2,1,0:T(4,128)S(1)} %reshape.97.bias_ref, bf16[640,384]{1,0:T(8,128)(2,1)S(1)} %stack.42.refs_0_, ...), custom_call_target="tpu_custom_call" | custom-call | flops 6000000000 | bytes 1048576 | tf_op jit(solution)/shard_map/attend_last/pallas_call | solution.py:204
  60.5 0.1 collective-permute-start.15
  60.6 0.5 collective-permute-start.14
  61.1 2.8 %collective-permute-done.14.ob = bf16[4,160,384]{2,1,0:T(8,128)(2,1)S(1)} collective-permute-done((bf16[4,160,384]{2,1,0:T(8,128)(2,1)S(1)}, bf16[4,160,384]{2,1,0:T(8,128)(2,1)S(1)}, u32[]{:S(2)}, u32[]{:S(2)}) %collective-permute-start.14) | collective-permute-done | bytes 491552 | tf_op jit(solution)/shard_map/ppermute | solution.py:303
  63.8 1.0 %merge_cores.1 = (bf16[160,384]{1,0:T(8,128)(2,1)S(1)}, bf16[160,384]{1,0:T(8,128)(2,1)S(1)}, bf16[160,384]{1,0:T(8,128)(2,1)S(1)}, bf16[160,384]{1,0:T(8,128)(2,1)S(1)}) custom-call(s32[4]{0:T(128)S(1)} %copy-done.1, bf16[4,160,384]{2,1,0:T(8,128)(2,1)S(1)} %get-tuple-element.70.oa, f32[4,160,384]{2,1,0:T(8,128)S(1)} %get-tuple-element.71.la, ...), custom_call_target="tpu_custom_call" | custom-call | tf_op jit(solution)/shard_map/merge_cores/pallas_call | solution.py:232
  64.8 0.9 collective-permute-start.16
  65.8 2.4 %collective-permute-start.17 = (bf16[160,384]{1,0:T(8,128)(2,1)S(1)}, bf16[160,384]{1,0:T(8,128)(2,1)S(1)}, u32[]{:S(2)}, u32[]{:S(2)}) collective-permute-start(bf16[160,384]{1,0:T(8,128)(2,1)S(1)} %get-tuple-element.76), channel_id=1, source_target_pairs={{0,96},{32,0},{64,32},{96,64},{1,97},{33,1},{65,33},{97,65},{2,98}... | collective-permute-start | bytes 368648 | tf_op jit(solution)/shard_map/ppermute | solution.py:303
  68.2 0.8 collective-permute-start.18
  69.0 2.5 %collective-permute-done.16.refs_1_ = bf16[160,384]{1,0:T(8,128)(2,1)S(1)} collective-permute-done((bf16[160,384]{1,0:T(8,128)(2,1)S(1)}, bf16[160,384]{1,0:T(8,128)(2,1)S(1)}, u32[]{:S(2)}, u32[]{:S(2)}) %collective-permute-start.16) | collective-permute-done | bytes 122912 | tf_op jit(solution)/shard_map/ppermute | solution.py:303
  71.5 1.9 %collective-permute-done.17.refs_2_ = bf16[160,384]{1,0:T(8,128)(2,1)S(1)} collective-permute-done((bf16[160,384]{1,0:T(8,128)(2,1)S(1)}, bf16[160,384]{1,0:T(8,128)(2,1)S(1)}, u32[]{:S(2)}, u32[]{:S(2)}) %collective-permute-start.17) | collective-permute-done | bytes 122912 | tf_op jit(solution)/shard_map/ppermute | solution.py:303
  73.4 1.1 %collective-permute-done.18.refs_3_ = bf16[160,384]{1,0:T(8,128)(2,1)S(1)} collective-permute-done((bf16[160,384]{1,0:T(8,128)(2,1)S(1)}, bf16[160,384]{1,0:T(8,128)(2,1)S(1)}, u32[]{:S(2)}, u32[]{:S(2)}) %collective-permute-start.18) | collective-permute-done | bytes 122912 | tf_op jit(solution)/shard_map/ppermute | solution.py:303
  74.6 1.6 %project.6 = (bf16[160,768]{1,0:T(8,128)(2,1)S(1)}, bf16[160,768]{1,0:T(8,128)(2,1)S(1)}) custom-call(s32[4]{0:T(128)S(1)} %copy-done.1, bf16[160,384]{1,0:T(8,128)(2,1)S(1)} %get-tuple-element.74.refs_0_, bf16[160,384]{1,0:T(8,128)(2,1)S(1)} %collective-permute-done.16.refs_1_, bf16[160,384]{1,0:T(8,128)(2,1)S(1)} %collective-permute-done.17.refs_2_, ...), custom_call_target="tpu_custom_call" | custom-call | flops 754974720 | bytes 4718592 | tf_op jit(solution)/shard_map/project/pallas_call | solution.py:262
  76.1 0.5 collective-permute-start.21
  76.7 1.5 %collective-permute-start.22 = (bf16[160,768]{1,0:T(8,128)(2,1)S(1)}, bf16[160,768]{1,0:T(8,128)(2,1)S(1)}, u32[]{:S(2)}, u32[]{:S(2)}) collective-permute-start(bf16[160,768]{1,0:T(8,128)(2,1)S(1)} %get-tuple-element.83), channel_id=1, source_target_pairs={{0,3},{1,0},{2,1},{3,2},{4,7},{5,4},{6,5},{7,6},{8,11},{9,8},{10,9... | collective-permute-start | bytes 737288 | tf_op jit(solution)/shard_map/ppermute | solution.py:303
  78.2 1.6 %project.5 = (bf16[160,768]{1,0:T(8,128)(2,1)S(1)}, bf16[160,768]{1,0:T(8,128)(2,1)S(1)}) custom-call(s32[4]{0:T(128)S(1)} %copy-done.1, bf16[160,384]{1,0:T(8,128)(2,1)S(1)} %get-tuple-element.74.refs_0_, bf16[160,384]{1,0:T(8,128)(2,1)S(1)} %collective-permute-done.16.refs_1_, bf16[160,384]{1,0:T(8,128)(2,1)S(1)} %collective-permute-done.17.refs_2_, ...), custom_call_target="tpu_custom_call" | custom-call | flops 754974720 | bytes 4718592 | tf_op jit(solution)/shard_map/project/pallas_call | solution.py:262
  79.8 0.9 collective-permute-start.19
  80.7 2.4 %collective-permute-start.20 = (bf16[160,768]{1,0:T(8,128)(2,1)S(1)}, bf16[160,768]{1,0:T(8,128)(2,1)S(1)}, u32[]{:S(2)}, u32[]{:S(2)}) collective-permute-start(bf16[160,768]{1,0:T(8,128)(2,1)S(1)} %get-tuple-element.81), channel_id=1, source_target_pairs={{0,1},{1,2},{2,3},{3,0},{4,5},{5,6},{6,7},{7,4},{8,9},{9,10},{10,1... | collective-permute-start | bytes 737288 | tf_op jit(solution)/shard_map/ppermute | solution.py:303
  83.1 1.0 %collective-permute-done.21.refs_5_ = bf16[160,768]{1,0:T(8,128)(2,1)S(1)} collective-permute-done((bf16[160,768]{1,0:T(8,128)(2,1)S(1)}, bf16[160,768]{1,0:T(8,128)(2,1)S(1)}, u32[]{:S(2)}, u32[]{:S(2)}) %collective-permute-start.21) | collective-permute-done | bytes 245792 | tf_op jit(solution)/shard_map/ppermute | solution.py:303
  84.1 2.5 %collective-permute-done.22.refs_6_ = bf16[160,768]{1,0:T(8,128)(2,1)S(1)} collective-permute-done((bf16[160,768]{1,0:T(8,128)(2,1)S(1)}, bf16[160,768]{1,0:T(8,128)(2,1)S(1)}, u32[]{:S(2)}, u32[]{:S(2)}) %collective-permute-start.22) | collective-permute-done | bytes 245792 | tf_op jit(solution)/shard_map/ppermute | solution.py:303
  86.6 1.6 %project.7 = (bf16[160,768]{1,0:T(8,128)(2,1)S(1)}, bf16[160,768]{1,0:T(8,128)(2,1)S(1)}) custom-call(s32[4]{0:T(128)S(1)} %copy-done.1, bf16[160,384]{1,0:T(8,128)(2,1)S(1)} %get-tuple-element.74.refs_0_, bf16[160,384]{1,0:T(8,128)(2,1)S(1)} %collective-permute-done.16.refs_1_, bf16[160,384]{1,0:T(8,128)(2,1)S(1)} %collective-permute-done.17.refs_2_, ...), custom_call_target="tpu_custom_call" | custom-call | flops 754974720 | bytes 4718592 | tf_op jit(solution)/shard_map/project/pallas_call | solution.py:262
  88.2 0.2 collective-permute-start.23
  88.4 1.9 %collective-permute-start.24 = (bf16[160,768]{1,0:T(8,128)(2,1)S(1)}, bf16[160,768]{1,0:T(8,128)(2,1)S(1)}, u32[]{:S(2)}, u32[]{:S(2)}) collective-permute-start(bf16[160,768]{1,0:T(8,128)(2,1)S(1)} %get-tuple-element.85), channel_id=1, source_target_pairs={{0,3},{1,0},{2,1},{3,2},{4,7},{5,4},{6,5},{7,6},{8,11},{9,8},{10,9... | collective-permute-start | bytes 737288 | tf_op jit(solution)/shard_map/ppermute | solution.py:303
  90.3 1.5 %project.4 = (f32[160,768]{1,0:T(8,128)S(1)}, f32[160,768]{1,0:T(8,128)S(1)}) custom-call(s32[4]{0:T(128)S(1)} %copy-done.1, bf16[160,384]{1,0:T(8,128)(2,1)S(1)} %get-tuple-element.74.refs_0_, bf16[160,384]{1,0:T(8,128)(2,1)S(1)} %collective-permute-done.16.refs_1_, bf16[160,384]{1,0:T(8,128)(2,1)S(1)} %collective-permute-done.17.refs_2_, ...), custom_call_target="tpu_custom_call" | custom-call | flops 754974720 | bytes 4718592 | tf_op jit(solution)/shard_map/project/pallas_call | solution.py:262
  91.9 2.6 %collective-permute-done.23.summed_a = bf16[160,768]{1,0:T(8,128)(2,1)S(1)} collective-permute-done((bf16[160,768]{1,0:T(8,128)(2,1)S(1)}, bf16[160,768]{1,0:T(8,128)(2,1)S(1)}, u32[]{:S(2)}, u32[]{:S(2)}) %collective-permute-start.23) | collective-permute-done | bytes 245792 | tf_op jit(solution)/shard_map/ppermute | solution.py:303
  94.5 1.3 %collective-permute-done.24.summed_b = bf16[160,768]{1,0:T(8,128)(2,1)S(1)} collective-permute-done((bf16[160,768]{1,0:T(8,128)(2,1)S(1)}, bf16[160,768]{1,0:T(8,128)(2,1)S(1)}, u32[]{:S(2)}, u32[]{:S(2)}) %collective-permute-start.24) | collective-permute-done | bytes 245792 | tf_op jit(solution)/shard_map/ppermute | solution.py:303
  95.8 1.0 finish.1
  (39 shorter events, 0.1 us)
Async XLA Ops:
  0.0 16.6 %copy-start.6 = (s32[4]{0:T(128)S(1)}, s32[4]{0:T(128)}, u32[]{:S(2)}) copy-start(s32[4]{0:T(128)} %param.13) | copy-start | bytes 52
  3.7 23.9 %copy-start.5 = (bf16[160,384]{1,0:T(8,128)(2,1)S(1)}, bf16[160,384]{1,0:T(8,128)(2,1)}, u32[]{:S(2)}) copy-start(bf16[160,384]{1,0:T(8,128)(2,1)} %get-tuple-element.55) | copy-start | bytes 368644
  3.7 25.0 %copy-start.4 = (bf16[160,384]{1,0:T(8,128)(2,1)S(1)}, bf16[160,384]{1,0:T(8,128)(2,1)}, u32[]{:S(2)}) copy-start(bf16[160,384]{1,0:T(8,128)(2,1)} %get-tuple-element.56) | copy-start | bytes 368644
  3.7 27.1 %copy-start.3 = (bf16[160,384]{1,0:T(8,128)(2,1)S(1)}, bf16[160,384]{1,0:T(8,128)(2,1)}, u32[]{:S(2)}) copy-start(bf16[160,384]{1,0:T(8,128)(2,1)} %get-tuple-element.57) | copy-start | bytes 368644
  3.7 33.5 %copy-start = (bf16[160,384]{1,0:T(8,128)(2,1)S(1)}, bf16[160,384]{1,0:T(8,128)(2,1)}, u32[]{:S(2)}) copy-start(bf16[160,384]{1,0:T(8,128)(2,1)} %get-tuple-element.54.refs_0_) | copy-start | bytes 368644
  3.7 10.3 %collective-permute-start.3 = (bf16[160,768]{1,0:T(8,128)(2,1)}, bf16[160,768]{1,0:T(8,128)(2,1)S(1)}, u32[]{:S(2)}, u32[]{:S(2)}) collective-permute-start(bf16[160,768]{1,0:T(8,128)(2,1)} %get-tuple-element.52.refs_2_), channel_id=1, source_target_pairs={{0,8},{8,16},{16,24},{24,0},{1,9},{9,17},{17,25},{25,1},{2,10},{10... | collective-permute-start | bytes 737288 | tf_op jit(solution)/shard_map/ppermute | solution.py:303
  5.7 14.5 %collective-permute-start.4 = (bf16[160,768]{1,0:T(8,128)(2,1)}, bf16[160,768]{1,0:T(8,128)(2,1)S(1)}, u32[]{:S(2)}, u32[]{:S(2)}) collective-permute-start(bf16[160,768]{1,0:T(8,128)(2,1)} %get-tuple-element.52.refs_2_), channel_id=1, source_target_pairs={{0,24},{8,0},{16,8},{24,16},{1,25},{9,1},{17,9},{25,17},{2,26},{10... | collective-permute-start | bytes 737288 | tf_op jit(solution)/shard_map/ppermute | solution.py:303
  7.9 12.3 %collective-permute-start = (bf16[160,768]{1,0:T(8,128)(2,1)}, bf16[160,768]{1,0:T(8,128)(2,1)S(1)}, u32[]{:S(2)}, u32[]{:S(2)}) collective-permute-start(bf16[160,768]{1,0:T(8,128)(2,1)} %get-tuple-element.46), channel_id=1, source_target_pairs={{0,32},{32,64},{64,96},{96,0},{1,33},{33,65},{65,97},{97,1},{2,34}... | collective-permute-start | bytes 737288 | tf_op jit(solution)/shard_map/ppermute | solution.py:303
  9.5 10.7 %collective-permute-start.1 = (bf16[160,768]{1,0:T(8,128)(2,1)}, bf16[160,768]{1,0:T(8,128)(2,1)S(1)}, u32[]{:S(2)}, u32[]{:S(2)}) collective-permute-start(bf16[160,768]{1,0:T(8,128)(2,1)} %get-tuple-element.47), channel_id=1, source_target_pairs={{0,96},{32,0},{64,32},{96,64},{1,97},{33,1},{65,33},{97,65},{2,98}... | collective-permute-start | bytes 737288 | tf_op jit(solution)/shard_map/ppermute | solution.py:303
  11.1 12.1 %collective-permute-start.2 = (bf16[160,768]{1,0:T(8,128)(2,1)}, bf16[160,768]{1,0:T(8,128)(2,1)S(1)}, u32[]{:S(2)}, u32[]{:S(2)}) collective-permute-start(bf16[160,768]{1,0:T(8,128)(2,1)} %get-tuple-element.48), channel_id=1, source_target_pairs={{0,64},{32,96},{64,0},{96,32},{1,65},{33,97},{65,1},{97,33},{2,66}... | collective-permute-start | bytes 737288 | tf_op jit(solution)/shard_map/ppermute | solution.py:303
  14.0 9.3 %collective-permute-start.5 = (bf16[160,768]{1,0:T(8,128)(2,1)S(1)}, bf16[160,768]{1,0:T(8,128)(2,1)S(1)}, u32[]{:S(2)}, u32[]{:S(2)}) collective-permute-start(bf16[160,768]{1,0:T(8,128)(2,1)S(1)} %collective-permute-done.3.refs_4_), channel_id=1, source_target_pairs={{0,8},{8,16},{16,24},{24,0},{1,9},{9,17},{17,25},{25,1},{2,10},{10... | collective-permute-start | bytes 737288 | tf_op jit(solution)/shard_map/ppermute | solution.py:303
  24.2 22.3 %copy-start.1 = (s32[4]{0:T(128)S(1)}, s32[4]{0:T(128)}, u32[]{:S(2)}) copy-start(s32[4]{0:T(128)} %pad_add_fusion.place_ref) | copy-start | bytes 52
  24.2 22.3 %copy-start.2 = (bf16[160,768]{1,0:T(8,128)(2,1)S(1)}, bf16[160,768]{1,0:T(8,128)(2,1)}, u32[]{:S(2)}) copy-start(bf16[160,768]{1,0:T(8,128)(2,1)} %get-tuple-element.52.refs_2_) | copy-start | bytes 737284
  24.3 18.3 %collective-permute-start.10 = (bf16[480,768]{1,0:T(8,128)(2,1)S(1)}, bf16[480,768]{1,0:T(8,128)(2,1)S(1)}, u32[]{:S(2)}, u32[]{:S(2)}) collective-permute-start(bf16[480,768]{1,0:T(8,128)(2,1)S(1)} %stack.43.refs_3_), channel_id=1, source_target_pairs={{0,8},{8,16},{16,24},{24,0},{1,9},{9,17},{17,25},{25,1},{2,10},{10... | collective-permute-start | bytes 2211848 | tf_op jit(solution)/shard_map/ppermute | solution.py:303
  24.3 18.2 %collective-permute-start.11 = (bf16[480,768]{1,0:T(8,128)(2,1)S(1)}, bf16[480,768]{1,0:T(8,128)(2,1)S(1)}, u32[]{:S(2)}, u32[]{:S(2)}) collective-permute-start(bf16[480,768]{1,0:T(8,128)(2,1)S(1)} %stack.43.refs_3_), channel_id=1, source_target_pairs={{0,24},{8,0},{16,8},{24,16},{1,25},{9,1},{17,9},{25,17},{2,26},{10... | collective-permute-start | bytes 2211848 | tf_op jit(solution)/shard_map/ppermute | solution.py:303
  27.6 7.4 %collective-permute-start.6 = (bf16[160,384]{1,0:T(8,128)(2,1)S(1)}, bf16[160,384]{1,0:T(8,128)(2,1)S(1)}, u32[]{:S(2)}, u32[]{:S(2)}) collective-permute-start(bf16[160,384]{1,0:T(8,128)(2,1)S(1)} %copy-done.5), channel_id=1, source_target_pairs={{0,32},{32,64},{64,96},{96,0},{1,33},{33,65},{65,97},{97,1},{2,34}... | collective-permute-start | bytes 368648 | tf_op jit(solution)/shard_map/ppermute | solution.py:303
  28.7 6.3 %collective-permute-start.7 = (bf16[160,384]{1,0:T(8,128)(2,1)S(1)}, bf16[160,384]{1,0:T(8,128)(2,1)S(1)}, u32[]{:S(2)}, u32[]{:S(2)}) collective-permute-start(bf16[160,384]{1,0:T(8,128)(2,1)S(1)} %copy-done.4), channel_id=1, source_target_pairs={{0,96},{32,0},{64,32},{96,64},{1,97},{33,1},{65,33},{97,65},{2,98}... | collective-permute-start | bytes 368648 | tf_op jit(solution)/shard_map/ppermute | solution.py:303
  30.8 6.4 %collective-permute-start.8 = (bf16[160,384]{1,0:T(8,128)(2,1)S(1)}, bf16[160,384]{1,0:T(8,128)(2,1)S(1)}, u32[]{:S(2)}, u32[]{:S(2)}) collective-permute-start(bf16[160,384]{1,0:T(8,128)(2,1)S(1)} %copy-done.3), channel_id=1, source_target_pairs={{0,64},{32,96},{64,0},{96,32},{1,65},{33,97},{65,1},{97,33},{2,66}... | collective-permute-start | bytes 368648 | tf_op jit(solution)/shard_map/ppermute | solution.py:303
  37.9 1.9 %collective-permute-start.9 = (bf16[640,384]{1,0:T(8,128)(2,1)S(1)}, bf16[640,384]{1,0:T(8,128)(2,1)S(1)}, u32[]{:S(2)}, u32[]{:S(2)}) collective-permute-start(bf16[640,384]{1,0:T(8,128)(2,1)S(1)} %stack.42.refs_0_), channel_id=1, source_target_pairs={{0,4},{4,0},{1,5},{5,1},{2,6},{6,2},{3,7},{7,3},{8,12},{12,8},{9,1... | collective-permute-start | bytes 1474568 | tf_op jit(solution)/shard_map/ppermute | solution.py:303
  42.7 12.8 %collective-permute-start.12 = (bf16[240,768]{1,0:T(8,128)(2,1)S(1)}, bf16[240,768]{1,0:T(8,128)(2,1)S(1)}, u32[]{:S(2)}, u32[]{:S(2)}) collective-permute-start(bf16[240,768]{1,0:T(8,128)(2,1)S(1)} %take_rows.2), channel_id=1, source_target_pairs={{0,8},{8,16},{16,24},{24,0},{1,9},{9,17},{17,25},{25,1},{2,10},{10... | collective-permute-start | bytes 1105928 | tf_op jit(solution)/shard_map/ppermute | solution.py:303
  42.8 31.7 %slice-start = ((s8[18874368]{0:T(1024)(128)(4,1)}), s8[4194304]{0:T(1024)(128)(4,1)S(1)}, s32[]{:S(2)}) async-start(s8[18874368]{0:T(1024)(128)(4,1)} %bitcast.7), calls=%async_computation | async-start | bytes 8388608
  43.0 31.5 %slice-start.1 = ((s8[18874368]{0:T(1024)(128)(4,1)}), s8[4194304]{0:T(1024)(128)(4,1)S(1)}, s32[]{:S(2)}) async-start(s8[18874368]{0:T(1024)(128)(4,1)} %bitcast.7), calls=%async_computation.1 | async-start | bytes 8388608
  43.0 31.5 %slice-start.2 = ((s8[18874368]{0:T(1024)(128)(4,1)}), s8[4194304]{0:T(1024)(128)(4,1)S(1)}, s32[]{:S(2)}) async-start(s8[18874368]{0:T(1024)(128)(4,1)} %bitcast.7), calls=%async_computation.2 | async-start | bytes 8388608
  43.0 31.5 %slice-start.3 = ((s8[18874368]{0:T(1024)(128)(4,1)}), s8[4194304]{0:T(1024)(128)(4,1)S(1)}, s32[]{:S(2)}) async-start(s8[18874368]{0:T(1024)(128)(4,1)} %bitcast.7), calls=%async_computation.3 | async-start | bytes 8388608
  43.0 31.5 %slice-start.4 = ((s8[18874368]{0:T(1024)(128)(4,1)}), s8[2097152]{0:T(1024)(128)(4,1)S(1)}, s32[]{:S(2)}) async-start(s8[18874368]{0:T(1024)(128)(4,1)} %bitcast.7), calls=%async_computation.4 | async-start | bytes 4194304
  43.1 12.5 %collective-permute-start.13 = (bf16[240,768]{1,0:T(8,128)(2,1)S(1)}, bf16[240,768]{1,0:T(8,128)(2,1)S(1)}, u32[]{:S(2)}, u32[]{:S(2)}) collective-permute-start(bf16[240,768]{1,0:T(8,128)(2,1)S(1)} %take_rows.3), channel_id=1, source_target_pairs={{0,24},{8,0},{16,8},{24,16},{1,25},{9,1},{17,9},{25,17},{2,26},{10... | collective-permute-start | bytes 1105928 | tf_op jit(solution)/shard_map/ppermute | solution.py:303
  60.5 3.4 %collective-permute-start.15 = (f32[4,160,384]{2,1,0:T(8,128)S(1)}, f32[4,160,384]{2,1,0:T(8,128)S(1)}, u32[]{:S(2)}, u32[]{:S(2)}) collective-permute-start(f32[4,160,384]{2,1,0:T(8,128)S(1)} %get-tuple-element.73), channel_id=1, source_target_pairs={{0,4},{4,0},{1,5},{5,1},{2,6},{6,2},{3,7},{7,3},{8,12},{12,8},{9,1... | collective-permute-start | bytes 2949128 | tf_op jit(solution)/shard_map/ppermute | solution.py:303
  60.6 3.3 %collective-permute-start.14 = (bf16[4,160,384]{2,1,0:T(8,128)(2,1)S(1)}, bf16[4,160,384]{2,1,0:T(8,128)(2,1)S(1)}, u32[]{:S(2)}, u32[]{:S(2)}) collective-permute-start(bf16[4,160,384]{2,1,0:T(8,128)(2,1)S(1)} %get-tuple-element.72), channel_id=1, source_target_pairs={{0,4},{4,0},{1,5},{5,1},{2,6},{6,2},{3,7},{7,3},{8,12},{12,8},{9,1... | collective-permute-start | bytes 1474568 | tf_op jit(solution)/shard_map/ppermute | solution.py:303
  64.8 6.6 %collective-permute-start.16 = (bf16[160,384]{1,0:T(8,128)(2,1)S(1)}, bf16[160,384]{1,0:T(8,128)(2,1)S(1)}, u32[]{:S(2)}, u32[]{:S(2)}) collective-permute-start(bf16[160,384]{1,0:T(8,128)(2,1)S(1)} %get-tuple-element.75), channel_id=1, source_target_pairs={{0,32},{32,64},{64,96},{96,0},{1,33},{33,65},{65,97},{97,1},{2,34}... | collective-permute-start | bytes 368648 | tf_op jit(solution)/shard_map/ppermute | solution.py:303
  65.8 7.6 %collective-permute-start.17 = (bf16[160,384]{1,0:T(8,128)(2,1)S(1)}, bf16[160,384]{1,0:T(8,128)(2,1)S(1)}, u32[]{:S(2)}, u32[]{:S(2)}) collective-permute-start(bf16[160,384]{1,0:T(8,128)(2,1)S(1)} %get-tuple-element.76), channel_id=1, source_target_pairs={{0,96},{32,0},{64,32},{96,64},{1,97},{33,1},{65,33},{97,65},{2,98}... | collective-permute-start | bytes 368648 | tf_op jit(solution)/shard_map/ppermute | solution.py:303
  68.2 6.4 %collective-permute-start.18 = (bf16[160,384]{1,0:T(8,128)(2,1)S(1)}, bf16[160,384]{1,0:T(8,128)(2,1)S(1)}, u32[]{:S(2)}, u32[]{:S(2)}) collective-permute-start(bf16[160,384]{1,0:T(8,128)(2,1)S(1)} %get-tuple-element.77), channel_id=1, source_target_pairs={{0,64},{32,96},{64,0},{96,32},{1,65},{33,97},{65,1},{97,33},{2,66}... | collective-permute-start | bytes 368648 | tf_op jit(solution)/shard_map/ppermute | solution.py:303
  76.1 8.0 %collective-permute-start.21 = (bf16[160,768]{1,0:T(8,128)(2,1)S(1)}, bf16[160,768]{1,0:T(8,128)(2,1)S(1)}, u32[]{:S(2)}, u32[]{:S(2)}) collective-permute-start(bf16[160,768]{1,0:T(8,128)(2,1)S(1)} %get-tuple-element.82), channel_id=1, source_target_pairs={{0,1},{1,2},{2,3},{3,0},{4,5},{5,6},{6,7},{7,4},{8,9},{9,10},{10,1... | collective-permute-start | bytes 737288 | tf_op jit(solution)/shard_map/ppermute | solution.py:303
  76.7 10.0 %collective-permute-start.22 = (bf16[160,768]{1,0:T(8,128)(2,1)S(1)}, bf16[160,768]{1,0:T(8,128)(2,1)S(1)}, u32[]{:S(2)}, u32[]{:S(2)}) collective-permute-start(bf16[160,768]{1,0:T(8,128)(2,1)S(1)} %get-tuple-element.83), channel_id=1, source_target_pairs={{0,3},{1,0},{2,1},{3,2},{4,7},{5,4},{6,5},{7,6},{8,11},{9,8},{10,9... | collective-permute-start | bytes 737288 | tf_op jit(solution)/shard_map/ppermute | solution.py:303
  79.8 12.1 %collective-permute-start.19 = (bf16[160,768]{1,0:T(8,128)(2,1)S(1)}, bf16[160,768]{1,0:T(8,128)(2,1)S(1)}, u32[]{:S(2)}, u32[]{:S(2)}) collective-permute-start(bf16[160,768]{1,0:T(8,128)(2,1)S(1)} %get-tuple-element.80), channel_id=1, source_target_pairs={{0,3},{1,0},{2,1},{3,2},{4,7},{5,4},{6,5},{7,6},{8,11},{9,8},{10,9... | collective-permute-start | bytes 737288 | tf_op jit(solution)/shard_map/ppermute | solution.py:303
  80.7 11.2 %collective-permute-start.20 = (bf16[160,768]{1,0:T(8,128)(2,1)S(1)}, bf16[160,768]{1,0:T(8,128)(2,1)S(1)}, u32[]{:S(2)}, u32[]{:S(2)}) collective-permute-start(bf16[160,768]{1,0:T(8,128)(2,1)S(1)} %get-tuple-element.81), channel_id=1, source_target_pairs={{0,1},{1,2},{2,3},{3,0},{4,5},{5,6},{6,7},{7,4},{8,9},{9,10},{10,1... | collective-permute-start | bytes 737288 | tf_op jit(solution)/shard_map/ppermute | solution.py:303
  88.2 6.3 %collective-permute-start.23 = (bf16[160,768]{1,0:T(8,128)(2,1)S(1)}, bf16[160,768]{1,0:T(8,128)(2,1)S(1)}, u32[]{:S(2)}, u32[]{:S(2)}) collective-permute-start(bf16[160,768]{1,0:T(8,128)(2,1)S(1)} %get-tuple-element.84), channel_id=1, source_target_pairs={{0,1},{1,2},{2,3},{3,0},{4,5},{5,6},{6,7},{7,4},{8,9},{9,10},{10,1... | collective-permute-start | bytes 737288 | tf_op jit(solution)/shard_map/ppermute | solution.py:303
  88.4 7.4 %collective-permute-start.24 = (bf16[160,768]{1,0:T(8,128)(2,1)S(1)}, bf16[160,768]{1,0:T(8,128)(2,1)S(1)}, u32[]{:S(2)}, u32[]{:S(2)}) collective-permute-start(bf16[160,768]{1,0:T(8,128)(2,1)S(1)} %get-tuple-element.85), channel_id=1, source_target_pairs={{0,3},{1,0},{2,1},{3,2},{4,7},{5,4},{6,5},{7,6},{8,11},{9,8},{10,9... | collective-permute-start | bytes 737288 | tf_op jit(solution)/shard_map/ppermute | solution.py:303

commit v3 on v1

v3 whole, which is shorter than its diff:
```python
import functools

import jax
import jax.numpy as jnp
from jax import lax
from jax.experimental import pallas as pl
from jax.experimental.pallas import tpu as pltpu
from jax.sharding import Mesh, PartitionSpec as P

HEAD_DIM = 128
VIDEO_GROUPS = 4
TOK = 160
HEADS = 3
WIDTH = HEADS * HEAD_DIM
FACTOR = HEAD_DIM ** -0.5 * 1.4426950408889634

masked_score = -1e30
VMEM_GRANT = 56 * 2**20
VMEM_SMALL = 8 * 2**20
LOG_LANES = 32


def visible_matrix(block_mask):
    blocks = block_mask.shape[0]
    block = jnp.arange(blocks, dtype=jnp.int32)
    per_group = blocks // VIDEO_GROUPS
    earlier = block[None, :] // per_group <= block[:, None] // per_group
    return (block[None, :] == block[:, None]) | ((block_mask == 1) & earlier)


def take_kernel(first, x_ref, o_ref, sem):
    rows = o_ref.shape[0]
    copy = pltpu.make_async_copy(x_ref.at[pl.ds(first, rows), :], o_ref, sem)
    copy.start()
    copy.wait()


def take_rows(x, first, rows):
    return pl.pallas_call(
        functools.partial(take_kernel, first),
        in_specs=[pl.BlockSpec(memory_space=pltpu.VMEM)],
        out_specs=pl.BlockSpec(memory_space=pltpu.HBM),
        out_shape=jax.ShapeDtypeStruct((rows, x.shape[1]), x.dtype),
        scratch_shapes=[pltpu.SemaphoreType.DMA],
        compiler_params=pltpu.CompilerParams(vmem_limit_bytes=VMEM_SMALL),
        name="take_rows",
    )(x)


Y_OFFSETS = (0, 3, 1, 2)


def start_all(copies):
    for copy in copies:
        copy.start()


def wait_all(copies):
    for copy in copies:
        copy.wait()


def pack_kernel(queries, keys, values, *refs):
    outs, (both_s, query_s, sems, out_sems) = refs[:-4], refs[-4:]
    arrive, leave = [], []
    for j, distance in enumerate((0, 1, 3, 2)):
        first = lax.rem(lax.axis_index("y") + distance, 4) * WIDTH
        source = pl.ds(pl.multiple_of(first, WIDTH), WIDTH)
        pairs = (
            (keys.at[:, source], both_s.at[j, :, pl.ds(0, WIDTH)]),
            (values.at[:, source], both_s.at[j, :, pl.ds(WIDTH, WIDTH)]),
            (queries.at[:, source], query_s.at[j]),
        )
        for i, (src, dst) in enumerate(pairs):
            arrive.append(pltpu.make_async_copy(src, dst, sems.at[3 * j + i]))
        leave.append(pltpu.make_async_copy(both_s.at[j], outs[j], out_sems.at[j]))
        leave.append(pltpu.make_async_copy(query_s.at[j], outs[4 + j], out_sems.at[4 + j]))
    start_all(arrive)
    for j in range(4):
        wait_all(arrive[3 * j : 3 * j + 3])
        start_all(leave[2 * j : 2 * j + 2])
    wait_all(leave)


def pack_by_owner(queries, keys, values):
    shape = lambda width: jax.ShapeDtypeStruct((TOK, width), jnp.bfloat16)
    hbm = pl.BlockSpec(memory_space=pltpu.HBM)
    outs = pl.pallas_call(
        pack_kernel,
        in_specs=[hbm, hbm, hbm],
        out_specs=[hbm] * 8,
        out_shape=[shape(2 * WIDTH)] * 4 + [shape(WIDTH)] * 4,
        scratch_shapes=[
            pltpu.VMEM((4, TOK, 2 * WIDTH), jnp.bfloat16),
            pltpu.VMEM((4, TOK, WIDTH), jnp.bfloat16),
            pltpu.SemaphoreType.DMA((12,)),
            pltpu.SemaphoreType.DMA((8,)),
        ],
        compiler_params=pltpu.CompilerParams(vmem_limit_bytes=VMEM_GRANT),
        name="pack_by_owner",
    )(queries, keys, values)
    return outs[:4], outs[4:]


def stack_kernel(*refs):
    parts, out, sems = refs[:-2], refs[-2], refs[-1]
    rows = parts[0].shape[0]
    copies = [
        pltpu.make_async_copy(part, out.at[pl.ds(i * rows, rows), :], sems.at[i])
        for i, part in enumerate(parts)
    ]
    start_all(copies)
    wait_all(copies)


def stack(*parts, space=pltpu.HBM):
    rows, width = parts[0].shape
    return pl.pallas_call(
        stack_kernel,
        in_specs=[pl.BlockSpec(memory_space=pltpu.VMEM)] * len(parts),
        out_specs=pl.BlockSpec(memory_space=space),
        out_shape=jax.ShapeDtypeStruct((len(parts) * rows, width), parts[0].dtype),
        scratch_shapes=[pltpu.SemaphoreType.DMA((len(parts),))],
        compiler_params=pltpu.CompilerParams(vmem_limit_bytes=VMEM_SMALL),
        name="stack",
    )(*parts)


SEGMENTS = {
    2: ((0, 0, 160, 0, 0), (1, 0, 160, 1, 0), (1, 160, 160, 2, 0), (1, 320, 160, 3, 0)),
    3: (
        (0, 0, 160, 0, 0), (1, 0, 160, 1, 0), (1, 160, 80, 2, 0), (2, 0, 80, 2, 80),
        (2, 80, 160, 3, 0),
    ),
}


def lay_out(y, head, qs, pieces, q_s, k_s, v_s):
    keys = slice(head * HEAD_DIM, (head + 1) * HEAD_DIM)
    values = slice((HEADS + head) * HEAD_DIM, (HEADS + head + 1) * HEAD_DIM)
    for j, offset in enumerate(Y_OFFSETS):
        for r, q in enumerate(qs):
            first = (lax.rem(y + offset, 4) * len(qs) + r) * TOK
            place = pl.ds(pl.multiple_of(first, TOK), TOK)
            q_s[head, place, :] = q[j * TOK : (j + 1) * TOK, keys]
    for p, arrays in enumerate(pieces):
        for array, row, rows, j, start in SEGMENTS[len(arrays)]:
            group = lax.rem(y + Y_OFFSETS[j], 4)
            first = (group * len(pieces) + p) * TOK + start
            place = pl.ds(pl.multiple_of(first, 16), rows)
            k_s[head, place, :] = arrays[array][row : row + rows, keys]
            v_s[head, place, :] = arrays[array][row : row + rows, values]


def partial_attention(bias_ref, q_s, k_s, v_s, head):
    rows, keys_here = q_s.shape[1] // 4, k_s.shape[1]
    scores = []
    for yq in range(VIDEO_GROUPS):
        n = keys_here // 4 * (yq + 1)
        q = q_s[head, rows * yq : rows * (yq + 1), :]
        s = lax.dot_general(
            q, k_s[head, :n, :], (((1,), (1,)), ((), ())), preferred_element_type=jnp.float32
        )
        bias = [
            jnp.broadcast_to(bias_ref[r, yq : yq + 1, :n], (TOK, n)) for r in range(rows // TOK)
        ]
        scores.append(s + jnp.concatenate(bias, axis=0))
    tops = [jnp.max(s, axis=-1, keepdims=True) for s in scores]
    weights = [jnp.exp2((s - t) * FACTOR).astype(jnp.bfloat16) for s, t in zip(scores, tops)]
    ones = jnp.ones((keys_here, HEAD_DIM), jnp.bfloat16)
    values = jnp.concatenate([v_s[head], ones], axis=1)
    totals = [jnp.dot(w, values[: w.shape[1]], preferred_element_type=jnp.float32) for w in weights]
    return [
        (top * FACTOR, total[:, :HEAD_DIM], total[:, HEAD_DIM:]) for top, total in zip(tops, totals)
    ]


def merge_states(result, states):
    top, out, weight_sum = result
    both = functools.reduce(jnp.maximum, [log for _, log in states], top)
    factor = jnp.exp2(top - both)
    out, weight_sum = out * factor, weight_sum * factor
    for o, log in states:
        factor = jnp.exp2(log - both)
        out = out + o.astype(jnp.float32) * factor
        weight_sum = weight_sum + factor
    return both, out, weight_sum


def near_kernel(bias_ref, *refs):
    qs, refs, scratch = refs[:2], refs[2:-3], refs[-3:]
    pieces = [refs[2 * p : 2 * p + 2] for p in range(3)]
    o_here, log_here, o_there, log_there = refs[6:]
    place = lax.broadcasted_iota(jnp.int32, (TOK, HEAD_DIM), 1) // LOG_LANES
    for head in range(HEADS):
        columns = slice(head * HEAD_DIM, (head + 1) * HEAD_DIM)
        lay_out(lax.axis_index("y"), head, qs, pieces, *scratch)
        for yq, (top, out, weight_sum) in enumerate(partial_attention(bias_ref, *scratch, head)):
            out, log = out / weight_sum, top + jnp.log2(weight_sum)
            o_here[yq, :, columns], log_here[yq, :, columns] = out[:TOK], log[:TOK]
            o_there[yq, :, columns] = out[TOK:].astype(jnp.bfloat16)
            packed = log[TOK:]
            if head > 0:
                packed = jnp.where(place == head, packed, log_there[yq])
            log_there[yq] = packed


def far_kernel(bias_ref, q, *refs):
    parts, (o_in, log_in, o_out, log_out), scratch = refs[:3], refs[3:-3], refs[-3:]
    for head in range(HEADS):
        columns = slice(head * HEAD_DIM, (head + 1) * HEAD_DIM)
        lay_out(lax.axis_index("y"), head, (q,), (parts,), *scratch)
        for yq, result in enumerate(partial_attention(bias_ref, *scratch, head)):
            state = (o_in[yq, :, columns], log_in[yq, :, columns])
            top, out, weight_sum = merge_states(result, [state])
            o_out[yq, :, columns] = out / weight_sum
            log_out[yq, :, columns] = top + jnp.log2(weight_sum)


def last_kernel(bias_ref, q, *refs):
    parts, states, outs, scratch, o_s = refs[:3], refs[3:7], refs[7:11], refs[11:14], refs[14]
    o_here, log_here, o_there, log_there = states
    for head in range(HEADS):
        columns = slice(head * HEAD_DIM, (head + 1) * HEAD_DIM)
        lay_out(lax.axis_index("y"), head, (q,), (parts,), *scratch)
        for yq, result in enumerate(partial_attention(bias_ref, *scratch, head)):
            log = log_there[yq, :, head * LOG_LANES : head * LOG_LANES + 1]
            here = (o_here[yq, :, columns], log_here[yq, :, columns])
            there = (o_there[yq, :, columns], jnp.broadcast_to(log, (TOK, HEAD_DIM)))
            _, out, weight_sum = merge_states(result, [here, there])
            o_s[yq, :, columns] = (out / weight_sum).astype(jnp.bfloat16)
    for out, distance in zip(outs, (0, 1, 3, 2)):
        out[...] = o_s[lax.rem(lax.axis_index("y") + distance, 4)]


def attend(kernel, bias, qs, pieces, states, outs, scratch=()):
    vmem = pl.BlockSpec(memory_space=pltpu.VMEM)
    operands = [bias, *qs]
    for arrays in pieces:
        operands += arrays
    operands += states
    keys_here = 4 * TOK * len(pieces)
    return pl.pallas_call(
        kernel,
        in_specs=[vmem] * len(operands),
        out_specs=[vmem] * len(outs),
        out_shape=[jax.ShapeDtypeStruct(shape, dtype) for shape, dtype in outs],
        scratch_shapes=[
            pltpu.VMEM((HEADS, 4 * TOK * len(qs), HEAD_DIM), jnp.bfloat16),
            pltpu.VMEM((HEADS, keys_here, HEAD_DIM), jnp.bfloat16),
            pltpu.VMEM((HEADS, keys_here, HEAD_DIM), jnp.bfloat16),
            *scratch,
        ],
        compiler_params=pltpu.CompilerParams(vmem_limit_bytes=20 * 2**20),
        cost_estimate=pl.CostEstimate(
            flops=4 * 10**9 * len(pieces), bytes_accessed=2**20, transcendentals=0
        ),
        name=kernel.__name__,
    )(*operands)


def project_kernel(places, added, *refs):
    parts, w_ref, refs = refs[:4], refs[4], refs[5:]
    extra, outs, rows_s = refs[:added], refs[added:-1], refs[-1]
    for part, offset in zip(parts, Y_OFFSETS):
        first = lax.rem(lax.axis_index("y") + offset, 4) * WIDTH
        rows_s[:, pl.ds(pl.multiple_of(first, WIDTH), WIDTH)] = part[...]
    columns = w_ref.shape[1] // 8
    for i, (distance, half) in enumerate(places):
        first = (lax.rem(lax.axis_index("tp") + distance, 4) * 2 + half) * columns
        weights = w_ref[:, pl.ds(pl.multiple_of(first, columns), columns)]
        term = jnp.dot(rows_s[...], weights, preferred_element_type=jnp.float32)
        if added:
            term = term + extra[i][...].astype(jnp.float32)
        outs[i][...] = term.astype(outs[i].dtype)


def project(attended, out_weight, places, extra=(), dtype=jnp.bfloat16):
    depth, columns = out_weight.shape[0], out_weight.shape[1] // 8
    count = len(places)
    vmem = pl.BlockSpec(memory_space=pltpu.VMEM)
    return pl.pallas_call(
        functools.partial(project_kernel, places, len(extra)),
        in_specs=[vmem] * (5 + len(extra)),
        out_specs=[vmem] * count,
        out_shape=[jax.ShapeDtypeStruct((TOK, columns), dtype)] * count,
        scratch_shapes=[pltpu.VMEM((TOK, depth), jnp.bfloat16)],
        compiler_params=pltpu.CompilerParams(vmem_limit_bytes=VMEM_SMALL),
        cost_estimate=pl.CostEstimate(
            flops=2 * count * TOK * depth * columns,
            bytes_accessed=2 * count * depth * columns,
            transcendentals=0,
        ),
        name="project",
    )(*attended, out_weight, *extra)


def final_kernel(own_a, own_b, direct_a, direct_b, summed_a, summed_b, gate_ref, o_ref):
    columns = own_a.shape[1]
    for i, (own, direct, summed) in enumerate(
        ((own_a, direct_a, summed_a), (own_b, direct_b, summed_b))
    ):
        place = slice(i * columns, (i + 1) * columns)
        total = own[...] + direct[...].astype(jnp.float32) + summed[...].astype(jnp.float32)
        o_ref[:, place] = (total * gate_ref[:, place]).astype(o_ref.dtype)


def finish(halves, gate):
    rows, columns = halves[0].shape
    vmem = pl.BlockSpec(memory_space=pltpu.VMEM)
    return pl.pallas_call(
        final_kernel,
        in_specs=[vmem] * 7,
        out_specs=vmem,
        out_shape=jax.ShapeDtypeStruct((rows, 2 * columns), jnp.bfloat16),
        compiler_params=pltpu.CompilerParams(vmem_limit_bytes=VMEM_SMALL),
        name="finish",
    )(*halves, gate)


def shift(x, axis, step):
    size = lax.axis_size(axis)
    return lax.ppermute(x, axis, [(i, (i + step) % size) for i in range(size)])


def local(queries, keys, values, out_weight, gate_table, block_mask, levels):
    barrier = lax.optimization_barrier
    x, y, z, core = (lax.axis_index(name) for name in ("tp", "y", "z", "core"))

    visible = visible_matrix(block_mask).reshape(4, 4, 2, 4, 4, 2)
    seen = lax.dynamic_index_in_dim(visible, z, 1, keepdims=False)
    seen = jnp.stack(
        [lax.dynamic_index_in_dim(seen, (z + d) % 4, 3, keepdims=False) for d in (0, 3, 1, 2)],
        axis=3,
    )

    def bias_of(query_core, key_core, first, last):
        here = lax.dynamic_index_in_dim(seen, query_core, 1, keepdims=False)
        here = lax.dynamic_index_in_dim(here, key_core, 3, keepdims=False)[:, :, first:last]
        here = jnp.where(here, 0.0, masked_score).astype(jnp.float32)
        return jnp.repeat(here, TOK, axis=2).reshape(4, -1)

    biases = (
        jnp.stack([bias_of(core, core, 0, 3), bias_of(1 - core, core, 0, 3)]),
        bias_of(core, core, 3, 4)[None],
        bias_of(core, 1 - core, 3, 4)[None],
    )
    columns = gate_table.shape[1] // 4
    gate_part = lax.dynamic_slice(
        gate_table,
        (lax.dynamic_index_in_dim(levels, y, keepdims=False), x * columns),
        (1, columns),
    )

    (own, up, down, across), (q_own, q_up, q_down, q_across) = pack_by_owner(queries, keys, values)
    from_across = shift(across, "y", 2)
    from_down, from_up = shift(up, "y", 1), shift(down, "y", -1)
    own_before, own_after = shift(own, "z", 1), shift(own, "z", -1)
    own_far = shift(own_before, "z", 1)

    arrived = (from_down, from_up, from_across, q_up, q_down, q_across)
    arrived, own_before, own_after, own_far, biases, gate_part = barrier(
        (arrived, own_before, own_after, own_far, biases, gate_part)
    )
    from_down, from_up, from_across, q_up, q_down, q_across = arrived
    rest = stack(from_down, from_up, from_across)
    rest_before, rest_after = shift(rest, "z", 1), shift(rest, "z", -1)
    q_here = stack(q_own, shift(q_up, "y", 1), shift(q_down, "y", -1), shift(q_across, "y", 2))
    q_there = shift(q_here, "core", 1)
    own_near = stack(own, space=pltpu.VMEM)
    q_there, own_near, rest_before, rest_after = barrier(
        (q_there, own_near, rest_before, rest_after)
    )
    half = rest.shape[0] // 2
    far = (
        own_far,
        shift(take_rows(rest_before, 0, half), "z", 1),
        shift(take_rows(rest_after, half, half), "z", -1),
    )
    pieces = ((own_near, rest), (own_before, rest_before), (own_after, rest_after))
    f32, bf16 = jnp.float32, jnp.bfloat16
    state = (VIDEO_GROUPS, TOK, WIDTH)
    o_here, log_here, o_there, log_there = attend(
        near_kernel, biases[0], (q_here, q_there), pieces, (),
        [(state, f32), (state, f32), (state, bf16), ((VIDEO_GROUPS, TOK, HEAD_DIM), f32)],
    )
    o_here, far = barrier((o_here, far))
    far_there = tuple(shift(part, "core", 1) for part in far)
    here = attend(
        far_kernel, biases[1], (q_here,), (far,), (o_here, log_here),
        [(state, f32), (state, f32)],
    )
    there = (shift(o_there, "core", 1), shift(log_there, "core", 1))
    out, out_up, out_down, out_across = attend(
        last_kernel, biases[2], (q_here,), (far_there,), (*here, *there),
        [((TOK, WIDTH), bf16)] * 4, [pltpu.VMEM(state, bf16)],
    )
    attended = (out, shift(out_up, "y", 1), shift(out_down, "y", -1), shift(out_across, "y", 2))

    across_a, across_b = project(attended, out_weight, ((2, 0), (2, 1)))
    from_left, from_right = shift(across_a, "tp", 1), shift(across_b, "tp", -1)
    right_b, left_a = project(attended, out_weight, ((1, 1), (3, 0)))
    direct_b, direct_a = shift(right_b, "tp", 1), shift(left_a, "tp", -1)
    own_a, own_b = project(attended, out_weight, ((0, 0), (0, 1)), dtype=jnp.float32)
    right_a, left_b = project(
        attended, out_weight, ((1, 0), (3, 1)), (from_left, from_right)
    )
    summed_a, summed_b = shift(right_a, "tp", 1), shift(left_b, "tp", -1)
    return finish((own_a, own_b, direct_a, direct_b, summed_a, summed_b), gate_part)


def solution(mesh):
    fine = Mesh(mesh.devices.reshape(4, 4, 2, 4), ("y", "z", "core", "tp"))
    group = ("y", "z", "core")
    return jax.shard_map(
        local,
        mesh=fine,
        in_specs=(
            P(group, "tp"),
            P(group, "tp"),
            P(group, "tp"),
            P("tp", None),
            P(),
            P(),
            P(),
        ),
        out_specs=P(group, "tp"),
        check_vma=False,
    )
```

time: 162 us -> 90.1 us (0.56); the launches traced: 159 us -> 89.8 us
  waiting for transfers between devices: 69.9 us -> 25.5 us
  blocking collectives: 37.6 us -> 0 us
  starting transfers between devices: 0.04 us -> 33.5 us
  between operations: 15.5 us -> 2.16 us
  matrix products: 10.9 us -> 0 us
  Pallas kernels: 18.1 us -> 21.5 us
    all_gather x1 -> x0, waiting for transfers between devices: 47.5 us -> none  [local(): kv = lax.all_gather(kv, ('z', 'core'), axis=0, tiled=True)]
    all_to_all x2 -> x0, blocking collectives: 37.6 us -> none  [the longest x1 23.9 us: local(): lax.all_to_all(jnp.transpose(parts, (1, 0, 2)), 'y', 0, 0, tiled=True)]
    ppermute x0 -> x28, starting transfers between devices: none -> 33.5 us  [shift(): return lax.ppermute(x, axis, [(i, (i + step) % size) for i in range(size)])]
    ppermute x0 -> x28, waiting for transfers between devices: none -> 25.5 us  [shift(): return lax.ppermute(x, axis, [(i, (i + step) % size) for i in range(size)])]
    reduce_scatter x1 -> x0, waiting for transfers between devices: 22.4 us -> none  [local(): lax.psum_scatter(head_terms.astype(jnp.bfloat16), 'tp', scatter_dimension...]
    dot_general x1 -> x0, matrix products: 10.9 us -> none  [local(): jnp.dot(attended, out_weight, preferred_element_type=jnp.float32)]
    pallas_call x1 -> x14, Pallas kernels: 18.1 us -> 21.5 us  [the longest x3 11.9 us: attend(): pl.pallas_call(kernel, in_specs=[vmem] * len(operands), out_specs=[vmem]...]
    reshape x5 -> x1, local copies, waits for them, and re-layouts: 2.7 us -> 0.19 us  [local(): visible = visible_matrix(block_mask).reshape(4, 4, 2, 4, 4, 2)]
  transfers between devices with their start and end apart: 2 -> 28, of which waited for: 2 -> 14; matrix products, arithmetic and copies ran while one was open for 1% -> 6% of each run, Pallas kernels for 0% -> 15%
where the time goes in v3:
time: 90.1 us; the launch traced here: 89.8 us
  starting transfers between devices  33.5 us (37%)
  waiting for transfers between devices  25.5 us (28%)
  Pallas kernels  21.5 us (24%)
  local copies, waits for them, and re-layouts  6.02 us (7%)
  between operations  2.16 us (2%)
  other arithmetic  1.15 us (1%)
    ppermute x28, starting transfers between devices, shift(): return lax.ppermute(x, axis, [(i, (i + step) % size) for i in range(size)])  33.5 us
    ppermute x28, waiting for transfers between devices, shift(): return lax.ppermute(x, axis, [(i, (i + step) % size) for i in range(size)])  25.5 us
    pallas_call x3, Pallas kernels, attend(): pl.pallas_call(kernel, in_specs=[vmem] * len(operands), out_specs=[vmem]...  11.9 us
    pallas_call x4, Pallas kernels, project(): pl.pallas_call(functools.partial(project_kernel, places, len(extra)), in_...  4.11 us
    pallas_call x1, Pallas kernels, pack_by_owner(): pl.pallas_call(pack_kernel, in_specs=[hbm, hbm, hbm], out_specs=[hbm] * 8...  2.35 us
    pallas_call x3, Pallas kernels, stack(): pl.pallas_call(stack_kernel, in_specs=[pl.BlockSpec(memory_space=pltpu.VM...  1.88 us
    unnamed x14, local copies, waits for them, and re-layouts  1.86 us
  transfers between devices with their start and end apart: 28, of which 14 were waited for; matrix products, arithmetic and copies ran while one was open for 6% of the time, Pallas kernels for 15%

profile of v3, /device:TPU:6, one launch (start us, length us, event | category | flops | bytes accessed | tf_op | source)
XLA Modules:
  0.0 89.8 jit_solution(11978655515795418789)
XLA Ops:
  0.0 2.4 %pack_by_owner.1 = (bf16[160,768]{1,0:T(8,128)(2,1)}, bf16[160,768]{1,0:T(8,128)(2,1)}, bf16[160,768]{1,0:T(8,128)(2,1)}, bf16[160,768]{1,0:T(8,128)(2,1)}, bf16...) custom-call(bf16[160,1536]{1,0:T(8,128)(2,1)} %queries.1, ...), custom_call_target="tpu_custom_call" | custom-call | tf_op jit(solution)/shard_map/pack_by_owner/pallas_call | solution.py:88
  2.4 2.0 %collective-permute-start.3 = (bf16[160,768]{1,0:T(8,128)(2,1)}, bf16[160,768]{1,0:T(8,128)(2,1)S(1)}, u32[]{:S(2)}, u32[]{:S(2)}) collective-permute-start(bf16[160,768]{1,0:T(8,128)(2,1)} %get-tuple-element.58.refs_0_), channel_id=1, source_target_pairs={{0,8},{8,16},{16,24},{24,0},{1,9},{9,17},{17,25},{25,1},{2,10},{10... | collective-permute-start | bytes 737288 | tf_op jit(solution)/shard_map/ppermute | solution.py:323
  4.3 2.2 %collective-permute-start.4 = (bf16[160,768]{1,0:T(8,128)(2,1)}, bf16[160,768]{1,0:T(8,128)(2,1)S(1)}, u32[]{:S(2)}, u32[]{:S(2)}) collective-permute-start(bf16[160,768]{1,0:T(8,128)(2,1)} %get-tuple-element.58.refs_0_), channel_id=1, source_target_pairs={{0,24},{8,0},{16,8},{24,16},{1,25},{9,1},{17,9},{25,17},{2,26},{10... | collective-permute-start | bytes 737288 | tf_op jit(solution)/shard_map/ppermute | solution.py:323
  6.5 1.6 %collective-permute-start = (bf16[160,768]{1,0:T(8,128)(2,1)}, bf16[160,768]{1,0:T(8,128)(2,1)S(1)}, u32[]{:S(2)}, u32[]{:S(2)}) collective-permute-start(bf16[160,768]{1,0:T(8,128)(2,1)} %get-tuple-element.52), channel_id=1, source_target_pairs={{0,32},{32,64},{64,96},{96,0},{1,33},{33,65},{65,97},{97,1},{2,34}... | collective-permute-start | bytes 737288 | tf_op jit(solution)/shard_map/ppermute | solution.py:323
  8.1 1.7 %collective-permute-start.1 = (bf16[160,768]{1,0:T(8,128)(2,1)}, bf16[160,768]{1,0:T(8,128)(2,1)S(1)}, u32[]{:S(2)}, u32[]{:S(2)}) collective-permute-start(bf16[160,768]{1,0:T(8,128)(2,1)} %get-tuple-element.53), channel_id=1, source_target_pairs={{0,96},{32,0},{64,32},{96,64},{1,97},{33,1},{65,33},{97,65},{2,98}... | collective-permute-start | bytes 737288 | tf_op jit(solution)/shard_map/ppermute | solution.py:323
  9.8 2.0 %collective-permute-start.2 = (bf16[160,768]{1,0:T(8,128)(2,1)}, bf16[160,768]{1,0:T(8,128)(2,1)S(1)}, u32[]{:S(2)}, u32[]{:S(2)}) collective-permute-start(bf16[160,768]{1,0:T(8,128)(2,1)} %get-tuple-element.54), channel_id=1, source_target_pairs={{0,64},{32,96},{64,0},{96,32},{1,65},{33,97},{65,1},{97,33},{2,66}... | collective-permute-start | bytes 737288 | tf_op jit(solution)/shard_map/ppermute | solution.py:323
  11.8 0.8 fusion
  12.6 0.2 reshape.89
  12.9 0.1 copy.15
  13.0 0.1 copy.16
  13.2 0.1 copy.17
  13.3 0.1 copy.18
  13.5 0.1 copy.19
  13.6 0.2 select_reduce_fusion.1
  13.8 0.1 copy.20
  13.9 0.1 copy.21
  14.2 0.2 select_reduce_fusion
  15.1 1.3 %dynamic_slice.57 = s32[1]{0:T(128)} dynamic-slice(s32[4]{0:T(128)} %param.13, s32[]{:T(128)S(6)} %select_n.135), dynamic_slice_sizes={1} | dynamic-slice | bytes 12 | tf_op jit(solution)/shard_map/jit(dynamic_index_in_dim)/dynamic_slice | solution.py:351
  18.2 0.9 dynamic_slice.58.gate_ref
  19.1 2.8 %collective-permute-done.2.refs_2_ = bf16[160,768]{1,0:T(8,128)(2,1)S(1)} collective-permute-done((bf16[160,768]{1,0:T(8,128)(2,1)}, bf16[160,768]{1,0:T(8,128)(2,1)S(1)}, u32[]{:S(2)}, u32[]{:S(2)}) %collective-permute-start.2) | collective-permute-done | bytes 245792 | tf_op jit(solution)/shard_map/ppermute | solution.py:323
  21.9 0.9 %stack.17.refs_3_ = bf16[480,768]{1,0:T(8,128)(2,1)S(1)} custom-call(bf16[160,768]{1,0:T(8,128)(2,1)S(1)} %collective-permute-done.refs_0_, bf16[160,768]{1,0:T(8,128)(2,1)S(1)} %collective-permute-done.1.refs_1_, bf16[160,768]{1,0:T(8,128)(2,1)S(1)} %collective-permute-done.2.refs_2_), custom_call_target="tpu_custom_call" | custom-call | tf_op jit(solution)/shard_map/stack/pallas_call | solution.py:118
  23.0 3.2 %collective-permute-start.11 = (bf16[480,768]{1,0:T(8,128)(2,1)S(1)}, bf16[480,768]{1,0:T(8,128)(2,1)S(1)}, u32[]{:S(2)}, u32[]{:S(2)}) collective-permute-start(bf16[480,768]{1,0:T(8,128)(2,1)S(1)} %stack.17.refs_3_), channel_id=1, source_target_pairs={{0,24},{8,0},{16,8},{24,16},{1,25},{9,1},{17,9},{25,17},{2,26},{10... | collective-permute-start | bytes 2211848 | tf_op jit(solution)/shard_map/ppermute | solution.py:323
  26.2 1.1 %collective-permute-start.6 = (bf16[160,384]{1,0:T(8,128)(2,1)}, bf16[160,384]{1,0:T(8,128)(2,1)S(1)}, u32[]{:S(2)}, u32[]{:S(2)}) collective-permute-start(bf16[160,384]{1,0:T(8,128)(2,1)} %get-tuple-element.61), channel_id=1, source_target_pairs={{0,32},{32,64},{64,96},{96,0},{1,33},{33,65},{65,97},{97,1},{2,34}... | collective-permute-start | bytes 368648 | tf_op jit(solution)/shard_map/ppermute | solution.py:323
  27.3 2.1 %collective-permute-start.7 = (bf16[160,384]{1,0:T(8,128)(2,1)}, bf16[160,384]{1,0:T(8,128)(2,1)S(1)}, u32[]{:S(2)}, u32[]{:S(2)}) collective-permute-start(bf16[160,384]{1,0:T(8,128)(2,1)} %get-tuple-element.62), channel_id=1, source_target_pairs={{0,96},{32,0},{64,32},{96,64},{1,97},{33,1},{65,33},{97,65},{2,98}... | collective-permute-start | bytes 368648 | tf_op jit(solution)/shard_map/ppermute | solution.py:323
  29.4 1.0 %collective-permute-start.8 = (bf16[160,384]{1,0:T(8,128)(2,1)}, bf16[160,384]{1,0:T(8,128)(2,1)S(1)}, u32[]{:S(2)}, u32[]{:S(2)}) collective-permute-start(bf16[160,384]{1,0:T(8,128)(2,1)} %get-tuple-element.63), channel_id=1, source_target_pairs={{0,64},{32,96},{64,0},{96,32},{1,65},{33,97},{65,1},{97,33},{2,66}... | collective-permute-start | bytes 368648 | tf_op jit(solution)/shard_map/ppermute | solution.py:323
  30.5 3.3 %collective-permute-done.6.refs_1_ = bf16[160,384]{1,0:T(8,128)(2,1)S(1)} collective-permute-done((bf16[160,384]{1,0:T(8,128)(2,1)}, bf16[160,384]{1,0:T(8,128)(2,1)S(1)}, u32[]{:S(2)}, u32[]{:S(2)}) %collective-permute-start.6) | collective-permute-done | bytes 122912 | tf_op jit(solution)/shard_map/ppermute | solution.py:323
  33.8 2.2 %collective-permute-done.8.refs_3_ = bf16[160,384]{1,0:T(8,128)(2,1)S(1)} collective-permute-done((bf16[160,384]{1,0:T(8,128)(2,1)}, bf16[160,384]{1,0:T(8,128)(2,1)S(1)}, u32[]{:S(2)}, u32[]{:S(2)}) %collective-permute-start.8) | collective-permute-done | bytes 122912 | tf_op jit(solution)/shard_map/ppermute | solution.py:323
  36.0 0.9 %copy-done.1 = bf16[160,384]{1,0:T(8,128)(2,1)S(1)} copy-done((bf16[160,384]{1,0:T(8,128)(2,1)S(1)}, bf16[160,384]{1,0:T(8,128)(2,1)}, u32[]{:S(2)}) %copy-start.1) | copy-done | bytes 122904
  36.9 0.6 stack.15.refs_0_.q
  37.7 0.9 %copy-done = bf16[160,768]{1,0:T(8,128)(2,1)S(1)} copy-done((bf16[160,768]{1,0:T(8,128)(2,1)S(1)}, bf16[160,768]{1,0:T(8,128)(2,1)}, u32[]{:S(2)}) %copy-start) | copy-done | bytes 245784
  38.6 0.3 stack.16.refs_2_
  38.9 0.6 collective-permute-done.9.refs_1_
  39.5 1.7 %collective-permute-done.10.refs_5_.x_ref = bf16[480,768]{1,0:T(8,128)(2,1)S(1)} collective-permute-done((bf16[480,768]{1,0:T(8,128)(2,1)S(1)}, bf16[480,768]{1,0:T(8,128)(2,1)S(1)}, u32[]{:S(2)}, u32[]{:S(2)}) %collective-permute-start.10) | collective-permute-done | bytes 737312 | tf_op jit(solution)/shard_map/ppermute | solution.py:323
  41.2 0.2 take_rows.2
  41.4 0.2 take_rows.3
  41.6 3.5 %collective-permute-start.13 = (bf16[240,768]{1,0:T(8,128)(2,1)S(1)}, bf16[240,768]{1,0:T(8,128)(2,1)S(1)}, u32[]{:S(2)}, u32[]{:S(2)}) collective-permute-start(bf16[240,768]{1,0:T(8,128)(2,1)S(1)} %take_rows.3), channel_id=1, source_target_pairs={{0,24},{8,0},{16,8},{24,16},{1,25},{9,1},{17,9},{25,17},{2,26},{10... | collective-permute-start | bytes 1105928 | tf_op jit(solution)/shard_map/ppermute | solution.py:323
  45.1 7.2 %near_kernel.1 = (f32[4,160,384]{2,1,0:T(8,128)S(1)}, f32[4,160,384]{2,1,0:T(8,128)S(1)}, bf16[4,160,384]{2,1,0:T(8,128)(2,1)S(1)}, f32[4,160,128]{2,1,0:T(8,128)S(1)}) custom-call(f32[2,4,1920]{2,1,0:T(4,128)S(1)} %pad_maximum_fusion.bias_ref, bf16[640,384]{1,0:T(8,128)(2,1)S(1)} %stack.15.refs_0_.q, bf16[640,384]{1,0:T(8,128)(2,1)S(1)} %collective-permute-done.9.refs_1_, ...), custom_call_target="tpu_custom_call" | custom-call | flops 12000000000 | bytes 1048576 | tf_op jit(solution)/shard_map/near_kernel/pallas_call | solution.py:243
  52.4 0.5 collective-permute-start.18
  53.0 0.4 collective-permute-start.16
  53.6 2.1 %far_kernel.1 = (f32[4,160,384]{2,1,0:T(8,128)S(1)}, f32[4,160,384]{2,1,0:T(8,128)S(1)}) custom-call(f32[1,4,640]{2,1,0:T(4,128)S(1)} %broadcast_in_dim_reshape_reshape.6.bias_ref, bf16[640,384]{1,0:T(8,128)(2,1)S(1)} %stack.15.refs_0_.q, bf16[160,768]{1,0:T(8,128)(2,1)S(1)} %collective-permute-done.5.refs_0_, ...), custom_call_target="tpu_custom_call" | custom-call | flops 4000000000 | bytes 1048576 | tf_op jit(solution)/shard_map/far_kernel/pallas_call | solution.py:243
  55.7 0.5 collective-permute-done.14.refs_0_
  56.2 2.5 %last_kernel.1 = (bf16[160,384]{1,0:T(8,128)(2,1)S(1)}, bf16[160,384]{1,0:T(8,128)(2,1)S(1)}, bf16[160,384]{1,0:T(8,128)(2,1)S(1)}, bf16[160,384]{1,0:T(8,128)(2,1)S(1)}) custom-call(f32[1,4,640]{2,1,0:T(4,128)S(1)} %broadcast_in_dim_reshape_reshape.7.bias_ref, bf16[640,384]{1,0:T(8,128)(2,1)S(1)} %stack.15.refs_0_.q, ...), custom_call_target="tpu_custom_call" | custom-call | flops 4000000000 | bytes 1048576 | tf_op jit(solution)/shard_map/last_kernel/pallas_call | solution.py:243
  58.7 0.9 %collective-permute-start.19 = (bf16[160,384]{1,0:T(8,128)(2,1)S(1)}, bf16[160,384]{1,0:T(8,128)(2,1)S(1)}, u32[]{:S(2)}, u32[]{:S(2)}) collective-permute-start(bf16[160,384]{1,0:T(8,128)(2,1)S(1)} %get-tuple-element.87), channel_id=1, source_target_pairs={{0,32},{32,64},{64,96},{96,0},{1,33},{33,65},{65,97},{97,1},{2,34}... | collective-permute-start | bytes 368648 | tf_op jit(solution)/shard_map/ppermute | solution.py:323
  59.6 2.4 %collective-permute-start.20 = (bf16[160,384]{1,0:T(8,128)(2,1)S(1)}, bf16[160,384]{1,0:T(8,128)(2,1)S(1)}, u32[]{:S(2)}, u32[]{:S(2)}) collective-permute-start(bf16[160,384]{1,0:T(8,128)(2,1)S(1)} %get-tuple-element.88), channel_id=1, source_target_pairs={{0,96},{32,0},{64,32},{96,64},{1,97},{33,1},{65,33},{97,65},{2,98}... | collective-permute-start | bytes 368648 | tf_op jit(solution)/shard_map/ppermute | solution.py:323
  62.0 0.8 collective-permute-start.21
  62.8 2.5 %collective-permute-done.19.refs_1_ = bf16[160,384]{1,0:T(8,128)(2,1)S(1)} collective-permute-done((bf16[160,384]{1,0:T(8,128)(2,1)S(1)}, bf16[160,384]{1,0:T(8,128)(2,1)S(1)}, u32[]{:S(2)}, u32[]{:S(2)}) %collective-permute-start.19) | collective-permute-done | bytes 122912 | tf_op jit(solution)/shard_map/ppermute | solution.py:323
  65.4 1.9 %collective-permute-done.20.refs_2_ = bf16[160,384]{1,0:T(8,128)(2,1)S(1)} collective-permute-done((bf16[160,384]{1,0:T(8,128)(2,1)S(1)}, bf16[160,384]{1,0:T(8,128)(2,1)S(1)}, u32[]{:S(2)}, u32[]{:S(2)}) %collective-permute-start.20) | collective-permute-done | bytes 122912 | tf_op jit(solution)/shard_map/ppermute | solution.py:323
  67.3 1.1 %collective-permute-done.21.refs_3_ = bf16[160,384]{1,0:T(8,128)(2,1)S(1)} collective-permute-done((bf16[160,384]{1,0:T(8,128)(2,1)S(1)}, bf16[160,384]{1,0:T(8,128)(2,1)S(1)}, u32[]{:S(2)}, u32[]{:S(2)}) %collective-permute-start.21) | collective-permute-done | bytes 122912 | tf_op jit(solution)/shard_map/ppermute | solution.py:323
  68.5 1.0 %project.6 = (bf16[160,768]{1,0:T(8,128)(2,1)S(1)}, bf16[160,768]{1,0:T(8,128)(2,1)S(1)}) custom-call(bf16[160,384]{1,0:T(8,128)(2,1)S(1)} %get-tuple-element.86.refs_0_, bf16[160,384]{1,0:T(8,128)(2,1)S(1)} %collective-permute-done.19.refs_1_, bf16[160,384]{1,0:T(8,128)(2,1)S(1)} %collective-permute-done.20.refs_2_, ...), custom_call_target="tpu_custom_call" | custom-call | flops 754974720 | bytes 4718592 | tf_op jit(solution)/shard_map/project/pallas_call | solution.py:282
  69.5 0.5 collective-permute-start.24
  70.0 1.5 %collective-permute-start.25 = (bf16[160,768]{1,0:T(8,128)(2,1)S(1)}, bf16[160,768]{1,0:T(8,128)(2,1)S(1)}, u32[]{:S(2)}, u32[]{:S(2)}) collective-permute-start(bf16[160,768]{1,0:T(8,128)(2,1)S(1)} %get-tuple-element.95), channel_id=1, source_target_pairs={{0,3},{1,0},{2,1},{3,2},{4,7},{5,4},{6,5},{7,6},{8,11},{9,8},{10,9... | collective-permute-start | bytes 737288 | tf_op jit(solution)/shard_map/ppermute | solution.py:323
  71.6 1.0 %project.5 = (bf16[160,768]{1,0:T(8,128)(2,1)S(1)}, bf16[160,768]{1,0:T(8,128)(2,1)S(1)}) custom-call(bf16[160,384]{1,0:T(8,128)(2,1)S(1)} %get-tuple-element.86.refs_0_, bf16[160,384]{1,0:T(8,128)(2,1)S(1)} %collective-permute-done.19.refs_1_, bf16[160,384]{1,0:T(8,128)(2,1)S(1)} %collective-permute-done.20.refs_2_, ...), custom_call_target="tpu_custom_call" | custom-call | flops 754974720 | bytes 4718592 | tf_op jit(solution)/shard_map/project/pallas_call | solution.py:282
  72.6 0.9 collective-permute-start.22
  73.5 2.4 %collective-permute-start.23 = (bf16[160,768]{1,0:T(8,128)(2,1)S(1)}, bf16[160,768]{1,0:T(8,128)(2,1)S(1)}, u32[]{:S(2)}, u32[]{:S(2)}) collective-permute-start(bf16[160,768]{1,0:T(8,128)(2,1)S(1)} %get-tuple-element.93), channel_id=1, source_target_pairs={{0,1},{1,2},{2,3},{3,0},{4,5},{5,6},{6,7},{7,4},{8,9},{9,10},{10,1... | collective-permute-start | bytes 737288 | tf_op jit(solution)/shard_map/ppermute | solution.py:323
  75.9 2.1 %collective-permute-done.24.refs_5_ = bf16[160,768]{1,0:T(8,128)(2,1)S(1)} collective-permute-done((bf16[160,768]{1,0:T(8,128)(2,1)S(1)}, bf16[160,768]{1,0:T(8,128)(2,1)S(1)}, u32[]{:S(2)}, u32[]{:S(2)}) %collective-permute-start.24) | collective-permute-done | bytes 245792 | tf_op jit(solution)/shard_map/ppermute | solution.py:323
  78.1 2.0 %collective-permute-done.25.refs_6_ = bf16[160,768]{1,0:T(8,128)(2,1)S(1)} collective-permute-done((bf16[160,768]{1,0:T(8,128)(2,1)S(1)}, bf16[160,768]{1,0:T(8,128)(2,1)S(1)}, u32[]{:S(2)}, u32[]{:S(2)}) %collective-permute-start.25) | collective-permute-done | bytes 245792 | tf_op jit(solution)/shard_map/ppermute | solution.py:323
  80.0 1.0 %project.7 = (bf16[160,768]{1,0:T(8,128)(2,1)S(1)}, bf16[160,768]{1,0:T(8,128)(2,1)S(1)}) custom-call(bf16[160,384]{1,0:T(8,128)(2,1)S(1)} %get-tuple-element.86.refs_0_, bf16[160,384]{1,0:T(8,128)(2,1)S(1)} %collective-permute-done.19.refs_1_, bf16[160,384]{1,0:T(8,128)(2,1)S(1)} %collective-permute-done.20.refs_2_, ...), custom_call_target="tpu_custom_call" | custom-call | flops 754974720 | bytes 4718592 | tf_op jit(solution)/shard_map/project/pallas_call | solution.py:282
  81.1 0.4 collective-permute-start.26
  81.4 1.7 %collective-permute-start.27 = (bf16[160,768]{1,0:T(8,128)(2,1)S(1)}, bf16[160,768]{1,0:T(8,128)(2,1)S(1)}, u32[]{:S(2)}, u32[]{:S(2)}) collective-permute-start(bf16[160,768]{1,0:T(8,128)(2,1)S(1)} %get-tuple-element.97), channel_id=1, source_target_pairs={{0,3},{1,0},{2,1},{3,2},{4,7},{5,4},{6,5},{7,6},{8,11},{9,8},{10,9... | collective-permute-start | bytes 737288 | tf_op jit(solution)/shard_map/ppermute | solution.py:323
  83.2 1.0 %project.4 = (f32[160,768]{1,0:T(8,128)S(1)}, f32[160,768]{1,0:T(8,128)S(1)}) custom-call(bf16[160,384]{1,0:T(8,128)(2,1)S(1)} %get-tuple-element.86.refs_0_, bf16[160,384]{1,0:T(8,128)(2,1)S(1)} %collective-permute-done.19.refs_1_, bf16[160,384]{1,0:T(8,128)(2,1)S(1)} %collective-permute-done.20.refs_2_, ...), custom_call_target="tpu_custom_call" | custom-call | flops 754974720 | bytes 4718592 | tf_op jit(solution)/shard_map/project/pallas_call | solution.py:282
  84.2 1.0 %collective-permute-done.22.direct_a = bf16[160,768]{1,0:T(8,128)(2,1)S(1)} collective-permute-done((bf16[160,768]{1,0:T(8,128)(2,1)S(1)}, bf16[160,768]{1,0:T(8,128)(2,1)S(1)}, u32[]{:S(2)}, u32[]{:S(2)}) %collective-permute-start.22) | collective-permute-done | bytes 245792 | tf_op jit(solution)/shard_map/ppermute | solution.py:323
  85.2 2.2 %collective-permute-done.26.summed_a = bf16[160,768]{1,0:T(8,128)(2,1)S(1)} collective-permute-done((bf16[160,768]{1,0:T(8,128)(2,1)S(1)}, bf16[160,768]{1,0:T(8,128)(2,1)S(1)}, u32[]{:S(2)}, u32[]{:S(2)}) %collective-permute-start.26) | collective-permute-done | bytes 245792 | tf_op jit(solution)/shard_map/ppermute | solution.py:323
  87.4 1.5 %collective-permute-done.27.summed_b = bf16[160,768]{1,0:T(8,128)(2,1)S(1)} collective-permute-done((bf16[160,768]{1,0:T(8,128)(2,1)S(1)}, bf16[160,768]{1,0:T(8,128)(2,1)S(1)}, u32[]{:S(2)}, u32[]{:S(2)}) %collective-permute-start.27) | collective-permute-done | bytes 245792 | tf_op jit(solution)/shard_map/ppermute | solution.py:323
  88.8 1.0 %finish.1 = bf16[160,1536]{1,0:T(8,128)(2,1)} custom-call(f32[160,768]{1,0:T(8,128)S(1)} %get-tuple-element.90.own_a, f32[160,768]{1,0:T(8,128)S(1)} %get-tuple-element.91.own_b, bf16[160,768]{1,0:T(8,128)(2,1)S(1)} %collective-permute-done.22.direct_a, bf16[160,768]{1,0:T(8,128)(2,1)S(1)} %collective-permute-done.23.direct_b, ...), custom_call_target="tpu_custom_call" | custom-call | tf_op jit(solution)/shard_map/finish/pallas_call | solution.py:311
  (49 shorter events, 1.6 us)
Async XLA Ops:
  2.4 11.7 %collective-permute-start.3 = (bf16[160,768]{1,0:T(8,128)(2,1)}, bf16[160,768]{1,0:T(8,128)(2,1)S(1)}, u32[]{:S(2)}, u32[]{:S(2)}) collective-permute-start(bf16[160,768]{1,0:T(8,128)(2,1)} %get-tuple-element.58.refs_0_), channel_id=1, source_target_pairs={{0,8},{8,16},{16,24},{24,0},{1,9},{9,17},{17,25},{25,1},{2,10},{10... | collective-permute-start | bytes 737288 | tf_op jit(solution)/shard_map/ppermute | solution.py:323
  4.3 14.7 %collective-permute-start.4 = (bf16[160,768]{1,0:T(8,128)(2,1)}, bf16[160,768]{1,0:T(8,128)(2,1)S(1)}, u32[]{:S(2)}, u32[]{:S(2)}) collective-permute-start(bf16[160,768]{1,0:T(8,128)(2,1)} %get-tuple-element.58.refs_0_), channel_id=1, source_target_pairs={{0,24},{8,0},{16,8},{24,16},{1,25},{9,1},{17,9},{25,17},{2,26},{10... | collective-permute-start | bytes 737288 | tf_op jit(solution)/shard_map/ppermute | solution.py:323
  6.5 12.5 %collective-permute-start = (bf16[160,768]{1,0:T(8,128)(2,1)}, bf16[160,768]{1,0:T(8,128)(2,1)S(1)}, u32[]{:S(2)}, u32[]{:S(2)}) collective-permute-start(bf16[160,768]{1,0:T(8,128)(2,1)} %get-tuple-element.52), channel_id=1, source_target_pairs={{0,32},{32,64},{64,96},{96,0},{1,33},{33,65},{65,97},{97,1},{2,34}... | collective-permute-start | bytes 737288 | tf_op jit(solution)/shard_map/ppermute | solution.py:323
  8.1 11.0 %collective-permute-start.1 = (bf16[160,768]{1,0:T(8,128)(2,1)}, bf16[160,768]{1,0:T(8,128)(2,1)S(1)}, u32[]{:S(2)}, u32[]{:S(2)}) collective-permute-start(bf16[160,768]{1,0:T(8,128)(2,1)} %get-tuple-element.53), channel_id=1, source_target_pairs={{0,96},{32,0},{64,32},{96,64},{1,97},{33,1},{65,33},{97,65},{2,98}... | collective-permute-start | bytes 737288 | tf_op jit(solution)/shard_map/ppermute | solution.py:323
  9.8 12.1 %collective-permute-start.2 = (bf16[160,768]{1,0:T(8,128)(2,1)}, bf16[160,768]{1,0:T(8,128)(2,1)S(1)}, u32[]{:S(2)}, u32[]{:S(2)}) collective-permute-start(bf16[160,768]{1,0:T(8,128)(2,1)} %get-tuple-element.54), channel_id=1, source_target_pairs={{0,64},{32,96},{64,0},{96,32},{1,65},{33,97},{65,1},{97,33},{2,66}... | collective-permute-start | bytes 737288 | tf_op jit(solution)/shard_map/ppermute | solution.py:323
  14.1 7.9 %collective-permute-start.5 = (bf16[160,768]{1,0:T(8,128)(2,1)S(1)}, bf16[160,768]{1,0:T(8,128)(2,1)S(1)}, u32[]{:S(2)}, u32[]{:S(2)}) collective-permute-start(bf16[160,768]{1,0:T(8,128)(2,1)S(1)} %collective-permute-done.3.refs_4_), channel_id=1, source_target_pairs={{0,8},{8,16},{16,24},{24,0},{1,9},{9,17},{17,25},{25,1},{2,10},{10... | collective-permute-start | bytes 737288 | tf_op jit(solution)/shard_map/ppermute | solution.py:323
  22.9 18.3 %collective-permute-start.10 = (bf16[480,768]{1,0:T(8,128)(2,1)S(1)}, bf16[480,768]{1,0:T(8,128)(2,1)S(1)}, u32[]{:S(2)}, u32[]{:S(2)}) collective-permute-start(bf16[480,768]{1,0:T(8,128)(2,1)S(1)} %stack.17.refs_3_), channel_id=1, source_target_pairs={{0,8},{8,16},{16,24},{24,0},{1,9},{9,17},{17,25},{25,1},{2,10},{10... | collective-permute-start | bytes 2211848 | tf_op jit(solution)/shard_map/ppermute | solution.py:323
  23.0 18.2 %collective-permute-start.11 = (bf16[480,768]{1,0:T(8,128)(2,1)S(1)}, bf16[480,768]{1,0:T(8,128)(2,1)S(1)}, u32[]{:S(2)}, u32[]{:S(2)}) collective-permute-start(bf16[480,768]{1,0:T(8,128)(2,1)S(1)} %stack.17.refs_3_), channel_id=1, source_target_pairs={{0,24},{8,0},{16,8},{24,16},{1,25},{9,1},{17,9},{25,17},{2,26},{10... | collective-permute-start | bytes 2211848 | tf_op jit(solution)/shard_map/ppermute | solution.py:323
  26.2 7.6 %collective-permute-start.6 = (bf16[160,384]{1,0:T(8,128)(2,1)}, bf16[160,384]{1,0:T(8,128)(2,1)S(1)}, u32[]{:S(2)}, u32[]{:S(2)}) collective-permute-start(bf16[160,384]{1,0:T(8,128)(2,1)} %get-tuple-element.61), channel_id=1, source_target_pairs={{0,32},{32,64},{64,96},{96,0},{1,33},{33,65},{65,97},{97,1},{2,34}... | collective-permute-start | bytes 368648 | tf_op jit(solution)/shard_map/ppermute | solution.py:323
  27.3 6.5 %collective-permute-start.7 = (bf16[160,384]{1,0:T(8,128)(2,1)}, bf16[160,384]{1,0:T(8,128)(2,1)S(1)}, u32[]{:S(2)}, u32[]{:S(2)}) collective-permute-start(bf16[160,384]{1,0:T(8,128)(2,1)} %get-tuple-element.62), channel_id=1, source_target_pairs={{0,96},{32,0},{64,32},{96,64},{1,97},{33,1},{65,33},{97,65},{2,98}... | collective-permute-start | bytes 368648 | tf_op jit(solution)/shard_map/ppermute | solution.py:323
  29.4 6.6 %collective-permute-start.8 = (bf16[160,384]{1,0:T(8,128)(2,1)}, bf16[160,384]{1,0:T(8,128)(2,1)S(1)}, u32[]{:S(2)}, u32[]{:S(2)}) collective-permute-start(bf16[160,384]{1,0:T(8,128)(2,1)} %get-tuple-element.63), channel_id=1, source_target_pairs={{0,64},{32,96},{64,0},{96,32},{1,65},{33,97},{65,1},{97,33},{2,66}... | collective-permute-start | bytes 368648 | tf_op jit(solution)/shard_map/ppermute | solution.py:323
  36.0 0.9 %copy-start.1 = (bf16[160,384]{1,0:T(8,128)(2,1)S(1)}, bf16[160,384]{1,0:T(8,128)(2,1)}, u32[]{:S(2)}) copy-start(bf16[160,384]{1,0:T(8,128)(2,1)} %get-tuple-element.60.refs_0_) | copy-start | bytes 368644
  37.6 1.9 %collective-permute-start.9 = (bf16[640,384]{1,0:T(8,128)(2,1)S(1)}, bf16[640,384]{1,0:T(8,128)(2,1)S(1)}, u32[]{:S(2)}, u32[]{:S(2)}) collective-permute-start(bf16[640,384]{1,0:T(8,128)(2,1)S(1)} %stack.15.refs_0_.q), channel_id=1, source_target_pairs={{0,4},{4,0},{1,5},{5,1},{2,6},{6,2},{3,7},{7,3},{8,12},{12,8},{9,1... | collective-permute-start | bytes 1474568 | tf_op jit(solution)/shard_map/ppermute | solution.py:323
  37.7 0.9 %copy-start = (bf16[160,768]{1,0:T(8,128)(2,1)S(1)}, bf16[160,768]{1,0:T(8,128)(2,1)}, u32[]{:S(2)}) copy-start(bf16[160,768]{1,0:T(8,128)(2,1)} %get-tuple-element.58.refs_0_) | copy-start | bytes 737284
  41.4 11.6 %collective-permute-start.12 = (bf16[240,768]{1,0:T(8,128)(2,1)S(1)}, bf16[240,768]{1,0:T(8,128)(2,1)S(1)}, u32[]{:S(2)}, u32[]{:S(2)}) collective-permute-start(bf16[240,768]{1,0:T(8,128)(2,1)S(1)} %take_rows.2), channel_id=1, source_target_pairs={{0,8},{8,16},{16,24},{24,0},{1,9},{9,17},{17,25},{25,1},{2,10},{10... | collective-permute-start | bytes 1105928 | tf_op jit(solution)/shard_map/ppermute | solution.py:323
  41.6 11.3 %collective-permute-start.13 = (bf16[240,768]{1,0:T(8,128)(2,1)S(1)}, bf16[240,768]{1,0:T(8,128)(2,1)S(1)}, u32[]{:S(2)}, u32[]{:S(2)}) collective-permute-start(bf16[240,768]{1,0:T(8,128)(2,1)S(1)} %take_rows.3), channel_id=1, source_target_pairs={{0,24},{8,0},{16,8},{24,16},{1,25},{9,1},{17,9},{25,17},{2,26},{10... | collective-permute-start | bytes 1105928 | tf_op jit(solution)/shard_map/ppermute | solution.py:323
  45.1 23.3 %slice-start = ((s8[18874368]{0:T(1024)(128)(4,1)}), s8[4194304]{0:T(1024)(128)(4,1)S(1)}, s32[]{:S(2)}) async-start(s8[18874368]{0:T(1024)(128)(4,1)} %bitcast.12), calls=%async_computation | async-start | bytes 8388608
  45.1 23.3 %slice-start.1 = ((s8[18874368]{0:T(1024)(128)(4,1)}), s8[4194304]{0:T(1024)(128)(4,1)S(1)}, s32[]{:S(2)}) async-start(s8[18874368]{0:T(1024)(128)(4,1)} %bitcast.12), calls=%async_computation.1 | async-start | bytes 8388608
  45.1 23.3 %slice-start.2 = ((s8[18874368]{0:T(1024)(128)(4,1)}), s8[4194304]{0:T(1024)(128)(4,1)S(1)}, s32[]{:S(2)}) async-start(s8[18874368]{0:T(1024)(128)(4,1)} %bitcast.12), calls=%async_computation.2 | async-start | bytes 8388608
  52.3 3.3 %collective-permute-start.17 = (bf16[4,160,384]{2,1,0:T(8,128)(2,1)S(1)}, bf16[4,160,384]{2,1,0:T(8,128)(2,1)S(1)}, u32[]{:S(2)}, u32[]{:S(2)}) collective-permute-start(bf16[4,160,384]{2,1,0:T(8,128)(2,1)S(1)} %get-tuple-element.84), channel_id=1, source_target_pairs={{0,4},{4,0},{1,5},{5,1},{2,6},{6,2},{3,7},{7,3},{8,12},{12,8},{9,1... | collective-permute-start | bytes 1474568 | tf_op jit(solution)/shard_map/ppermute | solution.py:323
  52.4 3.2 %collective-permute-start.18 = (f32[4,160,128]{2,1,0:T(8,128)S(1)}, f32[4,160,128]{2,1,0:T(8,128)S(1)}, u32[]{:S(2)}, u32[]{:S(2)}) collective-permute-start(f32[4,160,128]{2,1,0:T(8,128)S(1)} %get-tuple-element.85), channel_id=1, source_target_pairs={{0,4},{4,0},{1,5},{5,1},{2,6},{6,2},{3,7},{7,3},{8,12},{12,8},{9,1... | collective-permute-start | bytes 983048 | tf_op jit(solution)/shard_map/ppermute | solution.py:323
  52.9 3.2 %collective-permute-start.15 = (bf16[240,768]{1,0:T(8,128)(2,1)S(1)}, bf16[240,768]{1,0:T(8,128)(2,1)S(1)}, u32[]{:S(2)}, u32[]{:S(2)}) collective-permute-start(bf16[240,768]{1,0:T(8,128)(2,1)S(1)} %collective-permute-done.12.refs_1_), channel_id=1, source_target_pairs={{0,4},{4,0},{1,5},{5,1},{2,6},{6,2},{3,7},{7,3},{8,12},{12,8},{9,1... | collective-permute-start | bytes 1105928 | tf_op jit(solution)/shard_map/ppermute | solution.py:323
  53.0 3.1 %collective-permute-start.16 = (bf16[240,768]{1,0:T(8,128)(2,1)S(1)}, bf16[240,768]{1,0:T(8,128)(2,1)S(1)}, u32[]{:S(2)}, u32[]{:S(2)}) collective-permute-start(bf16[240,768]{1,0:T(8,128)(2,1)S(1)} %collective-permute-done.13.refs_2_), channel_id=1, source_target_pairs={{0,4},{4,0},{1,5},{5,1},{2,6},{6,2},{3,7},{7,3},{8,12},{12,8},{9,1... | collective-permute-start | bytes 1105928 | tf_op jit(solution)/shard_map/ppermute | solution.py:323
  53.5 2.7 %collective-permute-start.14 = (bf16[160,768]{1,0:T(8,128)(2,1)S(1)}, bf16[160,768]{1,0:T(8,128)(2,1)S(1)}, u32[]{:S(2)}, u32[]{:S(2)}) collective-permute-start(bf16[160,768]{1,0:T(8,128)(2,1)S(1)} %collective-permute-done.5.refs_0_), channel_id=1, source_target_pairs={{0,4},{4,0},{1,5},{5,1},{2,6},{6,2},{3,7},{7,3},{8,12},{12,8},{9,1... | collective-permute-start | bytes 737288 | tf_op jit(solution)/shard_map/ppermute | solution.py:323
  53.6 14.9 %slice-start.3 = ((s8[18874368]{0:T(1024)(128)(4,1)}), s8[4194304]{0:T(1024)(128)(4,1)S(1)}, s32[]{:S(2)}) async-start(s8[18874368]{0:T(1024)(128)(4,1)} %bitcast.12), calls=%async_computation.3 | async-start | bytes 8388608
  56.2 12.3 %slice-start.4 = ((s8[18874368]{0:T(1024)(128)(4,1)}), s8[2097152]{0:T(1024)(128)(4,1)S(1)}, s32[]{:S(2)}) async-start(s8[18874368]{0:T(1024)(128)(4,1)} %bitcast.12), calls=%async_computation.4 | async-start | bytes 4194304
  58.7 6.6 %collective-permute-start.19 = (bf16[160,384]{1,0:T(8,128)(2,1)S(1)}, bf16[160,384]{1,0:T(8,128)(2,1)S(1)}, u32[]{:S(2)}, u32[]{:S(2)}) collective-permute-start(bf16[160,384]{1,0:T(8,128)(2,1)S(1)} %get-tuple-element.87), channel_id=1, source_target_pairs={{0,32},{32,64},{64,96},{96,0},{1,33},{33,65},{65,97},{97,1},{2,34}... | collective-permute-start | bytes 368648 | tf_op jit(solution)/shard_map/ppermute | solution.py:323
  59.6 7.7 %collective-permute-start.20 = (bf16[160,384]{1,0:T(8,128)(2,1)S(1)}, bf16[160,384]{1,0:T(8,128)(2,1)S(1)}, u32[]{:S(2)}, u32[]{:S(2)}) collective-permute-start(bf16[160,384]{1,0:T(8,128)(2,1)S(1)} %get-tuple-element.88), channel_id=1, source_target_pairs={{0,96},{32,0},{64,32},{96,64},{1,97},{33,1},{65,33},{97,65},{2,98}... | collective-permute-start | bytes 368648 | tf_op jit(solution)/shard_map/ppermute | solution.py:323
  62.0 6.4 %collective-permute-start.21 = (bf16[160,384]{1,0:T(8,128)(2,1)S(1)}, bf16[160,384]{1,0:T(8,128)(2,1)S(1)}, u32[]{:S(2)}, u32[]{:S(2)}) collective-permute-start(bf16[160,384]{1,0:T(8,128)(2,1)S(1)} %get-tuple-element.89), channel_id=1, source_target_pairs={{0,64},{32,96},{64,0},{96,32},{1,65},{33,97},{65,1},{97,33},{2,66}... | collective-permute-start | bytes 368648 | tf_op jit(solution)/shard_map/ppermute | solution.py:323
  69.5 8.6 %collective-permute-start.24 = (bf16[160,768]{1,0:T(8,128)(2,1)S(1)}, bf16[160,768]{1,0:T(8,128)(2,1)S(1)}, u32[]{:S(2)}, u32[]{:S(2)}) collective-permute-start(bf16[160,768]{1,0:T(8,128)(2,1)S(1)} %get-tuple-element.94), channel_id=1, source_target_pairs={{0,1},{1,2},{2,3},{3,0},{4,5},{5,6},{6,7},{7,4},{8,9},{9,10},{10,1... | collective-permute-start | bytes 737288 | tf_op jit(solution)/shard_map/ppermute | solution.py:323
  70.0 10.0 %collective-permute-start.25 = (bf16[160,768]{1,0:T(8,128)(2,1)S(1)}, bf16[160,768]{1,0:T(8,128)(2,1)S(1)}, u32[]{:S(2)}, u32[]{:S(2)}) collective-permute-start(bf16[160,768]{1,0:T(8,128)(2,1)S(1)} %get-tuple-element.95), channel_id=1, source_target_pairs={{0,3},{1,0},{2,1},{3,2},{4,7},{5,4},{6,5},{7,6},{8,11},{9,8},{10,9... | collective-permute-start | bytes 737288 | tf_op jit(solution)/shard_map/ppermute | solution.py:323
  72.6 12.5 %collective-permute-start.22 = (bf16[160,768]{1,0:T(8,128)(2,1)S(1)}, bf16[160,768]{1,0:T(8,128)(2,1)S(1)}, u32[]{:S(2)}, u32[]{:S(2)}) collective-permute-start(bf16[160,768]{1,0:T(8,128)(2,1)S(1)} %get-tuple-element.92), channel_id=1, source_target_pairs={{0,3},{1,0},{2,1},{3,2},{4,7},{5,4},{6,5},{7,6},{8,11},{9,8},{10,9... | collective-permute-start | bytes 737288 | tf_op jit(solution)/shard_map/ppermute | solution.py:323
  73.5 11.7 %collective-permute-start.23 = (bf16[160,768]{1,0:T(8,128)(2,1)S(1)}, bf16[160,768]{1,0:T(8,128)(2,1)S(1)}, u32[]{:S(2)}, u32[]{:S(2)}) collective-permute-start(bf16[160,768]{1,0:T(8,128)(2,1)S(1)} %get-tuple-element.93), channel_id=1, source_target_pairs={{0,1},{1,2},{2,3},{3,0},{4,5},{5,6},{6,7},{7,4},{8,9},{9,10},{10,1... | collective-permute-start | bytes 737288 | tf_op jit(solution)/shard_map/ppermute | solution.py:323
  81.1 6.3 %collective-permute-start.26 = (bf16[160,768]{1,0:T(8,128)(2,1)S(1)}, bf16[160,768]{1,0:T(8,128)(2,1)S(1)}, u32[]{:S(2)}, u32[]{:S(2)}) collective-permute-start(bf16[160,768]{1,0:T(8,128)(2,1)S(1)} %get-tuple-element.96), channel_id=1, source_target_pairs={{0,1},{1,2},{2,3},{3,0},{4,5},{5,6},{6,7},{7,4},{8,9},{9,10},{10,1... | collective-permute-start | bytes 737288 | tf_op jit(solution)/shard_map/ppermute | solution.py:323
  81.4 7.4 %collective-permute-start.27 = (bf16[160,768]{1,0:T(8,128)(2,1)S(1)}, bf16[160,768]{1,0:T(8,128)(2,1)S(1)}, u32[]{:S(2)}, u32[]{:S(2)}) collective-permute-start(bf16[160,768]{1,0:T(8,128)(2,1)S(1)} %get-tuple-element.97), channel_id=1, source_target_pairs={{0,3},{1,0},{2,1},{3,2},{4,7},{5,4},{6,5},{7,6},{8,11},{9,8},{10,9... | collective-permute-start | bytes 737288 | tf_op jit(solution)/shard_map/ppermute | solution.py:323

commit v4 on v3

--- a/solution.py
+++ b/solution.py
@@ -60,46 +60,39 @@
         copy.wait()
 
 
-def pack_kernel(queries, keys, values, *refs):
-    outs, (both_s, query_s, sems, out_sems) = refs[:-4], refs[-4:]
+def pack_kernel(count, *refs):
+    sources, outs, (stage_s, sems, out_sems) = refs[:count], refs[count:-3], refs[-3:]
     arrive, leave = [], []
     for j, distance in enumerate((0, 1, 3, 2)):
         first = lax.rem(lax.axis_index("y") + distance, 4) * WIDTH
         source = pl.ds(pl.multiple_of(first, WIDTH), WIDTH)
-        pairs = (
-            (keys.at[:, source], both_s.at[j, :, pl.ds(0, WIDTH)]),
-            (values.at[:, source], both_s.at[j, :, pl.ds(WIDTH, WIDTH)]),
-            (queries.at[:, source], query_s.at[j]),
-        )
-        for i, (src, dst) in enumerate(pairs):
-            arrive.append(pltpu.make_async_copy(src, dst, sems.at[3 * j + i]))
-        leave.append(pltpu.make_async_copy(both_s.at[j], outs[j], out_sems.at[j]))
-        leave.append(pltpu.make_async_copy(query_s.at[j], outs[4 + j], out_sems.at[4 + j]))
+        for i, array in enumerate(sources):
+            stage = stage_s.at[j, :, pl.ds(i * WIDTH, WIDTH)]
+            arrive.append(pltpu.make_async_copy(array.at[:, source], stage, sems.at[j, i]))
+        leave.append(pltpu.make_async_copy(stage_s.at[j], outs[j], out_sems.at[j]))
     start_all(arrive)
     for j in range(4):
-        wait_all(arrive[3 * j : 3 * j + 3])
-        start_all(leave[2 * j : 2 * j + 2])
+        wait_all(arrive[count * j : count * (j + 1)])
+        leave[j].start()
     wait_all(leave)
 
 
-def pack_by_owner(queries, keys, values):
-    shape = lambda width: jax.ShapeDtypeStruct((TOK, width), jnp.bfloat16)
+def pack_by_owner(*arrays):
+    count = len(arrays)
     hbm = pl.BlockSpec(memory_space=pltpu.HBM)
-    outs = pl.pallas_call(
-        pack_kernel,
-        in_specs=[hbm, hbm, hbm],
-        out_specs=[hbm] * 8,
-        out_shape=[shape(2 * WIDTH)] * 4 + [shape(WIDTH)] * 4,
+    return pl.pallas_call(
+        functools.partial(pack_kernel, count),
+        in_specs=[hbm] * count,
+        out_specs=[hbm] * 4,
+        out_shape=[jax.ShapeDtypeStruct((TOK, count * WIDTH), jnp.bfloat16)] * 4,
         scratch_shapes=[
-            pltpu.VMEM((4, TOK, 2 * WIDTH), jnp.bfloat16),
-            pltpu.VMEM((4, TOK, WIDTH), jnp.bfloat16),
-            pltpu.SemaphoreType.DMA((12,)),
-            pltpu.SemaphoreType.DMA((8,)),
+            pltpu.VMEM((4, TOK, count * WIDTH), jnp.bfloat16),
+            pltpu.SemaphoreType.DMA((4, count)),
+            pltpu.SemaphoreType.DMA((4,)),
         ],
         compiler_params=pltpu.CompilerParams(vmem_limit_bytes=VMEM_GRANT),
         name="pack_by_owner",
-    )(queries, keys, values)
-    return outs[:4], outs[4:]
+    )(*arrays)
 
 
 def stack_kernel(*refs):
@@ -259,9 +252,8 @@
     )(*operands)
 
 
-def project_kernel(places, added, *refs):
-    parts, w_ref, refs = refs[:4], refs[4], refs[5:]
-    extra, outs, rows_s = refs[:added], refs[added:-1], refs[-1]
+def project_kernel(places, *refs):
+    parts, w_ref, outs, rows_s = refs[:4], refs[4], refs[5:-1], refs[-1]
     for part, offset in zip(parts, Y_OFFSETS):
         first = lax.rem(lax.axis_index("y") + offset, 4) * WIDTH
         rows_s[:, pl.ds(pl.multiple_of(first, WIDTH), WIDTH)] = part[...]
@@ -270,18 +262,16 @@
         first = (lax.rem(lax.axis_index("tp") + distance, 4) * 2 + half) * columns
         weights = w_ref[:, pl.ds(pl.multiple_of(first, columns), columns)]
         term = jnp.dot(rows_s[...], weights, preferred_element_type=jnp.float32)
-        if added:
-            term = term + extra[i][...].astype(jnp.float32)
         outs[i][...] = term.astype(outs[i].dtype)
 
 
-def project(attended, out_weight, places, extra=(), dtype=jnp.bfloat16):
+def project(attended, out_weight, places, dtype=jnp.bfloat16):
     depth, columns = out_weight.shape[0], out_weight.shape[1] // 8
     count = len(places)
     vmem = pl.BlockSpec(memory_space=pltpu.VMEM)
     return pl.pallas_call(
-        functools.partial(project_kernel, places, len(extra)),
-        in_specs=[vmem] * (5 + len(extra)),
+        functools.partial(project_kernel, places),
+        in_specs=[vmem] * 5,
         out_specs=[vmem] * count,
         out_shape=[jax.ShapeDtypeStruct((TOK, columns), dtype)] * count,
         scratch_shapes=[pltpu.VMEM((TOK, depth), jnp.bfloat16)],
@@ -292,16 +282,33 @@
             transcendentals=0,
         ),
         name="project",
-    )(*attended, out_weight, *extra)
-
-
-def final_kernel(own_a, own_b, direct_a, direct_b, summed_a, summed_b, gate_ref, o_ref):
+    )(*attended, out_weight)
+
+
+def add_kernel(*refs):
+    count = len(refs) // 3
+    for i in range(count):
+        total = refs[i][...] + refs[count + i][...].astype(jnp.float32)
+        refs[2 * count + i][...] = total.astype(refs[2 * count + i].dtype)
+
+
+def add(terms, arrived, dtype):
+    vmem = pl.BlockSpec(memory_space=pltpu.VMEM)
+    return pl.pallas_call(
+        add_kernel,
+        in_specs=[vmem] * 4,
+        out_specs=[vmem] * 2,
+        out_shape=[jax.ShapeDtypeStruct(terms[0].shape, dtype)] * 2,
+        compiler_params=pltpu.CompilerParams(vmem_limit_bytes=VMEM_SMALL),
+        name="add",
+    )(*terms, *arrived)
+
+
+def final_kernel(own_a, own_b, summed_a, summed_b, gate_ref, o_ref):
     columns = own_a.shape[1]
-    for i, (own, direct, summed) in enumerate(
-        ((own_a, direct_a, summed_a), (own_b, direct_b, summed_b))
-    ):
+    for i, (own, summed) in enumerate(((own_a, summed_a), (own_b, summed_b))):
         place = slice(i * columns, (i + 1) * columns)
-        total = own[...] + direct[...].astype(jnp.float32) + summed[...].astype(jnp.float32)
+        total = own[...] + summed[...].astype(jnp.float32)
         o_ref[:, place] = (total * gate_ref[:, place]).astype(o_ref.dtype)
 
 
@@ -310,7 +317,7 @@
     vmem = pl.BlockSpec(memory_space=pltpu.VMEM)
     return pl.pallas_call(
         final_kernel,
-        in_specs=[vmem] * 7,
+        in_specs=[vmem] * 5,
         out_specs=vmem,
         out_shape=jax.ShapeDtypeStruct((rows, 2 * columns), jnp.bfloat16),
         compiler_params=pltpu.CompilerParams(vmem_limit_bytes=VMEM_SMALL),
@@ -352,7 +359,8 @@
         (1, columns),
     )
 
-    (own, up, down, across), (q_own, q_up, q_down, q_across) = pack_by_owner(queries, keys, values)
+    own, up, down, across = pack_by_owner(keys, values)
+    q_own, q_up, q_down, q_across = pack_by_owner(queries)
     from_across = shift(across, "y", 2)
     from_down, from_up = shift(up, "y", 1), shift(down, "y", -1)
     own_before, own_after = shift(own, "z", 1), shift(own, "z", -1)
@@ -401,12 +409,13 @@
     from_left, from_right = shift(across_a, "tp", 1), shift(across_b, "tp", -1)
     right_b, left_a = project(attended, out_weight, ((1, 1), (3, 0)))
     direct_b, direct_a = shift(right_b, "tp", 1), shift(left_a, "tp", -1)
-    own_a, own_b = project(attended, out_weight, ((0, 0), (0, 1)), dtype=jnp.float32)
-    right_a, left_b = project(
-        attended, out_weight, ((1, 0), (3, 1)), (from_left, from_right)
-    )
+    right_a, left_b, own_a, own_b = project(
+        attended, out_weight, ((1, 0), (3, 1), (0, 0), (0, 1)), dtype=f32
+    )
+    right_a, left_b = add((right_a, left_b), (from_left, from_right), bf16)
     summed_a, summed_b = shift(right_a, "tp", 1), shift(left_b, "tp", -1)
-    return finish((own_a, own_b, direct_a, direct_b, summed_a, summed_b), gate_part)
+    own_a, own_b = add((own_a, own_b), (direct_a, direct_b), f32)
+    return finish((own_a, own_b, summed_a, summed_b), gate_part)
 
 
 def solution(mesh):

time: 90.1 us -> 89 us (0.988)
  waiting for transfers between devices: 25.5 us -> 22.6 us
  Pallas kernels: 21.5 us -> 23 us
    ppermute x28, waiting for transfers between devices: 25.5 us -> 22.6 us  [shift(): return lax.ppermute(x, axis, [(i, (i + step) % size) for i in range(size)])]
    pallas_call x6 -> x8, Pallas kernels: 7.43 us -> 8.86 us  [the longest x2 3.91 us: pack_by_owner(): pl.pallas_call(functools.partial(pack_kernel, count), in_specs=[hbm] * co...]
  transfers between devices with their start and end apart: 28 -> 28, of which waited for: 14 -> 14; matrix products, arithmetic and copies ran while one was open for 6% -> 6% of each run, Pallas kernels for 15% -> 17%
where the time goes in v4:
time: 89 us; the launch traced here: 88.7 us
  starting transfers between devices  33.5 us (38%)
  Pallas kernels  23 us (26%)
  waiting for transfers between devices  22.6 us (25%)
  local copies, waits for them, and re-layouts  6.04 us (7%)
  between operations  2.33 us (3%)
  other arithmetic  1.15 us (1%)
    ppermute x28, starting transfers between devices, shift(): return lax.ppermute(x, axis, [(i, (i + step) % size) for i in range(size)])  33.5 us
    ppermute x28, waiting for transfers between devices, shift(): return lax.ppermute(x, axis, [(i, (i + step) % size) for i in range(size)])  22.6 us
    pallas_call x3, Pallas kernels, attend(): pl.pallas_call(kernel, in_specs=[vmem] * len(operands), out_specs=[vmem]...  11.9 us
    pallas_call x2, Pallas kernels, pack_by_owner(): pl.pallas_call(functools.partial(pack_kernel, count), in_specs=[hbm] * co...  3.91 us
    pallas_call x3, Pallas kernels, project(): pl.pallas_call(functools.partial(project_kernel, places), in_specs=[vmem]...  3.86 us
    pallas_call x3, Pallas kernels, stack(): pl.pallas_call(stack_kernel, in_specs=[pl.BlockSpec(memory_space=pltpu.VM...  1.88 us
    unnamed x14, local copies, waits for them, and re-layouts  1.86 us
  transfers between devices with their start and end apart: 28, of which 14 were waited for; matrix products, arithmetic and copies ran while one was open for 6% of the time, Pallas kernels for 17%

profile of v4, /device:TPU:6, one launch (start us, length us, event | category | flops | bytes accessed | tf_op | source)
XLA Modules:
  0.0 88.7 jit_solution(11028169468444038601)
XLA Ops:
  0.0 2.1 %pack_by_owner.2 = (bf16[160,768]{1,0:T(8,128)(2,1)}, bf16[160,768]{1,0:T(8,128)(2,1)}, bf16[160,768]{1,0:T(8,128)(2,1)}, bf16[160,768]{1,0:T(8,128)(2,1)}) custom-call(bf16[160,1536]{1,0:T(8,128)(2,1)} %refs_0_.2, bf16[160,1536]{1,0:T(8,128)(2,1)} %refs_1_.1), custom_call_target="tpu_custom_call" | custom-call | tf_op jit(solution)/shard_map/pack_by_owner/pallas_call | solution.py:83
  2.1 2.0 %collective-permute-start.3 = (bf16[160,768]{1,0:T(8,128)(2,1)}, bf16[160,768]{1,0:T(8,128)(2,1)S(1)}, u32[]{:S(2)}, u32[]{:S(2)}) collective-permute-start(bf16[160,768]{1,0:T(8,128)(2,1)} %get-tuple-element.62.refs_0_), channel_id=1, source_target_pairs={{0,8},{8,16},{16,24},{24,0},{1,9},{9,17},{17,25},{25,1},{2,10},{10... | collective-permute-start | bytes 737288 | tf_op jit(solution)/shard_map/ppermute | solution.py:330
  4.1 2.2 %collective-permute-start.4 = (bf16[160,768]{1,0:T(8,128)(2,1)}, bf16[160,768]{1,0:T(8,128)(2,1)S(1)}, u32[]{:S(2)}, u32[]{:S(2)}) collective-permute-start(bf16[160,768]{1,0:T(8,128)(2,1)} %get-tuple-element.62.refs_0_), channel_id=1, source_target_pairs={{0,24},{8,0},{16,8},{24,16},{1,25},{9,1},{17,9},{25,17},{2,26},{10... | collective-permute-start | bytes 737288 | tf_op jit(solution)/shard_map/ppermute | solution.py:330
  6.3 1.6 %collective-permute-start = (bf16[160,768]{1,0:T(8,128)(2,1)}, bf16[160,768]{1,0:T(8,128)(2,1)S(1)}, u32[]{:S(2)}, u32[]{:S(2)}) collective-permute-start(bf16[160,768]{1,0:T(8,128)(2,1)} %get-tuple-element.56), channel_id=1, source_target_pairs={{0,32},{32,64},{64,96},{96,0},{1,33},{33,65},{65,97},{97,1},{2,34}... | collective-permute-start | bytes 737288 | tf_op jit(solution)/shard_map/ppermute | solution.py:330
  7.9 1.7 %collective-permute-start.1 = (bf16[160,768]{1,0:T(8,128)(2,1)}, bf16[160,768]{1,0:T(8,128)(2,1)S(1)}, u32[]{:S(2)}, u32[]{:S(2)}) collective-permute-start(bf16[160,768]{1,0:T(8,128)(2,1)} %get-tuple-element.57), channel_id=1, source_target_pairs={{0,96},{32,0},{64,32},{96,64},{1,97},{33,1},{65,33},{97,65},{2,98}... | collective-permute-start | bytes 737288 | tf_op jit(solution)/shard_map/ppermute | solution.py:330
  9.5 2.0 %collective-permute-start.2 = (bf16[160,768]{1,0:T(8,128)(2,1)}, bf16[160,768]{1,0:T(8,128)(2,1)S(1)}, u32[]{:S(2)}, u32[]{:S(2)}) collective-permute-start(bf16[160,768]{1,0:T(8,128)(2,1)} %get-tuple-element.58), channel_id=1, source_target_pairs={{0,64},{32,96},{64,0},{96,32},{1,65},{33,97},{65,1},{97,33},{2,66}... | collective-permute-start | bytes 737288 | tf_op jit(solution)/shard_map/ppermute | solution.py:330
  11.5 0.8 fusion
  12.3 0.2 reshape.89
  12.6 0.1 copy.15
  12.8 0.1 copy.16
  12.9 0.1 copy.17
  13.1 0.1 copy.18
  13.3 0.1 copy.19
  13.4 0.2 select_reduce_fusion.1
  13.9 0.2 select_reduce_fusion
  14.8 1.3 %dynamic_slice.57 = s32[1]{0:T(128)} dynamic-slice(s32[4]{0:T(128)} %param.13, s32[]{:T(128)S(6)} %select_n.135), dynamic_slice_sizes={1} | dynamic-slice | bytes 12 | tf_op jit(solution)/shard_map/jit(dynamic_index_in_dim)/dynamic_slice | solution.py:358
  17.4 1.8 %pack_by_owner.3 = (bf16[160,384]{1,0:T(8,128)(2,1)}, bf16[160,384]{1,0:T(8,128)(2,1)}, bf16[160,384]{1,0:T(8,128)(2,1)}, bf16[160,384]{1,0:T(8,128)(2,1)}) custom-call(bf16[160,1536]{1,0:T(8,128)(2,1)} %refs_0_.3), custom_call_target="tpu_custom_call" | custom-call | tf_op jit(solution)/shard_map/pack_by_owner/pallas_call | solution.py:83
  19.9 0.9 dynamic_slice.58.gate_ref
  20.9 0.7 collective-permute-done.2.refs_2_
  21.7 0.9 %stack.17.refs_3_ = bf16[480,768]{1,0:T(8,128)(2,1)S(1)} custom-call(bf16[160,768]{1,0:T(8,128)(2,1)S(1)} %collective-permute-done.refs_0_, bf16[160,768]{1,0:T(8,128)(2,1)S(1)} %collective-permute-done.1.refs_1_, bf16[160,768]{1,0:T(8,128)(2,1)S(1)} %collective-permute-done.2.refs_2_), custom_call_target="tpu_custom_call" | custom-call | tf_op jit(solution)/shard_map/stack/pallas_call | solution.py:111
  22.6 1.1 %collective-permute-start.10 = (bf16[480,768]{1,0:T(8,128)(2,1)S(1)}, bf16[480,768]{1,0:T(8,128)(2,1)S(1)}, u32[]{:S(2)}, u32[]{:S(2)}) collective-permute-start(bf16[480,768]{1,0:T(8,128)(2,1)S(1)} %stack.17.refs_3_), channel_id=1, source_target_pairs={{0,8},{8,16},{16,24},{24,0},{1,9},{9,17},{17,25},{25,1},{2,10},{10... | collective-permute-start | bytes 2211848 | tf_op jit(solution)/shard_map/ppermute | solution.py:330
  23.7 2.2 %collective-permute-start.11 = (bf16[480,768]{1,0:T(8,128)(2,1)S(1)}, bf16[480,768]{1,0:T(8,128)(2,1)S(1)}, u32[]{:S(2)}, u32[]{:S(2)}) collective-permute-start(bf16[480,768]{1,0:T(8,128)(2,1)S(1)} %stack.17.refs_3_), channel_id=1, source_target_pairs={{0,24},{8,0},{16,8},{24,16},{1,25},{9,1},{17,9},{25,17},{2,26},{10... | collective-permute-start | bytes 2211848 | tf_op jit(solution)/shard_map/ppermute | solution.py:330
  25.9 1.1 %collective-permute-start.6 = (bf16[160,384]{1,0:T(8,128)(2,1)}, bf16[160,384]{1,0:T(8,128)(2,1)S(1)}, u32[]{:S(2)}, u32[]{:S(2)}) collective-permute-start(bf16[160,384]{1,0:T(8,128)(2,1)} %get-tuple-element.65), channel_id=1, source_target_pairs={{0,32},{32,64},{64,96},{96,0},{1,33},{33,65},{65,97},{97,1},{2,34}... | collective-permute-start | bytes 368648 | tf_op jit(solution)/shard_map/ppermute | solution.py:330
  27.1 2.1 %collective-permute-start.7 = (bf16[160,384]{1,0:T(8,128)(2,1)}, bf16[160,384]{1,0:T(8,128)(2,1)S(1)}, u32[]{:S(2)}, u32[]{:S(2)}) collective-permute-start(bf16[160,384]{1,0:T(8,128)(2,1)} %get-tuple-element.66), channel_id=1, source_target_pairs={{0,96},{32,0},{64,32},{96,64},{1,97},{33,1},{65,33},{97,65},{2,98}... | collective-permute-start | bytes 368648 | tf_op jit(solution)/shard_map/ppermute | solution.py:330
  29.2 1.0 %collective-permute-start.8 = (bf16[160,384]{1,0:T(8,128)(2,1)}, bf16[160,384]{1,0:T(8,128)(2,1)S(1)}, u32[]{:S(2)}, u32[]{:S(2)}) collective-permute-start(bf16[160,384]{1,0:T(8,128)(2,1)} %get-tuple-element.67), channel_id=1, source_target_pairs={{0,64},{32,96},{64,0},{96,32},{1,65},{33,97},{65,1},{97,33},{2,66}... | collective-permute-start | bytes 368648 | tf_op jit(solution)/shard_map/ppermute | solution.py:330
  30.2 3.3 %collective-permute-done.6.refs_1_ = bf16[160,384]{1,0:T(8,128)(2,1)S(1)} collective-permute-done((bf16[160,384]{1,0:T(8,128)(2,1)}, bf16[160,384]{1,0:T(8,128)(2,1)S(1)}, u32[]{:S(2)}, u32[]{:S(2)}) %collective-permute-start.6) | collective-permute-done | bytes 122912 | tf_op jit(solution)/shard_map/ppermute | solution.py:330
  33.5 2.2 %collective-permute-done.8.refs_3_ = bf16[160,384]{1,0:T(8,128)(2,1)S(1)} collective-permute-done((bf16[160,384]{1,0:T(8,128)(2,1)}, bf16[160,384]{1,0:T(8,128)(2,1)S(1)}, u32[]{:S(2)}, u32[]{:S(2)}) %collective-permute-start.8) | collective-permute-done | bytes 122912 | tf_op jit(solution)/shard_map/ppermute | solution.py:330
  35.8 0.9 %copy-done.1 = bf16[160,384]{1,0:T(8,128)(2,1)S(1)} copy-done((bf16[160,384]{1,0:T(8,128)(2,1)S(1)}, bf16[160,384]{1,0:T(8,128)(2,1)}, u32[]{:S(2)}) %copy-start.1) | copy-done | bytes 122904
  36.7 0.6 stack.15.refs_0_.q
  37.4 0.9 %copy-done = bf16[160,768]{1,0:T(8,128)(2,1)S(1)} copy-done((bf16[160,768]{1,0:T(8,128)(2,1)S(1)}, bf16[160,768]{1,0:T(8,128)(2,1)}, u32[]{:S(2)}) %copy-start) | copy-done | bytes 245784
  38.4 0.3 stack.16.refs_2_
  38.7 0.6 collective-permute-done.9.refs_1_
  39.3 1.7 %collective-permute-done.10.refs_5_.x_ref = bf16[480,768]{1,0:T(8,128)(2,1)S(1)} collective-permute-done((bf16[480,768]{1,0:T(8,128)(2,1)S(1)}, bf16[480,768]{1,0:T(8,128)(2,1)S(1)}, u32[]{:S(2)}, u32[]{:S(2)}) %collective-permute-start.10) | collective-permute-done | bytes 737312 | tf_op jit(solution)/shard_map/ppermute | solution.py:330
  40.9 0.2 take_rows.2
  41.1 0.7 collective-permute-start.12
  41.8 0.2 take_rows.3
  42.0 2.8 %collective-permute-start.13 = (bf16[240,768]{1,0:T(8,128)(2,1)S(1)}, bf16[240,768]{1,0:T(8,128)(2,1)S(1)}, u32[]{:S(2)}, u32[]{:S(2)}) collective-permute-start(bf16[240,768]{1,0:T(8,128)(2,1)S(1)} %take_rows.3), channel_id=1, source_target_pairs={{0,24},{8,0},{16,8},{24,16},{1,25},{9,1},{17,9},{25,17},{2,26},{10... | collective-permute-start | bytes 1105928 | tf_op jit(solution)/shard_map/ppermute | solution.py:330
  44.8 7.3 %near_kernel.1 = (f32[4,160,384]{2,1,0:T(8,128)S(1)}, f32[4,160,384]{2,1,0:T(8,128)S(1)}, bf16[4,160,384]{2,1,0:T(8,128)(2,1)S(1)}, f32[4,160,128]{2,1,0:T(8,128)S(1)}) custom-call(f32[2,4,1920]{2,1,0:T(4,128)S(1)} %pad_maximum_fusion.bias_ref, bf16[640,384]{1,0:T(8,128)(2,1)S(1)} %stack.15.refs_0_.q, bf16[640,384]{1,0:T(8,128)(2,1)S(1)} %collective-permute-done.9.refs_1_, ...), custom_call_target="tpu_custom_call" | custom-call | flops 12000000000 | bytes 1048576 | tf_op jit(solution)/shard_map/near_kernel/pallas_call | solution.py:236
  52.2 0.5 collective-permute-start.18
  52.8 0.4 collective-permute-start.16
  53.3 2.1 %far_kernel.1 = (f32[4,160,384]{2,1,0:T(8,128)S(1)}, f32[4,160,384]{2,1,0:T(8,128)S(1)}) custom-call(f32[1,4,640]{2,1,0:T(4,128)S(1)} %broadcast_in_dim_reshape_reshape.6.bias_ref, bf16[640,384]{1,0:T(8,128)(2,1)S(1)} %stack.15.refs_0_.q, bf16[160,768]{1,0:T(8,128)(2,1)S(1)} %collective-permute-done.5.refs_0_, ...), custom_call_target="tpu_custom_call" | custom-call | flops 4000000000 | bytes 1048576 | tf_op jit(solution)/shard_map/far_kernel/pallas_call | solution.py:236
  55.4 0.5 collective-permute-done.14.refs_0_
  55.9 2.5 %last_kernel.1 = (bf16[160,384]{1,0:T(8,128)(2,1)S(1)}, bf16[160,384]{1,0:T(8,128)(2,1)S(1)}, bf16[160,384]{1,0:T(8,128)(2,1)S(1)}, bf16[160,384]{1,0:T(8,128)(2,1)S(1)}) custom-call(f32[1,4,640]{2,1,0:T(4,128)S(1)} %broadcast_in_dim_reshape_reshape.7.bias_ref, bf16[640,384]{1,0:T(8,128)(2,1)S(1)} %stack.15.refs_0_.q, ...), custom_call_target="tpu_custom_call" | custom-call | flops 4000000000 | bytes 1048576 | tf_op jit(solution)/shard_map/last_kernel/pallas_call | solution.py:236
  58.5 0.9 %collective-permute-start.19 = (bf16[160,384]{1,0:T(8,128)(2,1)S(1)}, bf16[160,384]{1,0:T(8,128)(2,1)S(1)}, u32[]{:S(2)}, u32[]{:S(2)}) collective-permute-start(bf16[160,384]{1,0:T(8,128)(2,1)S(1)} %get-tuple-element.91), channel_id=1, source_target_pairs={{0,32},{32,64},{64,96},{96,0},{1,33},{33,65},{65,97},{97,1},{2,34}... | collective-permute-start | bytes 368648 | tf_op jit(solution)/shard_map/ppermute | solution.py:330
  59.4 2.4 %collective-permute-start.20 = (bf16[160,384]{1,0:T(8,128)(2,1)S(1)}, bf16[160,384]{1,0:T(8,128)(2,1)S(1)}, u32[]{:S(2)}, u32[]{:S(2)}) collective-permute-start(bf16[160,384]{1,0:T(8,128)(2,1)S(1)} %get-tuple-element.92), channel_id=1, source_target_pairs={{0,96},{32,0},{64,32},{96,64},{1,97},{33,1},{65,33},{97,65},{2,98}... | collective-permute-start | bytes 368648 | tf_op jit(solution)/shard_map/ppermute | solution.py:330
  61.8 0.8 collective-permute-start.21
  62.6 2.5 %collective-permute-done.19.refs_1_ = bf16[160,384]{1,0:T(8,128)(2,1)S(1)} collective-permute-done((bf16[160,384]{1,0:T(8,128)(2,1)S(1)}, bf16[160,384]{1,0:T(8,128)(2,1)S(1)}, u32[]{:S(2)}, u32[]{:S(2)}) %collective-permute-start.19) | collective-permute-done | bytes 122912 | tf_op jit(solution)/shard_map/ppermute | solution.py:330
  65.1 1.9 %collective-permute-done.20.refs_2_ = bf16[160,384]{1,0:T(8,128)(2,1)S(1)} collective-permute-done((bf16[160,384]{1,0:T(8,128)(2,1)S(1)}, bf16[160,384]{1,0:T(8,128)(2,1)S(1)}, u32[]{:S(2)}, u32[]{:S(2)}) %collective-permute-start.20) | collective-permute-done | bytes 122912 | tf_op jit(solution)/shard_map/ppermute | solution.py:330
  67.0 1.1 %collective-permute-done.21.refs_3_ = bf16[160,384]{1,0:T(8,128)(2,1)S(1)} collective-permute-done((bf16[160,384]{1,0:T(8,128)(2,1)S(1)}, bf16[160,384]{1,0:T(8,128)(2,1)S(1)}, u32[]{:S(2)}, u32[]{:S(2)}) %collective-permute-start.21) | collective-permute-done | bytes 122912 | tf_op jit(solution)/shard_map/ppermute | solution.py:330
  68.2 1.0 %project.5 = (bf16[160,768]{1,0:T(8,128)(2,1)S(1)}, bf16[160,768]{1,0:T(8,128)(2,1)S(1)}) custom-call(bf16[160,384]{1,0:T(8,128)(2,1)S(1)} %get-tuple-element.90.refs_0_, bf16[160,384]{1,0:T(8,128)(2,1)S(1)} %collective-permute-done.19.refs_1_, bf16[160,384]{1,0:T(8,128)(2,1)S(1)} %collective-permute-done.20.refs_2_, ...), custom_call_target="tpu_custom_call" | custom-call | flops 754974720 | bytes 4718592 | tf_op jit(solution)/shard_map/project/pallas_call | solution.py:272
  69.2 0.5 collective-permute-start.24
  69.8 1.6 %collective-permute-start.25 = (bf16[160,768]{1,0:T(8,128)(2,1)S(1)}, bf16[160,768]{1,0:T(8,128)(2,1)S(1)}, u32[]{:S(2)}, u32[]{:S(2)}) collective-permute-start(bf16[160,768]{1,0:T(8,128)(2,1)S(1)} %get-tuple-element.103), channel_id=1, source_target_pairs={{0,3},{1,0},{2,1},{3,2},{4,7},{5,4},{6,5},{7,6},{8,11},{9,8},{10,9... | collective-permute-start | bytes 737288 | tf_op jit(solution)/shard_map/ppermute | solution.py:330
  71.3 1.0 %project.4 = (bf16[160,768]{1,0:T(8,128)(2,1)S(1)}, bf16[160,768]{1,0:T(8,128)(2,1)S(1)}) custom-call(bf16[160,384]{1,0:T(8,128)(2,1)S(1)} %get-tuple-element.90.refs_0_, bf16[160,384]{1,0:T(8,128)(2,1)S(1)} %collective-permute-done.19.refs_1_, bf16[160,384]{1,0:T(8,128)(2,1)S(1)} %collective-permute-done.20.refs_2_, ...), custom_call_target="tpu_custom_call" | custom-call | flops 754974720 | bytes 4718592 | tf_op jit(solution)/shard_map/project/pallas_call | solution.py:272
  72.4 0.9 %collective-permute-start.22 = (bf16[160,768]{1,0:T(8,128)(2,1)S(1)}, bf16[160,768]{1,0:T(8,128)(2,1)S(1)}, u32[]{:S(2)}, u32[]{:S(2)}) collective-permute-start(bf16[160,768]{1,0:T(8,128)(2,1)S(1)} %get-tuple-element.96), channel_id=1, source_target_pairs={{0,3},{1,0},{2,1},{3,2},{4,7},{5,4},{6,5},{7,6},{8,11},{9,8},{10,9... | collective-permute-start | bytes 737288 | tf_op jit(solution)/shard_map/ppermute | solution.py:330
  73.3 2.4 %collective-permute-start.23 = (bf16[160,768]{1,0:T(8,128)(2,1)S(1)}, bf16[160,768]{1,0:T(8,128)(2,1)S(1)}, u32[]{:S(2)}, u32[]{:S(2)}) collective-permute-start(bf16[160,768]{1,0:T(8,128)(2,1)S(1)} %get-tuple-element.97), channel_id=1, source_target_pairs={{0,1},{1,2},{2,3},{3,0},{4,5},{5,6},{6,7},{7,4},{8,9},{9,10},{10,1... | collective-permute-start | bytes 737288 | tf_op jit(solution)/shard_map/ppermute | solution.py:330
  75.7 1.8 %project.3 = (f32[160,768]{1,0:T(8,128)S(1)}, f32[160,768]{1,0:T(8,128)S(1)}, f32[160,768]{1,0:T(8,128)S(1)}, f32[160,768]{1,0:T(8,128)S(1)}) custom-call(bf16[160,384]{1,0:T(8,128)(2,1)S(1)} %get-tuple-element.90.refs_0_, bf16[160,384]{1,0:T(8,128)(2,1)S(1)} %collective-permute-done.19.refs_1_, bf16[160,384]{1,0:T(8,128)(2,1)S(1)} %collective-permute-done.20.refs_2_, ...), custom_call_target="tpu_custom_call" | custom-call | flops 1509949440 | bytes 9437184 | tf_op jit(solution)/shard_map/project/pallas_call | solution.py:272
  77.5 0.3 collective-permute-done.24.refs_2_
  77.8 2.1 %collective-permute-done.25.refs_3_ = bf16[160,768]{1,0:T(8,128)(2,1)S(1)} collective-permute-done((bf16[160,768]{1,0:T(8,128)(2,1)S(1)}, bf16[160,768]{1,0:T(8,128)(2,1)S(1)}, u32[]{:S(2)}, u32[]{:S(2)}) %collective-permute-start.25) | collective-permute-done | bytes 245792 | tf_op jit(solution)/shard_map/ppermute | solution.py:330
  80.0 0.4 collective-permute-start.26
  80.4 1.7 %collective-permute-start.27 = (bf16[160,768]{1,0:T(8,128)(2,1)S(1)}, bf16[160,768]{1,0:T(8,128)(2,1)S(1)}, u32[]{:S(2)}, u32[]{:S(2)}) collective-permute-start(bf16[160,768]{1,0:T(8,128)(2,1)S(1)} %get-tuple-element.105), channel_id=1, source_target_pairs={{0,3},{1,0},{2,1},{3,2},{4,7},{5,4},{6,5},{7,6},{8,11},{9,8},{10,9... | collective-permute-start | bytes 737288 | tf_op jit(solution)/shard_map/ppermute | solution.py:330
  82.1 2.8 %collective-permute-done.22.refs_2_ = bf16[160,768]{1,0:T(8,128)(2,1)S(1)} collective-permute-done((bf16[160,768]{1,0:T(8,128)(2,1)S(1)}, bf16[160,768]{1,0:T(8,128)(2,1)S(1)}, u32[]{:S(2)}, u32[]{:S(2)}) %collective-permute-start.22) | collective-permute-done | bytes 245792 | tf_op jit(solution)/shard_map/ppermute | solution.py:330
  85.0 1.3 %collective-permute-done.26.summed_a = bf16[160,768]{1,0:T(8,128)(2,1)S(1)} collective-permute-done((bf16[160,768]{1,0:T(8,128)(2,1)S(1)}, bf16[160,768]{1,0:T(8,128)(2,1)S(1)}, u32[]{:S(2)}, u32[]{:S(2)}) %collective-permute-start.26) | collective-permute-done | bytes 245792 | tf_op jit(solution)/shard_map/ppermute | solution.py:330
  86.3 1.5 %collective-permute-done.27.summed_b = bf16[160,768]{1,0:T(8,128)(2,1)S(1)} collective-permute-done((bf16[160,768]{1,0:T(8,128)(2,1)S(1)}, bf16[160,768]{1,0:T(8,128)(2,1)S(1)}, u32[]{:S(2)}, u32[]{:S(2)}) %collective-permute-start.27) | collective-permute-done | bytes 245792 | tf_op jit(solution)/shard_map/ppermute | solution.py:330
  87.8 0.9 %finish.1 = bf16[160,1536]{1,0:T(8,128)(2,1)} custom-call(f32[160,768]{1,0:T(8,128)S(1)} %get-tuple-element.98.own_a, f32[160,768]{1,0:T(8,128)S(1)} %get-tuple-element.99.own_b, bf16[160,768]{1,0:T(8,128)(2,1)S(1)} %collective-permute-done.26.summed_a, bf16[160,768]{1,0:T(8,128)(2,1)S(1)} %collective-permute-done.27.summed_b, ...), custom_call_target="tpu_custom_call" | custom-call | tf_op jit(solution)/shard_map/finish/pallas_call | solution.py:318
  (51 shorter events, 1.9 us)
Async XLA Ops:
  2.1 11.7 %collective-permute-start.3 = (bf16[160,768]{1,0:T(8,128)(2,1)}, bf16[160,768]{1,0:T(8,128)(2,1)S(1)}, u32[]{:S(2)}, u32[]{:S(2)}) collective-permute-start(bf16[160,768]{1,0:T(8,128)(2,1)} %get-tuple-element.62.refs_0_), channel_id=1, source_target_pairs={{0,8},{8,16},{16,24},{24,0},{1,9},{9,17},{17,25},{25,1},{2,10},{10... | collective-permute-start | bytes 737288 | tf_op jit(solution)/shard_map/ppermute | solution.py:330
  4.1 16.8 %collective-permute-start.4 = (bf16[160,768]{1,0:T(8,128)(2,1)}, bf16[160,768]{1,0:T(8,128)(2,1)S(1)}, u32[]{:S(2)}, u32[]{:S(2)}) collective-permute-start(bf16[160,768]{1,0:T(8,128)(2,1)} %get-tuple-element.62.refs_0_), channel_id=1, source_target_pairs={{0,24},{8,0},{16,8},{24,16},{1,25},{9,1},{17,9},{25,17},{2,26},{10... | collective-permute-start | bytes 737288 | tf_op jit(solution)/shard_map/ppermute | solution.py:330
  6.3 14.6 %collective-permute-start = (bf16[160,768]{1,0:T(8,128)(2,1)}, bf16[160,768]{1,0:T(8,128)(2,1)S(1)}, u32[]{:S(2)}, u32[]{:S(2)}) collective-permute-start(bf16[160,768]{1,0:T(8,128)(2,1)} %get-tuple-element.56), channel_id=1, source_target_pairs={{0,32},{32,64},{64,96},{96,0},{1,33},{33,65},{65,97},{97,1},{2,34}... | collective-permute-start | bytes 737288 | tf_op jit(solution)/shard_map/ppermute | solution.py:330
  7.9 13.0 %collective-permute-start.1 = (bf16[160,768]{1,0:T(8,128)(2,1)}, bf16[160,768]{1,0:T(8,128)(2,1)S(1)}, u32[]{:S(2)}, u32[]{:S(2)}) collective-permute-start(bf16[160,768]{1,0:T(8,128)(2,1)} %get-tuple-element.57), channel_id=1, source_target_pairs={{0,96},{32,0},{64,32},{96,64},{1,97},{33,1},{65,33},{97,65},{2,98}... | collective-permute-start | bytes 737288 | tf_op jit(solution)/shard_map/ppermute | solution.py:330
  9.5 12.1 %collective-permute-start.2 = (bf16[160,768]{1,0:T(8,128)(2,1)}, bf16[160,768]{1,0:T(8,128)(2,1)S(1)}, u32[]{:S(2)}, u32[]{:S(2)}) collective-permute-start(bf16[160,768]{1,0:T(8,128)(2,1)} %get-tuple-element.58), channel_id=1, source_target_pairs={{0,64},{32,96},{64,0},{96,32},{1,65},{33,97},{65,1},{97,33},{2,66}... | collective-permute-start | bytes 737288 | tf_op jit(solution)/shard_map/ppermute | solution.py:330
  13.8 7.9 %collective-permute-start.5 = (bf16[160,768]{1,0:T(8,128)(2,1)S(1)}, bf16[160,768]{1,0:T(8,128)(2,1)S(1)}, u32[]{:S(2)}, u32[]{:S(2)}) collective-permute-start(bf16[160,768]{1,0:T(8,128)(2,1)S(1)} %collective-permute-done.3.refs_4_), channel_id=1, source_target_pairs={{0,8},{8,16},{16,24},{24,0},{1,9},{9,17},{17,25},{25,1},{2,10},{10... | collective-permute-start | bytes 737288 | tf_op jit(solution)/shard_map/ppermute | solution.py:330
  22.6 18.3 %collective-permute-start.10 = (bf16[480,768]{1,0:T(8,128)(2,1)S(1)}, bf16[480,768]{1,0:T(8,128)(2,1)S(1)}, u32[]{:S(2)}, u32[]{:S(2)}) collective-permute-start(bf16[480,768]{1,0:T(8,128)(2,1)S(1)} %stack.17.refs_3_), channel_id=1, source_target_pairs={{0,8},{8,16},{16,24},{24,0},{1,9},{9,17},{17,25},{25,1},{2,10},{10... | collective-permute-start | bytes 2211848 | tf_op jit(solution)/shard_map/ppermute | solution.py:330
  23.7 17.2 %collective-permute-start.11 = (bf16[480,768]{1,0:T(8,128)(2,1)S(1)}, bf16[480,768]{1,0:T(8,128)(2,1)S(1)}, u32[]{:S(2)}, u32[]{:S(2)}) collective-permute-start(bf16[480,768]{1,0:T(8,128)(2,1)S(1)} %stack.17.refs_3_), channel_id=1, source_target_pairs={{0,24},{8,0},{16,8},{24,16},{1,25},{9,1},{17,9},{25,17},{2,26},{10... | collective-permute-start | bytes 2211848 | tf_op jit(solution)/shard_map/ppermute | solution.py:330
  25.9 7.6 %collective-permute-start.6 = (bf16[160,384]{1,0:T(8,128)(2,1)}, bf16[160,384]{1,0:T(8,128)(2,1)S(1)}, u32[]{:S(2)}, u32[]{:S(2)}) collective-permute-start(bf16[160,384]{1,0:T(8,128)(2,1)} %get-tuple-element.65), channel_id=1, source_target_pairs={{0,32},{32,64},{64,96},{96,0},{1,33},{33,65},{65,97},{97,1},{2,34}... | collective-permute-start | bytes 368648 | tf_op jit(solution)/shard_map/ppermute | solution.py:330
  27.1 6.5 %collective-permute-start.7 = (bf16[160,384]{1,0:T(8,128)(2,1)}, bf16[160,384]{1,0:T(8,128)(2,1)S(1)}, u32[]{:S(2)}, u32[]{:S(2)}) collective-permute-start(bf16[160,384]{1,0:T(8,128)(2,1)} %get-tuple-element.66), channel_id=1, source_target_pairs={{0,96},{32,0},{64,32},{96,64},{1,97},{33,1},{65,33},{97,65},{2,98}... | collective-permute-start | bytes 368648 | tf_op jit(solution)/shard_map/ppermute | solution.py:330
  29.2 6.6 %collective-permute-start.8 = (bf16[160,384]{1,0:T(8,128)(2,1)}, bf16[160,384]{1,0:T(8,128)(2,1)S(1)}, u32[]{:S(2)}, u32[]{:S(2)}) collective-permute-start(bf16[160,384]{1,0:T(8,128)(2,1)} %get-tuple-element.67), channel_id=1, source_target_pairs={{0,64},{32,96},{64,0},{96,32},{1,65},{33,97},{65,1},{97,33},{2,66}... | collective-permute-start | bytes 368648 | tf_op jit(solution)/shard_map/ppermute | solution.py:330
  35.8 0.9 %copy-start.1 = (bf16[160,384]{1,0:T(8,128)(2,1)S(1)}, bf16[160,384]{1,0:T(8,128)(2,1)}, u32[]{:S(2)}) copy-start(bf16[160,384]{1,0:T(8,128)(2,1)} %get-tuple-element.64.refs_0_) | copy-start | bytes 368644
  37.3 1.9 %collective-permute-start.9 = (bf16[640,384]{1,0:T(8,128)(2,1)S(1)}, bf16[640,384]{1,0:T(8,128)(2,1)S(1)}, u32[]{:S(2)}, u32[]{:S(2)}) collective-permute-start(bf16[640,384]{1,0:T(8,128)(2,1)S(1)} %stack.15.refs_0_.q), channel_id=1, source_target_pairs={{0,4},{4,0},{1,5},{5,1},{2,6},{6,2},{3,7},{7,3},{8,12},{12,8},{9,1... | collective-permute-start | bytes 1474568 | tf_op jit(solution)/shard_map/ppermute | solution.py:330
  37.4 0.9 %copy-start = (bf16[160,768]{1,0:T(8,128)(2,1)S(1)}, bf16[160,768]{1,0:T(8,128)(2,1)}, u32[]{:S(2)}) copy-start(bf16[160,768]{1,0:T(8,128)(2,1)} %get-tuple-element.62.refs_0_) | copy-start | bytes 737284
  41.1 11.6 %collective-permute-start.12 = (bf16[240,768]{1,0:T(8,128)(2,1)S(1)}, bf16[240,768]{1,0:T(8,128)(2,1)S(1)}, u32[]{:S(2)}, u32[]{:S(2)}) collective-permute-start(bf16[240,768]{1,0:T(8,128)(2,1)S(1)} %take_rows.2), channel_id=1, source_target_pairs={{0,8},{8,16},{16,24},{24,0},{1,9},{9,17},{17,25},{25,1},{2,10},{10... | collective-permute-start | bytes 1105928 | tf_op jit(solution)/shard_map/ppermute | solution.py:330
  42.0 10.7 %collective-permute-start.13 = (bf16[240,768]{1,0:T(8,128)(2,1)S(1)}, bf16[240,768]{1,0:T(8,128)(2,1)S(1)}, u32[]{:S(2)}, u32[]{:S(2)}) collective-permute-start(bf16[240,768]{1,0:T(8,128)(2,1)S(1)} %take_rows.3), channel_id=1, source_target_pairs={{0,24},{8,0},{16,8},{24,16},{1,25},{9,1},{17,9},{25,17},{2,26},{10... | collective-permute-start | bytes 1105928 | tf_op jit(solution)/shard_map/ppermute | solution.py:330
  44.8 23.3 %slice-start = ((s8[18874368]{0:T(1024)(128)(4,1)}), s8[4194304]{0:T(1024)(128)(4,1)S(1)}, s32[]{:S(2)}) async-start(s8[18874368]{0:T(1024)(128)(4,1)} %bitcast.12), calls=%async_computation | async-start | bytes 8388608
  44.8 23.3 %slice-start.1 = ((s8[18874368]{0:T(1024)(128)(4,1)}), s8[4194304]{0:T(1024)(128)(4,1)S(1)}, s32[]{:S(2)}) async-start(s8[18874368]{0:T(1024)(128)(4,1)} %bitcast.12), calls=%async_computation.1 | async-start | bytes 8388608
  44.8 23.3 %slice-start.2 = ((s8[18874368]{0:T(1024)(128)(4,1)}), s8[4194304]{0:T(1024)(128)(4,1)S(1)}, s32[]{:S(2)}) async-start(s8[18874368]{0:T(1024)(128)(4,1)} %bitcast.12), calls=%async_computation.2 | async-start | bytes 8388608
  52.1 3.4 %collective-permute-start.17 = (bf16[4,160,384]{2,1,0:T(8,128)(2,1)S(1)}, bf16[4,160,384]{2,1,0:T(8,128)(2,1)S(1)}, u32[]{:S(2)}, u32[]{:S(2)}) collective-permute-start(bf16[4,160,384]{2,1,0:T(8,128)(2,1)S(1)} %get-tuple-element.88), channel_id=1, source_target_pairs={{0,4},{4,0},{1,5},{5,1},{2,6},{6,2},{3,7},{7,3},{8,12},{12,8},{9,1... | collective-permute-start | bytes 1474568 | tf_op jit(solution)/shard_map/ppermute | solution.py:330
  52.2 3.3 %collective-permute-start.18 = (f32[4,160,128]{2,1,0:T(8,128)S(1)}, f32[4,160,128]{2,1,0:T(8,128)S(1)}, u32[]{:S(2)}, u32[]{:S(2)}) collective-permute-start(f32[4,160,128]{2,1,0:T(8,128)S(1)} %get-tuple-element.89), channel_id=1, source_target_pairs={{0,4},{4,0},{1,5},{5,1},{2,6},{6,2},{3,7},{7,3},{8,12},{12,8},{9,1... | collective-permute-start | bytes 983048 | tf_op jit(solution)/shard_map/ppermute | solution.py:330
  52.7 3.2 %collective-permute-start.15 = (bf16[240,768]{1,0:T(8,128)(2,1)S(1)}, bf16[240,768]{1,0:T(8,128)(2,1)S(1)}, u32[]{:S(2)}, u32[]{:S(2)}) collective-permute-start(bf16[240,768]{1,0:T(8,128)(2,1)S(1)} %collective-permute-done.12.refs_1_), channel_id=1, source_target_pairs={{0,4},{4,0},{1,5},{5,1},{2,6},{6,2},{3,7},{7,3},{8,12},{12,8},{9,1... | collective-permute-start | bytes 1105928 | tf_op jit(solution)/shard_map/ppermute | solution.py:330
  52.8 3.1 %collective-permute-start.16 = (bf16[240,768]{1,0:T(8,128)(2,1)S(1)}, bf16[240,768]{1,0:T(8,128)(2,1)S(1)}, u32[]{:S(2)}, u32[]{:S(2)}) collective-permute-start(bf16[240,768]{1,0:T(8,128)(2,1)S(1)} %collective-permute-done.13.refs_2_), channel_id=1, source_target_pairs={{0,4},{4,0},{1,5},{5,1},{2,6},{6,2},{3,7},{7,3},{8,12},{12,8},{9,1... | collective-permute-start | bytes 1105928 | tf_op jit(solution)/shard_map/ppermute | solution.py:330
  53.2 2.7 %collective-permute-start.14 = (bf16[160,768]{1,0:T(8,128)(2,1)S(1)}, bf16[160,768]{1,0:T(8,128)(2,1)S(1)}, u32[]{:S(2)}, u32[]{:S(2)}) collective-permute-start(bf16[160,768]{1,0:T(8,128)(2,1)S(1)} %collective-permute-done.5.refs_0_), channel_id=1, source_target_pairs={{0,4},{4,0},{1,5},{5,1},{2,6},{6,2},{3,7},{7,3},{8,12},{12,8},{9,1... | collective-permute-start | bytes 737288 | tf_op jit(solution)/shard_map/ppermute | solution.py:330
  53.3 14.9 %slice-start.3 = ((s8[18874368]{0:T(1024)(128)(4,1)}), s8[4194304]{0:T(1024)(128)(4,1)S(1)}, s32[]{:S(2)}) async-start(s8[18874368]{0:T(1024)(128)(4,1)} %bitcast.12), calls=%async_computation.3 | async-start | bytes 8388608
  55.9 12.3 %slice-start.4 = ((s8[18874368]{0:T(1024)(128)(4,1)}), s8[2097152]{0:T(1024)(128)(4,1)S(1)}, s32[]{:S(2)}) async-start(s8[18874368]{0:T(1024)(128)(4,1)} %bitcast.12), calls=%async_computation.4 | async-start | bytes 4194304
  58.5 6.6 %collective-permute-start.19 = (bf16[160,384]{1,0:T(8,128)(2,1)S(1)}, bf16[160,384]{1,0:T(8,128)(2,1)S(1)}, u32[]{:S(2)}, u32[]{:S(2)}) collective-permute-start(bf16[160,384]{1,0:T(8,128)(2,1)S(1)} %get-tuple-element.91), channel_id=1, source_target_pairs={{0,32},{32,64},{64,96},{96,0},{1,33},{33,65},{65,97},{97,1},{2,34}... | collective-permute-start | bytes 368648 | tf_op jit(solution)/shard_map/ppermute | solution.py:330
  59.4 7.7 %collective-permute-start.20 = (bf16[160,384]{1,0:T(8,128)(2,1)S(1)}, bf16[160,384]{1,0:T(8,128)(2,1)S(1)}, u32[]{:S(2)}, u32[]{:S(2)}) collective-permute-start(bf16[160,384]{1,0:T(8,128)(2,1)S(1)} %get-tuple-element.92), channel_id=1, source_target_pairs={{0,96},{32,0},{64,32},{96,64},{1,97},{33,1},{65,33},{97,65},{2,98}... | collective-permute-start | bytes 368648 | tf_op jit(solution)/shard_map/ppermute | solution.py:330
  61.8 6.4 %collective-permute-start.21 = (bf16[160,384]{1,0:T(8,128)(2,1)S(1)}, bf16[160,384]{1,0:T(8,128)(2,1)S(1)}, u32[]{:S(2)}, u32[]{:S(2)}) collective-permute-start(bf16[160,384]{1,0:T(8,128)(2,1)S(1)} %get-tuple-element.93), channel_id=1, source_target_pairs={{0,64},{32,96},{64,0},{96,32},{1,65},{33,97},{65,1},{97,33},{2,66}... | collective-permute-start | bytes 368648 | tf_op jit(solution)/shard_map/ppermute | solution.py:330
  69.2 8.6 %collective-permute-start.24 = (bf16[160,768]{1,0:T(8,128)(2,1)S(1)}, bf16[160,768]{1,0:T(8,128)(2,1)S(1)}, u32[]{:S(2)}, u32[]{:S(2)}) collective-permute-start(bf16[160,768]{1,0:T(8,128)(2,1)S(1)} %get-tuple-element.102), channel_id=1, source_target_pairs={{0,1},{1,2},{2,3},{3,0},{4,5},{5,6},{6,7},{7,4},{8,9},{9,10},{10,1... | collective-permute-start | bytes 737288 | tf_op jit(solution)/shard_map/ppermute | solution.py:330
  69.8 10.1 %collective-permute-start.25 = (bf16[160,768]{1,0:T(8,128)(2,1)S(1)}, bf16[160,768]{1,0:T(8,128)(2,1)S(1)}, u32[]{:S(2)}, u32[]{:S(2)}) collective-permute-start(bf16[160,768]{1,0:T(8,128)(2,1)S(1)} %get-tuple-element.103), channel_id=1, source_target_pairs={{0,3},{1,0},{2,1},{3,2},{4,7},{5,4},{6,5},{7,6},{8,11},{9,8},{10,9... | collective-permute-start | bytes 737288 | tf_op jit(solution)/shard_map/ppermute | solution.py:330
  72.4 12.5 %collective-permute-start.22 = (bf16[160,768]{1,0:T(8,128)(2,1)S(1)}, bf16[160,768]{1,0:T(8,128)(2,1)S(1)}, u32[]{:S(2)}, u32[]{:S(2)}) collective-permute-start(bf16[160,768]{1,0:T(8,128)(2,1)S(1)} %get-tuple-element.96), channel_id=1, source_target_pairs={{0,3},{1,0},{2,1},{3,2},{4,7},{5,4},{6,5},{7,6},{8,11},{9,8},{10,9... | collective-permute-start | bytes 737288 | tf_op jit(solution)/shard_map/ppermute | solution.py:330
  73.3 11.6 %collective-permute-start.23 = (bf16[160,768]{1,0:T(8,128)(2,1)S(1)}, bf16[160,768]{1,0:T(8,128)(2,1)S(1)}, u32[]{:S(2)}, u32[]{:S(2)}) collective-permute-start(bf16[160,768]{1,0:T(8,128)(2,1)S(1)} %get-tuple-element.97), channel_id=1, source_target_pairs={{0,1},{1,2},{2,3},{3,0},{4,5},{5,6},{6,7},{7,4},{8,9},{9,10},{10,1... | collective-permute-start | bytes 737288 | tf_op jit(solution)/shard_map/ppermute | solution.py:330
  80.0 6.3 %collective-permute-start.26 = (bf16[160,768]{1,0:T(8,128)(2,1)S(1)}, bf16[160,768]{1,0:T(8,128)(2,1)S(1)}, u32[]{:S(2)}, u32[]{:S(2)}) collective-permute-start(bf16[160,768]{1,0:T(8,128)(2,1)S(1)} %get-tuple-element.104), channel_id=1, source_target_pairs={{0,1},{1,2},{2,3},{3,0},{4,5},{5,6},{6,7},{7,4},{8,9},{9,10},{10,1... | collective-permute-start | bytes 737288 | tf_op jit(solution)/shard_map/ppermute | solution.py:330
  80.4 7.4 %collective-permute-start.27 = (bf16[160,768]{1,0:T(8,128)(2,1)S(1)}, bf16[160,768]{1,0:T(8,128)(2,1)S(1)}, u32[]{:S(2)}, u32[]{:S(2)}) collective-permute-start(bf16[160,768]{1,0:T(8,128)(2,1)S(1)} %get-tuple-element.105), channel_id=1, source_target_pairs={{0,3},{1,0},{2,1},{3,2},{4,7},{5,4},{6,5},{7,6},{8,11},{9,8},{10,9... | collective-permute-start | bytes 737288 | tf_op jit(solution)/shard_map/ppermute | solution.py:330

commit v5 on v4

--- a/solution.py
+++ b/solution.py
@@ -210,23 +210,38 @@
             log_out[yq, :, columns] = top + jnp.log2(weight_sum)
 
 
-def last_kernel(bias_ref, q, *refs):
-    parts, states, outs, scratch, o_s = refs[:3], refs[3:7], refs[7:11], refs[11:14], refs[14]
+def last_kernel(targets, bias_ref, q, *refs):
+    parts, states, outs, scratch = refs[:3], refs[3:7], refs[7:-3], refs[-3:]
     o_here, log_here, o_there, log_there = states
+    k_s, v_s = scratch[1:]
+    ones = jnp.ones((k_s.shape[1], HEAD_DIM), jnp.bfloat16)
     for head in range(HEADS):
         columns = slice(head * HEAD_DIM, (head + 1) * HEAD_DIM)
-        lay_out(lax.axis_index("y"), head, (q,), (parts,), *scratch)
-        for yq, result in enumerate(partial_attention(bias_ref, *scratch, head)):
-            log = log_there[yq, :, head * LOG_LANES : head * LOG_LANES + 1]
-            here = (o_here[yq, :, columns], log_here[yq, :, columns])
-            there = (o_there[yq, :, columns], jnp.broadcast_to(log, (TOK, HEAD_DIM)))
+        lay_out(lax.axis_index("y"), head, (), (parts,), *scratch)
+    groups = [lax.rem(lax.axis_index("y") + Y_OFFSETS[j], 4) for j in targets]
+    for head in range(HEADS):
+        columns = slice(head * HEAD_DIM, (head + 1) * HEAD_DIM)
+        scores = [
+            lax.dot_general(
+                q[j * TOK : (j + 1) * TOK, columns], k_s[head], (((1,), (1,)), ((), ())),
+                preferred_element_type=jnp.float32,
+            ) + bias_ref[0, pl.ds(group, 1), :]
+            for j, group in zip(targets, groups)
+        ]
+        tops = [jnp.max(s, axis=-1, keepdims=True) for s in scores]
+        weights = [jnp.exp2((s - t) * FACTOR).astype(jnp.bfloat16) for s, t in zip(scores, tops)]
+        values = jnp.concatenate([v_s[head], ones], axis=1)
+        for group, top, w, out_ref in zip(groups, tops, weights, outs):
+            total = jnp.dot(w, values, preferred_element_type=jnp.float32)
+            log = log_there[group, :, head * LOG_LANES : head * LOG_LANES + 1]
+            here = (o_here[group, :, columns], log_here[group, :, columns])
+            there = (o_there[group, :, columns], jnp.broadcast_to(log, (TOK, HEAD_DIM)))
+            result = (top * FACTOR, total[:, :HEAD_DIM], total[:, HEAD_DIM:])
             _, out, weight_sum = merge_states(result, [here, there])
-            o_s[yq, :, columns] = (out / weight_sum).astype(jnp.bfloat16)
-    for out, distance in zip(outs, (0, 1, 3, 2)):
-        out[...] = o_s[lax.rem(lax.axis_index("y") + distance, 4)]
-
-
-def attend(kernel, bias, qs, pieces, states, outs, scratch=()):
+            out_ref[:, columns] = (out / weight_sum).astype(jnp.bfloat16)
+
+
+def attend(kernel, bias, qs, pieces, states, outs, name):
     vmem = pl.BlockSpec(memory_space=pltpu.VMEM)
     operands = [bias, *qs]
     for arrays in pieces:
@@ -242,13 +257,12 @@
             pltpu.VMEM((HEADS, 4 * TOK * len(qs), HEAD_DIM), jnp.bfloat16),
             pltpu.VMEM((HEADS, keys_here, HEAD_DIM), jnp.bfloat16),
             pltpu.VMEM((HEADS, keys_here, HEAD_DIM), jnp.bfloat16),
-            *scratch,
         ],
         compiler_params=pltpu.CompilerParams(vmem_limit_bytes=20 * 2**20),
         cost_estimate=pl.CostEstimate(
             flops=4 * 10**9 * len(pieces), bytes_accessed=2**20, transcendentals=0
         ),
-        name=kernel.__name__,
+        name=name,
     )(*operands)
 
 
@@ -391,18 +405,25 @@
     o_here, log_here, o_there, log_there = attend(
         near_kernel, biases[0], (q_here, q_there), pieces, (),
         [(state, f32), (state, f32), (state, bf16), ((VIDEO_GROUPS, TOK, HEAD_DIM), f32)],
+        "attend_near",
     )
     o_here, far = barrier((o_here, far))
     far_there = tuple(shift(part, "core", 1) for part in far)
     here = attend(
         far_kernel, biases[1], (q_here,), (far,), (o_here, log_here),
-        [(state, f32), (state, f32)],
+        [(state, f32), (state, f32)], "attend_far",
     )
     there = (shift(o_there, "core", 1), shift(log_there, "core", 1))
-    out, out_up, out_down, out_across = attend(
-        last_kernel, biases[2], (q_here,), (far_there,), (*here, *there),
-        [((TOK, WIDTH), bf16)] * 4, [pltpu.VMEM(state, bf16)],
-    )
+
+    def last(*targets):
+        return attend(
+            functools.partial(last_kernel, targets), biases[2], (q_here,), (far_there,),
+            (*here, *there), [((TOK, WIDTH), bf16)] * len(targets), "attend_last",
+        )
+
+    (out_across,) = last(3)
+    out_down, out_up = last(1, 2)
+    (out,) = last(0)
     attended = (out, shift(out_up, "y", 1), shift(out_down, "y", -1), shift(out_across, "y", 2))
 
     across_a, across_b = project(attended, out_weight, ((2, 0), (2, 1)))

time: 89 us -> 88.7 us (level)
  waiting for transfers between devices: 22.6 us -> 19.4 us
  starting transfers between devices: 33.5 us -> 35 us
  Pallas kernels: 23 us -> 24.4 us
    ppermute x28, waiting for transfers between devices: 22.6 us -> 19.4 us  [shift(): return lax.ppermute(x, axis, [(i, (i + step) % size) for i in range(size)])]
    ppermute x28, starting transfers between devices: 33.5 us -> 35 us  [shift(): return lax.ppermute(x, axis, [(i, (i + step) % size) for i in range(size)])]
    pallas_call x3 -> x5, Pallas kernels: 11.9 us -> 13.3 us  [attend(): pl.pallas_call(kernel, in_specs=[vmem] * len(operands), out_specs=[vmem]...]
  transfers between devices with their start and end apart: 28 -> 28, of which waited for: 14 -> 12; matrix products, arithmetic and copies ran while one was open for 6% -> 6% of each run, Pallas kernels for 17% -> 21%
where the time goes in v5:
time: 88.7 us; the launch traced here: 88.4 us
  starting transfers between devices  35 us (39%)
  Pallas kernels  24.4 us (28%)
  waiting for transfers between devices  19.4 us (22%)
  local copies, waits for them, and re-layouts  6.05 us (7%)
  between operations  2.38 us (3%)
  other arithmetic  1.15 us (1%)
    ppermute x28, starting transfers between devices, shift(): return lax.ppermute(x, axis, [(i, (i + step) % size) for i in range(size)])  35 us
    ppermute x28, waiting for transfers between devices, shift(): return lax.ppermute(x, axis, [(i, (i + step) % size) for i in range(size)])  19.4 us
    pallas_call x5, Pallas kernels, attend(): pl.pallas_call(kernel, in_specs=[vmem] * len(operands), out_specs=[vmem]...  13.3 us
    pallas_call x2, Pallas kernels, pack_by_owner(): pl.pallas_call(functools.partial(pack_kernel, count), in_specs=[hbm] * co...  3.91 us
    pallas_call x3, Pallas kernels, project(): pl.pallas_call(functools.partial(project_kernel, places), in_specs=[vmem]...  3.87 us
    pallas_call x3, Pallas kernels, stack(): pl.pallas_call(stack_kernel, in_specs=[pl.BlockSpec(memory_space=pltpu.VM...  1.88 us
    unnamed x14, local copies, waits for them, and re-layouts  1.87 us
  transfers between devices with their start and end apart: 28, of which 12 were waited for; matrix products, arithmetic and copies ran while one was open for 6% of the time, Pallas kernels for 21%

profile of v5, /device:TPU:6, one launch (start us, length us, event | category | flops | bytes accessed | tf_op | source)
XLA Modules:
  0.0 88.4 jit_solution(12449459195306609439)
XLA Ops:
  0.0 2.1 %pack_by_owner.2 = (bf16[160,768]{1,0:T(8,128)(2,1)}, bf16[160,768]{1,0:T(8,128)(2,1)}, bf16[160,768]{1,0:T(8,128)(2,1)}, bf16[160,768]{1,0:T(8,128)(2,1)}) custom-call(bf16[160,1536]{1,0:T(8,128)(2,1)} %refs_0_.2, bf16[160,1536]{1,0:T(8,128)(2,1)} %refs_1_.1), custom_call_target="tpu_custom_call" | custom-call | tf_op jit(solution)/shard_map/pack_by_owner/pallas_call | solution.py:83
  2.1 2.0 %collective-permute-start.3 = (bf16[160,768]{1,0:T(8,128)(2,1)}, bf16[160,768]{1,0:T(8,128)(2,1)S(1)}, u32[]{:S(2)}, u32[]{:S(2)}) collective-permute-start(bf16[160,768]{1,0:T(8,128)(2,1)} %get-tuple-element.60.refs_0_), channel_id=1, source_target_pairs={{0,8},{8,16},{16,24},{24,0},{1,9},{9,17},{17,25},{25,1},{2,10},{10... | collective-permute-start | bytes 737288 | tf_op jit(solution)/shard_map/ppermute | solution.py:344
  4.1 2.2 %collective-permute-start.4 = (bf16[160,768]{1,0:T(8,128)(2,1)}, bf16[160,768]{1,0:T(8,128)(2,1)S(1)}, u32[]{:S(2)}, u32[]{:S(2)}) collective-permute-start(bf16[160,768]{1,0:T(8,128)(2,1)} %get-tuple-element.60.refs_0_), channel_id=1, source_target_pairs={{0,24},{8,0},{16,8},{24,16},{1,25},{9,1},{17,9},{25,17},{2,26},{10... | collective-permute-start | bytes 737288 | tf_op jit(solution)/shard_map/ppermute | solution.py:344
  6.3 1.6 %collective-permute-start = (bf16[160,768]{1,0:T(8,128)(2,1)}, bf16[160,768]{1,0:T(8,128)(2,1)S(1)}, u32[]{:S(2)}, u32[]{:S(2)}) collective-permute-start(bf16[160,768]{1,0:T(8,128)(2,1)} %get-tuple-element.54), channel_id=1, source_target_pairs={{0,32},{32,64},{64,96},{96,0},{1,33},{33,65},{65,97},{97,1},{2,34}... | collective-permute-start | bytes 737288 | tf_op jit(solution)/shard_map/ppermute | solution.py:344
  7.9 1.7 %collective-permute-start.1 = (bf16[160,768]{1,0:T(8,128)(2,1)}, bf16[160,768]{1,0:T(8,128)(2,1)S(1)}, u32[]{:S(2)}, u32[]{:S(2)}) collective-permute-start(bf16[160,768]{1,0:T(8,128)(2,1)} %get-tuple-element.55), channel_id=1, source_target_pairs={{0,96},{32,0},{64,32},{96,64},{1,97},{33,1},{65,33},{97,65},{2,98}... | collective-permute-start | bytes 737288 | tf_op jit(solution)/shard_map/ppermute | solution.py:344
  9.5 2.0 %collective-permute-start.2 = (bf16[160,768]{1,0:T(8,128)(2,1)}, bf16[160,768]{1,0:T(8,128)(2,1)S(1)}, u32[]{:S(2)}, u32[]{:S(2)}) collective-permute-start(bf16[160,768]{1,0:T(8,128)(2,1)} %get-tuple-element.56), channel_id=1, source_target_pairs={{0,64},{32,96},{64,0},{96,32},{1,65},{33,97},{65,1},{97,33},{2,66}... | collective-permute-start | bytes 737288 | tf_op jit(solution)/shard_map/ppermute | solution.py:344
  11.5 0.8 fusion
  12.3 0.2 reshape.89
  12.6 0.1 copy.15
  12.8 0.1 copy.16
  12.9 0.1 copy.17
  13.1 0.1 copy.18
  13.3 0.1 copy.19
  13.4 0.2 select_reduce_fusion.1
  13.9 0.2 select_reduce_fusion
  14.8 1.3 %dynamic_slice.57 = s32[1]{0:T(128)} dynamic-slice(s32[4]{0:T(128)} %param.13, s32[]{:T(128)S(6)} %select_n.135), dynamic_slice_sizes={1} | dynamic-slice | bytes 12 | tf_op jit(solution)/shard_map/jit(dynamic_index_in_dim)/dynamic_slice | solution.py:372
  17.4 1.8 %pack_by_owner.3 = (bf16[160,384]{1,0:T(8,128)(2,1)}, bf16[160,384]{1,0:T(8,128)(2,1)}, bf16[160,384]{1,0:T(8,128)(2,1)}, bf16[160,384]{1,0:T(8,128)(2,1)}) custom-call(bf16[160,1536]{1,0:T(8,128)(2,1)} %refs_0_.3), custom_call_target="tpu_custom_call" | custom-call | tf_op jit(solution)/shard_map/pack_by_owner/pallas_call | solution.py:83
  19.9 0.9 %dynamic_slice.58.gate_ref = f32[1,1536]{1,0:T(1,128)S(1)} dynamic-slice(f32[16,6144]{1,0:T(8,128)} %param.11, s32[]{:T(128)S(6)} %select_n.136, s32[]{:T(128)S(6)} %select_n.137), dynamic_slice_sizes={1,1536} | dynamic-slice | bytes 12292 | tf_op jit(solution)/shard_map/dynamic_slice | solution.py:370
  20.9 0.7 collective-permute-done.2.refs_2_
  21.7 0.9 %stack.17.refs_3_ = bf16[480,768]{1,0:T(8,128)(2,1)S(1)} custom-call(bf16[160,768]{1,0:T(8,128)(2,1)S(1)} %collective-permute-done.refs_0_, bf16[160,768]{1,0:T(8,128)(2,1)S(1)} %collective-permute-done.1.refs_1_, bf16[160,768]{1,0:T(8,128)(2,1)S(1)} %collective-permute-done.2.refs_2_), custom_call_target="tpu_custom_call" | custom-call | tf_op jit(solution)/shard_map/stack/pallas_call | solution.py:111
  22.6 1.1 %collective-permute-start.10 = (bf16[480,768]{1,0:T(8,128)(2,1)S(1)}, bf16[480,768]{1,0:T(8,128)(2,1)S(1)}, u32[]{:S(2)}, u32[]{:S(2)}) collective-permute-start(bf16[480,768]{1,0:T(8,128)(2,1)S(1)} %stack.17.refs_3_), channel_id=1, source_target_pairs={{0,8},{8,16},{16,24},{24,0},{1,9},{9,17},{17,25},{25,1},{2,10},{10... | collective-permute-start | bytes 2211848 | tf_op jit(solution)/shard_map/ppermute | solution.py:344
  23.7 2.2 %collective-permute-start.11 = (bf16[480,768]{1,0:T(8,128)(2,1)S(1)}, bf16[480,768]{1,0:T(8,128)(2,1)S(1)}, u32[]{:S(2)}, u32[]{:S(2)}) collective-permute-start(bf16[480,768]{1,0:T(8,128)(2,1)S(1)} %stack.17.refs_3_), channel_id=1, source_target_pairs={{0,24},{8,0},{16,8},{24,16},{1,25},{9,1},{17,9},{25,17},{2,26},{10... | collective-permute-start | bytes 2211848 | tf_op jit(solution)/shard_map/ppermute | solution.py:344
  25.9 1.1 %collective-permute-start.6 = (bf16[160,384]{1,0:T(8,128)(2,1)}, bf16[160,384]{1,0:T(8,128)(2,1)S(1)}, u32[]{:S(2)}, u32[]{:S(2)}) collective-permute-start(bf16[160,384]{1,0:T(8,128)(2,1)} %get-tuple-element.63), channel_id=1, source_target_pairs={{0,32},{32,64},{64,96},{96,0},{1,33},{33,65},{65,97},{97,1},{2,34}... | collective-permute-start | bytes 368648 | tf_op jit(solution)/shard_map/ppermute | solution.py:344
  27.1 2.1 %collective-permute-start.7 = (bf16[160,384]{1,0:T(8,128)(2,1)}, bf16[160,384]{1,0:T(8,128)(2,1)S(1)}, u32[]{:S(2)}, u32[]{:S(2)}) collective-permute-start(bf16[160,384]{1,0:T(8,128)(2,1)} %get-tuple-element.64), channel_id=1, source_target_pairs={{0,96},{32,0},{64,32},{96,64},{1,97},{33,1},{65,33},{97,65},{2,98}... | collective-permute-start | bytes 368648 | tf_op jit(solution)/shard_map/ppermute | solution.py:344
  29.2 1.0 %collective-permute-start.8 = (bf16[160,384]{1,0:T(8,128)(2,1)}, bf16[160,384]{1,0:T(8,128)(2,1)S(1)}, u32[]{:S(2)}, u32[]{:S(2)}) collective-permute-start(bf16[160,384]{1,0:T(8,128)(2,1)} %get-tuple-element.65), channel_id=1, source_target_pairs={{0,64},{32,96},{64,0},{96,32},{1,65},{33,97},{65,1},{97,33},{2,66}... | collective-permute-start | bytes 368648 | tf_op jit(solution)/shard_map/ppermute | solution.py:344
  30.2 3.3 %collective-permute-done.6.refs_1_ = bf16[160,384]{1,0:T(8,128)(2,1)S(1)} collective-permute-done((bf16[160,384]{1,0:T(8,128)(2,1)}, bf16[160,384]{1,0:T(8,128)(2,1)S(1)}, u32[]{:S(2)}, u32[]{:S(2)}) %collective-permute-start.6) | collective-permute-done | bytes 122912 | tf_op jit(solution)/shard_map/ppermute | solution.py:344
  33.5 2.2 %collective-permute-done.8.refs_3_ = bf16[160,384]{1,0:T(8,128)(2,1)S(1)} collective-permute-done((bf16[160,384]{1,0:T(8,128)(2,1)}, bf16[160,384]{1,0:T(8,128)(2,1)S(1)}, u32[]{:S(2)}, u32[]{:S(2)}) %collective-permute-start.8) | collective-permute-done | bytes 122912 | tf_op jit(solution)/shard_map/ppermute | solution.py:344
  35.8 0.9 %copy-done.1 = bf16[160,384]{1,0:T(8,128)(2,1)S(1)} copy-done((bf16[160,384]{1,0:T(8,128)(2,1)S(1)}, bf16[160,384]{1,0:T(8,128)(2,1)}, u32[]{:S(2)}) %copy-start.1) | copy-done | bytes 122904
  36.7 0.6 stack.15.refs_0_.q
  37.4 0.9 %copy-done = bf16[160,768]{1,0:T(8,128)(2,1)S(1)} copy-done((bf16[160,768]{1,0:T(8,128)(2,1)S(1)}, bf16[160,768]{1,0:T(8,128)(2,1)}, u32[]{:S(2)}) %copy-start) | copy-done | bytes 245784
  38.4 0.3 stack.16.refs_2_
  38.7 0.6 collective-permute-done.9.refs_1_
  39.3 1.7 %collective-permute-done.10.refs_5_.x_ref = bf16[480,768]{1,0:T(8,128)(2,1)S(1)} collective-permute-done((bf16[480,768]{1,0:T(8,128)(2,1)S(1)}, bf16[480,768]{1,0:T(8,128)(2,1)S(1)}, u32[]{:S(2)}, u32[]{:S(2)}) %collective-permute-start.10) | collective-permute-done | bytes 737312 | tf_op jit(solution)/shard_map/ppermute | solution.py:344
  40.9 0.2 take_rows.2
  41.1 0.7 collective-permute-start.12
  41.8 0.2 take_rows.3
  42.0 2.8 %collective-permute-start.13 = (bf16[240,768]{1,0:T(8,128)(2,1)S(1)}, bf16[240,768]{1,0:T(8,128)(2,1)S(1)}, u32[]{:S(2)}, u32[]{:S(2)}) collective-permute-start(bf16[240,768]{1,0:T(8,128)(2,1)S(1)} %take_rows.3), channel_id=1, source_target_pairs={{0,24},{8,0},{16,8},{24,16},{1,25},{9,1},{17,9},{25,17},{2,26},{10... | collective-permute-start | bytes 1105928 | tf_op jit(solution)/shard_map/ppermute | solution.py:344
  44.8 7.3 %attend_near.1 = (f32[4,160,384]{2,1,0:T(8,128)S(1)}, f32[4,160,384]{2,1,0:T(8,128)S(1)}, bf16[4,160,384]{2,1,0:T(8,128)(2,1)S(1)}, f32[4,160,128]{2,1,0:T(8,128)S(1)}) custom-call(f32[2,4,1920]{2,1,0:T(4,128)S(1)} %pad_maximum_fusion.bias_ref, bf16[640,384]{1,0:T(8,128)(2,1)S(1)} %stack.15.refs_0_.q, bf16[640,384]{1,0:T(8,128)(2,1)S(1)} %collective-permute-done.9.refs_1_, ...), custom_call_target="tpu_custom_call" | custom-call | flops 12000000000 | bytes 1048576 | tf_op jit(solution)/shard_map/attend_near/pallas_call | solution.py:251
  52.2 0.5 collective-permute-start.18
  52.8 0.4 collective-permute-start.16
  53.3 2.1 %attend_far.1 = (f32[4,160,384]{2,1,0:T(8,128)S(1)}, f32[4,160,384]{2,1,0:T(8,128)S(1)}) custom-call(f32[1,4,640]{2,1,0:T(4,128)S(1)} %broadcast_in_dim_reshape_reshape.6.bias_ref, bf16[640,384]{1,0:T(8,128)(2,1)S(1)} %stack.15.refs_0_.q, bf16[160,768]{1,0:T(8,128)(2,1)S(1)} %collective-permute-done.5.refs_0_, ...), custom_call_target="tpu_custom_call" | custom-call | flops 4000000000 | bytes 1048576 | tf_op jit(solution)/shard_map/attend_far/pallas_call | solution.py:251
  55.4 0.5 collective-permute-done.14.refs_0_
  55.9 1.0 %attend_last.5 = bf16[160,384]{1,0:T(8,128)(2,1)S(1)} custom-call(f32[1,4,640]{2,1,0:T(4,128)S(1)} %broadcast_in_dim_reshape_reshape.7.bias_ref, bf16[640,384]{1,0:T(8,128)(2,1)S(1)} %stack.15.refs_0_.q, bf16[160,768]{1,0:T(8,128)(2,1)S(1)} %collective-permute-done.14.refs_0_, bf16[240,768]{1,0:T(8,128)(2,1)S(1)} %collective-permute-done.15.refs_1_, ...), custom_call_target="tpu_custom_call" | custom-call | flops 4000000000 | bytes 1048576 | tf_op jit(solution)/shard_map/attend_last/pallas_call | solution.py:251
  57.0 2.3 %collective-permute-start.21 = (bf16[160,384]{1,0:T(8,128)(2,1)S(1)}, bf16[160,384]{1,0:T(8,128)(2,1)S(1)}, u32[]{:S(2)}, u32[]{:S(2)}) collective-permute-start(bf16[160,384]{1,0:T(8,128)(2,1)S(1)} %attend_last.5), channel_id=1, source_target_pairs={{0,64},{32,96},{64,0},{96,32},{1,65},{33,97},{65,1},{97,33},{2,66}... | collective-permute-start | bytes 368648 | tf_op jit(solution)/shard_map/ppermute | solution.py:344
  59.3 1.9 %attend_last.4 = (bf16[160,384]{1,0:T(8,128)(2,1)S(1)}, bf16[160,384]{1,0:T(8,128)(2,1)S(1)}) custom-call(f32[1,4,640]{2,1,0:T(4,128)S(1)} %broadcast_in_dim_reshape_reshape.7.bias_ref, bf16[640,384]{1,0:T(8,128)(2,1)S(1)} %stack.15.refs_0_.q, bf16[160,768]{1,0:T(8,128)(2,1)S(1)} %collective-permute-done.14.refs_0_, ...), custom_call_target="tpu_custom_call" | custom-call | flops 4000000000 | bytes 1048576 | tf_op jit(solution)/shard_map/attend_last/pallas_call | solution.py:251
  61.2 0.7 collective-permute-start.19
  61.9 2.6 %collective-permute-start.20 = (bf16[160,384]{1,0:T(8,128)(2,1)S(1)}, bf16[160,384]{1,0:T(8,128)(2,1)S(1)}, u32[]{:S(2)}, u32[]{:S(2)}) collective-permute-start(bf16[160,384]{1,0:T(8,128)(2,1)S(1)} %get-tuple-element.89), channel_id=1, source_target_pairs={{0,96},{32,0},{64,32},{96,64},{1,97},{33,1},{65,33},{97,65},{2,98}... | collective-permute-start | bytes 368648 | tf_op jit(solution)/shard_map/ppermute | solution.py:344
  64.5 1.0 %attend_last.3.refs_0_ = bf16[160,384]{1,0:T(8,128)(2,1)S(1)} custom-call(f32[1,4,640]{2,1,0:T(4,128)S(1)} %broadcast_in_dim_reshape_reshape.7.bias_ref, bf16[640,384]{1,0:T(8,128)(2,1)S(1)} %stack.15.refs_0_.q, bf16[160,768]{1,0:T(8,128)(2,1)S(1)} %collective-permute-done.14.refs_0_, bf16[240,768]{1,0:T(8,128)(2,1)S(1)} %collective-permute-done.15.refs_1_, ...), custom_call_target="tpu_custom_call" | custom-call | flops 4000000000 | bytes 1048576 | tf_op jit(solution)/shard_map/attend_last/pallas_call | solution.py:251
  65.5 2.0 %collective-permute-done.19.refs_1_ = bf16[160,384]{1,0:T(8,128)(2,1)S(1)} collective-permute-done((bf16[160,384]{1,0:T(8,128)(2,1)S(1)}, bf16[160,384]{1,0:T(8,128)(2,1)S(1)}, u32[]{:S(2)}, u32[]{:S(2)}) %collective-permute-start.19) | collective-permute-done | bytes 122912 | tf_op jit(solution)/shard_map/ppermute | solution.py:344
  67.6 1.0 %project.5 = (bf16[160,768]{1,0:T(8,128)(2,1)S(1)}, bf16[160,768]{1,0:T(8,128)(2,1)S(1)}) custom-call(bf16[160,384]{1,0:T(8,128)(2,1)S(1)} %attend_last.3.refs_0_, bf16[160,384]{1,0:T(8,128)(2,1)S(1)} %collective-permute-done.19.refs_1_, bf16[160,384]{1,0:T(8,128)(2,1)S(1)} %collective-permute-done.20.refs_2_, ...), custom_call_target="tpu_custom_call" | custom-call | flops 754974720 | bytes 4718592 | tf_op jit(solution)/shard_map/project/pallas_call | solution.py:286
  68.6 0.5 collective-permute-start.24
  69.1 1.6 %collective-permute-start.25 = (bf16[160,768]{1,0:T(8,128)(2,1)S(1)}, bf16[160,768]{1,0:T(8,128)(2,1)S(1)}, u32[]{:S(2)}, u32[]{:S(2)}) collective-permute-start(bf16[160,768]{1,0:T(8,128)(2,1)S(1)} %get-tuple-element.99), channel_id=1, source_target_pairs={{0,3},{1,0},{2,1},{3,2},{4,7},{5,4},{6,5},{7,6},{8,11},{9,8},{10,9... | collective-permute-start | bytes 737288 | tf_op jit(solution)/shard_map/ppermute | solution.py:344
  70.7 1.0 %project.4 = (bf16[160,768]{1,0:T(8,128)(2,1)S(1)}, bf16[160,768]{1,0:T(8,128)(2,1)S(1)}) custom-call(bf16[160,384]{1,0:T(8,128)(2,1)S(1)} %attend_last.3.refs_0_, bf16[160,384]{1,0:T(8,128)(2,1)S(1)} %collective-permute-done.19.refs_1_, bf16[160,384]{1,0:T(8,128)(2,1)S(1)} %collective-permute-done.20.refs_2_, ...), custom_call_target="tpu_custom_call" | custom-call | flops 754974720 | bytes 4718592 | tf_op jit(solution)/shard_map/project/pallas_call | solution.py:286
  71.7 0.9 %collective-permute-start.22 = (bf16[160,768]{1,0:T(8,128)(2,1)S(1)}, bf16[160,768]{1,0:T(8,128)(2,1)S(1)}, u32[]{:S(2)}, u32[]{:S(2)}) collective-permute-start(bf16[160,768]{1,0:T(8,128)(2,1)S(1)} %get-tuple-element.92), channel_id=1, source_target_pairs={{0,3},{1,0},{2,1},{3,2},{4,7},{5,4},{6,5},{7,6},{8,11},{9,8},{10,9... | collective-permute-start | bytes 737288 | tf_op jit(solution)/shard_map/ppermute | solution.py:344
  72.6 2.4 %collective-permute-start.23 = (bf16[160,768]{1,0:T(8,128)(2,1)S(1)}, bf16[160,768]{1,0:T(8,128)(2,1)S(1)}, u32[]{:S(2)}, u32[]{:S(2)}) collective-permute-start(bf16[160,768]{1,0:T(8,128)(2,1)S(1)} %get-tuple-element.93), channel_id=1, source_target_pairs={{0,1},{1,2},{2,3},{3,0},{4,5},{5,6},{6,7},{7,4},{8,9},{9,10},{10,1... | collective-permute-start | bytes 737288 | tf_op jit(solution)/shard_map/ppermute | solution.py:344
  75.0 1.8 %project.3 = (f32[160,768]{1,0:T(8,128)S(1)}, f32[160,768]{1,0:T(8,128)S(1)}, f32[160,768]{1,0:T(8,128)S(1)}, f32[160,768]{1,0:T(8,128)S(1)}) custom-call(bf16[160,384]{1,0:T(8,128)(2,1)S(1)} %attend_last.3.refs_0_, bf16[160,384]{1,0:T(8,128)(2,1)S(1)} %collective-permute-done.19.refs_1_, bf16[160,384]{1,0:T(8,128)(2,1)S(1)} %collective-permute-done.20.refs_2_, ...), custom_call_target="tpu_custom_call" | custom-call | flops 1509949440 | bytes 9437184 | tf_op jit(solution)/shard_map/project/pallas_call | solution.py:286
  76.9 0.7 collective-permute-done.24.refs_2_
  77.6 1.7 %collective-permute-done.25.refs_3_ = bf16[160,768]{1,0:T(8,128)(2,1)S(1)} collective-permute-done((bf16[160,768]{1,0:T(8,128)(2,1)S(1)}, bf16[160,768]{1,0:T(8,128)(2,1)S(1)}, u32[]{:S(2)}, u32[]{:S(2)}) %collective-permute-start.25) | collective-permute-done | bytes 245792 | tf_op jit(solution)/shard_map/ppermute | solution.py:344
  79.3 0.4 collective-permute-start.26
  79.7 1.7 %collective-permute-start.27 = (bf16[160,768]{1,0:T(8,128)(2,1)S(1)}, bf16[160,768]{1,0:T(8,128)(2,1)S(1)}, u32[]{:S(2)}, u32[]{:S(2)}) collective-permute-start(bf16[160,768]{1,0:T(8,128)(2,1)S(1)} %get-tuple-element.101), channel_id=1, source_target_pairs={{0,3},{1,0},{2,1},{3,2},{4,7},{5,4},{6,5},{7,6},{8,11},{9,8},{10,9... | collective-permute-start | bytes 737288 | tf_op jit(solution)/shard_map/ppermute | solution.py:344
  81.4 3.1 %collective-permute-done.22.refs_2_ = bf16[160,768]{1,0:T(8,128)(2,1)S(1)} collective-permute-done((bf16[160,768]{1,0:T(8,128)(2,1)S(1)}, bf16[160,768]{1,0:T(8,128)(2,1)S(1)}, u32[]{:S(2)}, u32[]{:S(2)}) %collective-permute-start.22) | collective-permute-done | bytes 245792 | tf_op jit(solution)/shard_map/ppermute | solution.py:344
  84.6 1.4 %collective-permute-done.26.summed_a = bf16[160,768]{1,0:T(8,128)(2,1)S(1)} collective-permute-done((bf16[160,768]{1,0:T(8,128)(2,1)S(1)}, bf16[160,768]{1,0:T(8,128)(2,1)S(1)}, u32[]{:S(2)}, u32[]{:S(2)}) %collective-permute-start.26) | collective-permute-done | bytes 245792 | tf_op jit(solution)/shard_map/ppermute | solution.py:344
  86.0 1.4 %collective-permute-done.27.summed_b = bf16[160,768]{1,0:T(8,128)(2,1)S(1)} collective-permute-done((bf16[160,768]{1,0:T(8,128)(2,1)S(1)}, bf16[160,768]{1,0:T(8,128)(2,1)S(1)}, u32[]{:S(2)}, u32[]{:S(2)}) %collective-permute-start.27) | collective-permute-done | bytes 245792 | tf_op jit(solution)/shard_map/ppermute | solution.py:344
  87.4 0.9 %finish.1 = bf16[160,1536]{1,0:T(8,128)(2,1)} custom-call(f32[160,768]{1,0:T(8,128)S(1)} %get-tuple-element.94.own_a, f32[160,768]{1,0:T(8,128)S(1)} %get-tuple-element.95.own_b, bf16[160,768]{1,0:T(8,128)(2,1)S(1)} %collective-permute-done.26.summed_a, bf16[160,768]{1,0:T(8,128)(2,1)S(1)} %collective-permute-done.27.summed_b, ...), custom_call_target="tpu_custom_call" | custom-call | tf_op jit(solution)/shard_map/finish/pallas_call | solution.py:332
  (53 shorter events, 1.9 us)
Async XLA Ops:
  2.1 11.7 %collective-permute-start.3 = (bf16[160,768]{1,0:T(8,128)(2,1)}, bf16[160,768]{1,0:T(8,128)(2,1)S(1)}, u32[]{:S(2)}, u32[]{:S(2)}) collective-permute-start(bf16[160,768]{1,0:T(8,128)(2,1)} %get-tuple-element.60.refs_0_), channel_id=1, source_target_pairs={{0,8},{8,16},{16,24},{24,0},{1,9},{9,17},{17,25},{25,1},{2,10},{10... | collective-permute-start | bytes 737288 | tf_op jit(solution)/shard_map/ppermute | solution.py:344
  4.1 16.8 %collective-permute-start.4 = (bf16[160,768]{1,0:T(8,128)(2,1)}, bf16[160,768]{1,0:T(8,128)(2,1)S(1)}, u32[]{:S(2)}, u32[]{:S(2)}) collective-permute-start(bf16[160,768]{1,0:T(8,128)(2,1)} %get-tuple-element.60.refs_0_), channel_id=1, source_target_pairs={{0,24},{8,0},{16,8},{24,16},{1,25},{9,1},{17,9},{25,17},{2,26},{10... | collective-permute-start | bytes 737288 | tf_op jit(solution)/shard_map/ppermute | solution.py:344
  6.3 14.6 %collective-permute-start = (bf16[160,768]{1,0:T(8,128)(2,1)}, bf16[160,768]{1,0:T(8,128)(2,1)S(1)}, u32[]{:S(2)}, u32[]{:S(2)}) collective-permute-start(bf16[160,768]{1,0:T(8,128)(2,1)} %get-tuple-element.54), channel_id=1, source_target_pairs={{0,32},{32,64},{64,96},{96,0},{1,33},{33,65},{65,97},{97,1},{2,34}... | collective-permute-start | bytes 737288 | tf_op jit(solution)/shard_map/ppermute | solution.py:344
  7.9 13.0 %collective-permute-start.1 = (bf16[160,768]{1,0:T(8,128)(2,1)}, bf16[160,768]{1,0:T(8,128)(2,1)S(1)}, u32[]{:S(2)}, u32[]{:S(2)}) collective-permute-start(bf16[160,768]{1,0:T(8,128)(2,1)} %get-tuple-element.55), channel_id=1, source_target_pairs={{0,96},{32,0},{64,32},{96,64},{1,97},{33,1},{65,33},{97,65},{2,98}... | collective-permute-start | bytes 737288 | tf_op jit(solution)/shard_map/ppermute | solution.py:344
  9.5 12.1 %collective-permute-start.2 = (bf16[160,768]{1,0:T(8,128)(2,1)}, bf16[160,768]{1,0:T(8,128)(2,1)S(1)}, u32[]{:S(2)}, u32[]{:S(2)}) collective-permute-start(bf16[160,768]{1,0:T(8,128)(2,1)} %get-tuple-element.56), channel_id=1, source_target_pairs={{0,64},{32,96},{64,0},{96,32},{1,65},{33,97},{65,1},{97,33},{2,66}... | collective-permute-start | bytes 737288 | tf_op jit(solution)/shard_map/ppermute | solution.py:344
  13.8 7.9 %collective-permute-start.5 = (bf16[160,768]{1,0:T(8,128)(2,1)S(1)}, bf16[160,768]{1,0:T(8,128)(2,1)S(1)}, u32[]{:S(2)}, u32[]{:S(2)}) collective-permute-start(bf16[160,768]{1,0:T(8,128)(2,1)S(1)} %collective-permute-done.3.refs_4_), channel_id=1, source_target_pairs={{0,8},{8,16},{16,24},{24,0},{1,9},{9,17},{17,25},{25,1},{2,10},{10... | collective-permute-start | bytes 737288 | tf_op jit(solution)/shard_map/ppermute | solution.py:344
  22.6 18.3 %collective-permute-start.10 = (bf16[480,768]{1,0:T(8,128)(2,1)S(1)}, bf16[480,768]{1,0:T(8,128)(2,1)S(1)}, u32[]{:S(2)}, u32[]{:S(2)}) collective-permute-start(bf16[480,768]{1,0:T(8,128)(2,1)S(1)} %stack.17.refs_3_), channel_id=1, source_target_pairs={{0,8},{8,16},{16,24},{24,0},{1,9},{9,17},{17,25},{25,1},{2,10},{10... | collective-permute-start | bytes 2211848 | tf_op jit(solution)/shard_map/ppermute | solution.py:344
  23.7 17.2 %collective-permute-start.11 = (bf16[480,768]{1,0:T(8,128)(2,1)S(1)}, bf16[480,768]{1,0:T(8,128)(2,1)S(1)}, u32[]{:S(2)}, u32[]{:S(2)}) collective-permute-start(bf16[480,768]{1,0:T(8,128)(2,1)S(1)} %stack.17.refs_3_), channel_id=1, source_target_pairs={{0,24},{8,0},{16,8},{24,16},{1,25},{9,1},{17,9},{25,17},{2,26},{10... | collective-permute-start | bytes 2211848 | tf_op jit(solution)/shard_map/ppermute | solution.py:344
  25.9 7.6 %collective-permute-start.6 = (bf16[160,384]{1,0:T(8,128)(2,1)}, bf16[160,384]{1,0:T(8,128)(2,1)S(1)}, u32[]{:S(2)}, u32[]{:S(2)}) collective-permute-start(bf16[160,384]{1,0:T(8,128)(2,1)} %get-tuple-element.63), channel_id=1, source_target_pairs={{0,32},{32,64},{64,96},{96,0},{1,33},{33,65},{65,97},{97,1},{2,34}... | collective-permute-start | bytes 368648 | tf_op jit(solution)/shard_map/ppermute | solution.py:344
  27.1 6.5 %collective-permute-start.7 = (bf16[160,384]{1,0:T(8,128)(2,1)}, bf16[160,384]{1,0:T(8,128)(2,1)S(1)}, u32[]{:S(2)}, u32[]{:S(2)}) collective-permute-start(bf16[160,384]{1,0:T(8,128)(2,1)} %get-tuple-element.64), channel_id=1, source_target_pairs={{0,96},{32,0},{64,32},{96,64},{1,97},{33,1},{65,33},{97,65},{2,98}... | collective-permute-start | bytes 368648 | tf_op jit(solution)/shard_map/ppermute | solution.py:344
  29.2 6.6 %collective-permute-start.8 = (bf16[160,384]{1,0:T(8,128)(2,1)}, bf16[160,384]{1,0:T(8,128)(2,1)S(1)}, u32[]{:S(2)}, u32[]{:S(2)}) collective-permute-start(bf16[160,384]{1,0:T(8,128)(2,1)} %get-tuple-element.65), channel_id=1, source_target_pairs={{0,64},{32,96},{64,0},{96,32},{1,65},{33,97},{65,1},{97,33},{2,66}... | collective-permute-start | bytes 368648 | tf_op jit(solution)/shard_map/ppermute | solution.py:344
  35.8 0.9 %copy-start.1 = (bf16[160,384]{1,0:T(8,128)(2,1)S(1)}, bf16[160,384]{1,0:T(8,128)(2,1)}, u32[]{:S(2)}) copy-start(bf16[160,384]{1,0:T(8,128)(2,1)} %get-tuple-element.62.refs_0_) | copy-start | bytes 368644
  37.3 1.9 %collective-permute-start.9 = (bf16[640,384]{1,0:T(8,128)(2,1)S(1)}, bf16[640,384]{1,0:T(8,128)(2,1)S(1)}, u32[]{:S(2)}, u32[]{:S(2)}) collective-permute-start(bf16[640,384]{1,0:T(8,128)(2,1)S(1)} %stack.15.refs_0_.q), channel_id=1, source_target_pairs={{0,4},{4,0},{1,5},{5,1},{2,6},{6,2},{3,7},{7,3},{8,12},{12,8},{9,1... | collective-permute-start | bytes 1474568 | tf_op jit(solution)/shard_map/ppermute | solution.py:344
  37.4 0.9 %copy-start = (bf16[160,768]{1,0:T(8,128)(2,1)S(1)}, bf16[160,768]{1,0:T(8,128)(2,1)}, u32[]{:S(2)}) copy-start(bf16[160,768]{1,0:T(8,128)(2,1)} %get-tuple-element.60.refs_0_) | copy-start | bytes 737284
  41.1 11.6 %collective-permute-start.12 = (bf16[240,768]{1,0:T(8,128)(2,1)S(1)}, bf16[240,768]{1,0:T(8,128)(2,1)S(1)}, u32[]{:S(2)}, u32[]{:S(2)}) collective-permute-start(bf16[240,768]{1,0:T(8,128)(2,1)S(1)} %take_rows.2), channel_id=1, source_target_pairs={{0,8},{8,16},{16,24},{24,0},{1,9},{9,17},{17,25},{25,1},{2,10},{10... | collective-permute-start | bytes 1105928 | tf_op jit(solution)/shard_map/ppermute | solution.py:344
  42.0 10.7 %collective-permute-start.13 = (bf16[240,768]{1,0:T(8,128)(2,1)S(1)}, bf16[240,768]{1,0:T(8,128)(2,1)S(1)}, u32[]{:S(2)}, u32[]{:S(2)}) collective-permute-start(bf16[240,768]{1,0:T(8,128)(2,1)S(1)} %take_rows.3), channel_id=1, source_target_pairs={{0,24},{8,0},{16,8},{24,16},{1,25},{9,1},{17,9},{25,17},{2,26},{10... | collective-permute-start | bytes 1105928 | tf_op jit(solution)/shard_map/ppermute | solution.py:344
  52.1 3.4 %collective-permute-start.17 = (bf16[4,160,384]{2,1,0:T(8,128)(2,1)S(1)}, bf16[4,160,384]{2,1,0:T(8,128)(2,1)S(1)}, u32[]{:S(2)}, u32[]{:S(2)}) collective-permute-start(bf16[4,160,384]{2,1,0:T(8,128)(2,1)S(1)} %get-tuple-element.86), channel_id=1, source_target_pairs={{0,4},{4,0},{1,5},{5,1},{2,6},{6,2},{3,7},{7,3},{8,12},{12,8},{9,1... | collective-permute-start | bytes 1474568 | tf_op jit(solution)/shard_map/ppermute | solution.py:344
  52.2 3.3 %collective-permute-start.18 = (f32[4,160,128]{2,1,0:T(8,128)S(1)}, f32[4,160,128]{2,1,0:T(8,128)S(1)}, u32[]{:S(2)}, u32[]{:S(2)}) collective-permute-start(f32[4,160,128]{2,1,0:T(8,128)S(1)} %get-tuple-element.87), channel_id=1, source_target_pairs={{0,4},{4,0},{1,5},{5,1},{2,6},{6,2},{3,7},{7,3},{8,12},{12,8},{9,1... | collective-permute-start | bytes 983048 | tf_op jit(solution)/shard_map/ppermute | solution.py:344
  52.7 3.2 %collective-permute-start.15 = (bf16[240,768]{1,0:T(8,128)(2,1)S(1)}, bf16[240,768]{1,0:T(8,128)(2,1)S(1)}, u32[]{:S(2)}, u32[]{:S(2)}) collective-permute-start(bf16[240,768]{1,0:T(8,128)(2,1)S(1)} %collective-permute-done.12.refs_1_), channel_id=1, source_target_pairs={{0,4},{4,0},{1,5},{5,1},{2,6},{6,2},{3,7},{7,3},{8,12},{12,8},{9,1... | collective-permute-start | bytes 1105928 | tf_op jit(solution)/shard_map/ppermute | solution.py:344
  52.8 3.1 %collective-permute-start.16 = (bf16[240,768]{1,0:T(8,128)(2,1)S(1)}, bf16[240,768]{1,0:T(8,128)(2,1)S(1)}, u32[]{:S(2)}, u32[]{:S(2)}) collective-permute-start(bf16[240,768]{1,0:T(8,128)(2,1)S(1)} %collective-permute-done.13.refs_2_), channel_id=1, source_target_pairs={{0,4},{4,0},{1,5},{5,1},{2,6},{6,2},{3,7},{7,3},{8,12},{12,8},{9,1... | collective-permute-start | bytes 1105928 | tf_op jit(solution)/shard_map/ppermute | solution.py:344
  53.2 2.7 %collective-permute-start.14 = (bf16[160,768]{1,0:T(8,128)(2,1)S(1)}, bf16[160,768]{1,0:T(8,128)(2,1)S(1)}, u32[]{:S(2)}, u32[]{:S(2)}) collective-permute-start(bf16[160,768]{1,0:T(8,128)(2,1)S(1)} %collective-permute-done.5.refs_0_), channel_id=1, source_target_pairs={{0,4},{4,0},{1,5},{5,1},{2,6},{6,2},{3,7},{7,3},{8,12},{12,8},{9,1... | collective-permute-start | bytes 737288 | tf_op jit(solution)/shard_map/ppermute | solution.py:344
  55.9 11.6 %slice-start = ((s8[18874368]{0:T(1024)(128)(4,1)}), s8[4194304]{0:T(1024)(128)(4,1)S(1)}, s32[]{:S(2)}) async-start(s8[18874368]{0:T(1024)(128)(4,1)} %bitcast.12), calls=%async_computation | async-start | bytes 8388608
  55.9 11.6 %slice-start.1 = ((s8[18874368]{0:T(1024)(128)(4,1)}), s8[4194304]{0:T(1024)(128)(4,1)S(1)}, s32[]{:S(2)}) async-start(s8[18874368]{0:T(1024)(128)(4,1)} %bitcast.12), calls=%async_computation.1 | async-start | bytes 8388608
  56.9 10.6 %slice-start.2 = ((s8[18874368]{0:T(1024)(128)(4,1)}), s8[4194304]{0:T(1024)(128)(4,1)S(1)}, s32[]{:S(2)}) async-start(s8[18874368]{0:T(1024)(128)(4,1)} %bitcast.12), calls=%async_computation.2 | async-start | bytes 8388608
  57.0 10.6 %slice-start.3 = ((s8[18874368]{0:T(1024)(128)(4,1)}), s8[4194304]{0:T(1024)(128)(4,1)S(1)}, s32[]{:S(2)}) async-start(s8[18874368]{0:T(1024)(128)(4,1)} %bitcast.12), calls=%async_computation.3 | async-start | bytes 8388608
  57.0 8.5 %collective-permute-start.21 = (bf16[160,384]{1,0:T(8,128)(2,1)S(1)}, bf16[160,384]{1,0:T(8,128)(2,1)S(1)}, u32[]{:S(2)}, u32[]{:S(2)}) collective-permute-start(bf16[160,384]{1,0:T(8,128)(2,1)S(1)} %attend_last.5), channel_id=1, source_target_pairs={{0,64},{32,96},{64,0},{96,32},{1,65},{33,97},{65,1},{97,33},{2,66}... | collective-permute-start | bytes 368648 | tf_op jit(solution)/shard_map/ppermute | solution.py:344
  61.2 6.4 %collective-permute-start.19 = (bf16[160,384]{1,0:T(8,128)(2,1)S(1)}, bf16[160,384]{1,0:T(8,128)(2,1)S(1)}, u32[]{:S(2)}, u32[]{:S(2)}) collective-permute-start(bf16[160,384]{1,0:T(8,128)(2,1)S(1)} %get-tuple-element.88), channel_id=1, source_target_pairs={{0,32},{32,64},{64,96},{96,0},{1,33},{33,65},{65,97},{97,1},{2,34}... | collective-permute-start | bytes 368648 | tf_op jit(solution)/shard_map/ppermute | solution.py:344
  61.9 5.7 %slice-start.4 = ((s8[18874368]{0:T(1024)(128)(4,1)}), s8[2097152]{0:T(1024)(128)(4,1)S(1)}, s32[]{:S(2)}) async-start(s8[18874368]{0:T(1024)(128)(4,1)} %bitcast.12), calls=%async_computation.4 | async-start | bytes 4194304
  61.9 5.6 %collective-permute-start.20 = (bf16[160,384]{1,0:T(8,128)(2,1)S(1)}, bf16[160,384]{1,0:T(8,128)(2,1)S(1)}, u32[]{:S(2)}, u32[]{:S(2)}) collective-permute-start(bf16[160,384]{1,0:T(8,128)(2,1)S(1)} %get-tuple-element.89), channel_id=1, source_target_pairs={{0,96},{32,0},{64,32},{96,64},{1,97},{33,1},{65,33},{97,65},{2,98}... | collective-permute-start | bytes 368648 | tf_op jit(solution)/shard_map/ppermute | solution.py:344
  68.6 9.0 %collective-permute-start.24 = (bf16[160,768]{1,0:T(8,128)(2,1)S(1)}, bf16[160,768]{1,0:T(8,128)(2,1)S(1)}, u32[]{:S(2)}, u32[]{:S(2)}) collective-permute-start(bf16[160,768]{1,0:T(8,128)(2,1)S(1)} %get-tuple-element.98), channel_id=1, source_target_pairs={{0,1},{1,2},{2,3},{3,0},{4,5},{5,6},{6,7},{7,4},{8,9},{9,10},{10,1... | collective-permute-start | bytes 737288 | tf_op jit(solution)/shard_map/ppermute | solution.py:344
  69.1 10.1 %collective-permute-start.25 = (bf16[160,768]{1,0:T(8,128)(2,1)S(1)}, bf16[160,768]{1,0:T(8,128)(2,1)S(1)}, u32[]{:S(2)}, u32[]{:S(2)}) collective-permute-start(bf16[160,768]{1,0:T(8,128)(2,1)S(1)} %get-tuple-element.99), channel_id=1, source_target_pairs={{0,3},{1,0},{2,1},{3,2},{4,7},{5,4},{6,5},{7,6},{8,11},{9,8},{10,9... | collective-permute-start | bytes 737288 | tf_op jit(solution)/shard_map/ppermute | solution.py:344
  71.7 12.8 %collective-permute-start.22 = (bf16[160,768]{1,0:T(8,128)(2,1)S(1)}, bf16[160,768]{1,0:T(8,128)(2,1)S(1)}, u32[]{:S(2)}, u32[]{:S(2)}) collective-permute-start(bf16[160,768]{1,0:T(8,128)(2,1)S(1)} %get-tuple-element.92), channel_id=1, source_target_pairs={{0,3},{1,0},{2,1},{3,2},{4,7},{5,4},{6,5},{7,6},{8,11},{9,8},{10,9... | collective-permute-start | bytes 737288 | tf_op jit(solution)/shard_map/ppermute | solution.py:344
  72.6 11.9 %collective-permute-start.23 = (bf16[160,768]{1,0:T(8,128)(2,1)S(1)}, bf16[160,768]{1,0:T(8,128)(2,1)S(1)}, u32[]{:S(2)}, u32[]{:S(2)}) collective-permute-start(bf16[160,768]{1,0:T(8,128)(2,1)S(1)} %get-tuple-element.93), channel_id=1, source_target_pairs={{0,1},{1,2},{2,3},{3,0},{4,5},{5,6},{6,7},{7,4},{8,9},{9,10},{10,1... | collective-permute-start | bytes 737288 | tf_op jit(solution)/shard_map/ppermute | solution.py:344
  79.3 6.7 %collective-permute-start.26 = (bf16[160,768]{1,0:T(8,128)(2,1)S(1)}, bf16[160,768]{1,0:T(8,128)(2,1)S(1)}, u32[]{:S(2)}, u32[]{:S(2)}) collective-permute-start(bf16[160,768]{1,0:T(8,128)(2,1)S(1)} %get-tuple-element.100), channel_id=1, source_target_pairs={{0,1},{1,2},{2,3},{3,0},{4,5},{5,6},{6,7},{7,4},{8,9},{9,10},{10,1... | collective-permute-start | bytes 737288 | tf_op jit(solution)/shard_map/ppermute | solution.py:344
  79.7 7.7 %collective-permute-start.27 = (bf16[160,768]{1,0:T(8,128)(2,1)S(1)}, bf16[160,768]{1,0:T(8,128)(2,1)S(1)}, u32[]{:S(2)}, u32[]{:S(2)}) collective-permute-start(bf16[160,768]{1,0:T(8,128)(2,1)S(1)} %get-tuple-element.101), channel_id=1, source_target_pairs={{0,3},{1,0},{2,1},{3,2},{4,7},{5,4},{6,5},{7,6},{8,11},{9,8},{10,9... | collective-permute-start | bytes 737288 | tf_op jit(solution)/shard_map/ppermute | solution.py:344
